TPU v7x, 32 devices: a whole 2x2x4 slice. The times are simulated.
32 devices in a mesh: dp: 8 (over y, x, core), fsdp: 4 (over z).
Axes of the slice: x: 2, y: 2, z: 4, core: 2. Of those that a mesh axis runs over, the one named last changes fastest.
Arguments:
- tokens: bfloat16 [24576, 1024], P(('dp', 'fsdp')), may hold values from -6 to 6
- lengths: int32 [32, 4], P(('dp', 'fsdp')), may hold values from 0 to 768, as said below
- cotangent: bfloat16 [24576, 1024], P(('dp', 'fsdp')), may hold values from -6 to 6
- norm_gain: float32 [1024], P('fsdp'), may hold values from 0.5 to 1.5
- input_weight: float32 [1024, 4096], P('fsdp'), may hold values from -0.1875 to 0.1875
- select_weight: float32 [96, 2048], P(None, 'fsdp'), may hold values from -0.125 to 0.125
- step_weight: float32 [64, 2048], P(None, 'fsdp'), may hold values from -0.75 to 0.75
- channel_params: float32 [23, 2048], P(None, 'fsdp'), may hold values from -10 to 4, as said below
- output_weight: float32 [2048, 1024], P('fsdp'), may hold values from -0.25 to 0.25
- moment_gain: float32 [1024], P('fsdp'), may hold values from -0.00390625 to 0.00390625
- moment_input: float32 [1024, 4096], P('fsdp'), may hold values from -0.00390625 to 0.00390625
- moment_select: float32 [96, 2048], P(None, 'fsdp'), may hold values from -0.00390625 to 0.00390625
- moment_step: float32 [64, 2048], P(None, 'fsdp'), may hold values from -0.00390625 to 0.00390625
- moment_channel: float32 [23, 2048], P(None, 'fsdp'), may hold values from -0.00390625 to 0.00390625
- moment_output: float32 [2048, 1024], P('fsdp'), may hold values from -0.00390625 to 0.00390625
- square_gain: float32 [1024], P('fsdp'), may hold values from 1e-08 to 1e-06
- square_input: float32 [1024, 4096], P('fsdp'), may hold values from 1e-08 to 1e-06
- square_select: float32 [96, 2048], P(None, 'fsdp'), may hold values from 1e-08 to 1e-06
- square_step: float32 [64, 2048], P(None, 'fsdp'), may hold values from 1e-08 to 1e-06
- square_channel: float32 [23, 2048], P(None, 'fsdp'), may hold values from 1e-08 to 1e-06
- square_output: float32 [2048, 1024], P('fsdp'), may hold values from 1e-08 to 1e-06
Outputs:
- layer_output: bfloat16 [24576, 1024], P(('dp', 'fsdp'))
- input_grad: bfloat16 [24576, 1024], P(('dp', 'fsdp'))
- grad_norm: float32 [], replicated
- update_gain: float32 [1024], P('fsdp')
- update_input: float32 [1024, 4096], P('fsdp')
- update_select: float32 [96, 2048], P(None, 'fsdp')
- update_step: float32 [64, 2048], P(None, 'fsdp')
- update_channel: float32 [23, 2048], P(None, 'fsdp')
- update_output: float32 [2048, 1024], P('fsdp')
- total_gain: float32 [1024], P('fsdp')
- total_input: float32 [1024, 4096], P('fsdp')
- total_select: float32 [96, 2048], P(None, 'fsdp')
- total_step: float32 [64, 2048], P(None, 'fsdp')
- total_channel: float32 [23, 2048], P(None, 'fsdp')
- total_output: float32 [2048, 1024], P('fsdp')
Inputs may be any that keep to these rules, and one draw needn't show every extreme that they name: Row k lists the cluster lengths of device k's 768 token slots in order; each row sums to between 384 and 768; in every draw some device holds one cluster of exactly 768 tokens, the rest of its row 0; a length may be 0. `channel_params`: rows 0 to 15 are logarithms of positive decay rates, the step-size bias row is the inverse softplus of a positive step size, the skip row is positive.
All inputs are finite; a program needn't handle non-finite values.
Results may differ from a plain program's by a relative error of at most 0.0065.
The roundings to bfloat16 on the way count: a program that leaves them out, or rounds other values in their place, can miss the bound.
Values may be sent and summed in bfloat16 or wider, within the bound.
A program may use at most 320 MiB of HBM per device.

v0:
```python
import jax
import jax.numpy as jnp
from jax import lax
from jax.sharding import PartitionSpec as P

DI = 2048
N = 16
R = 64
CONV = 4
SPAN = 64


norm_eps = 1e-05
beta_one = 0.9
beta_two = 0.95
adam_eps = 1e-08
decay_rate = 0.1
adam_step = 10.0
clip_norm = 1.0


def block_layout(lengths_row, count):
    ends = jnp.cumsum(lengths_row, dtype=jnp.int32)
    starts = ends - lengths_row
    places = jnp.arange(count, dtype=jnp.int32)
    live_mask = (places < ends[-1]).astype(jnp.float32)
    begun = jnp.where(
        starts[None, :] <= places[:, None], starts[None, :], jnp.zeros_like(starts)[None, :]
    )
    offset = places - jnp.max(begun, axis=1)
    return (live_mask, offset)


def rms_scale(values, scales):
    return (
        values
        * lax.rsqrt(jnp.mean(values * values, axis=1, keepdims=True) + norm_eps)
        * scales[None, :]
    )


def causal_conv(values, kernel, shift, offset):
    total = shift[None, :] + kernel[CONV - 1][None, :] * values
    for distance in range(1, CONV):
        moved = jnp.pad(values, ((distance, 0), (0, 0)))[:-distance]
        keep = (offset >= distance).astype(jnp.float32)[:, None]
        total = total + kernel[CONV - 1 - distance][None, :] * moved * keep
    return total


def scan_token(rates):

    def advance(carried, token_row):
        step_size, values, bsel, csel, restart = token_row
        carried = (
            jnp.exp(step_size[None, :] * rates) * (1.0 - restart) * carried
            + bsel[:, None] * (step_size * values)[None, :]
        )
        return (carried, jnp.sum(csel[:, None] * carried, axis=0))

    return advance


def selective_scan(rates, step_size, values, bsel, csel, restart):
    length = step_size.shape[0]
    blocks = length // SPAN

    def shaped(array):
        return array.reshape((blocks, SPAN) + array.shape[1:])

    @jax.checkpoint
    def one_block(carried, slices):
        return lax.scan(scan_token(rates), carried, slices, unroll=True)

    start = jnp.zeros(rates.shape, jnp.float32)
    _, scanned = lax.scan(
        one_block,
        start,
        (shaped(step_size), shaped(values), shaped(bsel), shaped(csel), shaped(restart)),
    )
    return scanned.reshape(length, rates.shape[1])


def mixer_core(values, bsel, csel, step_pre, gate_half, channel, restart):
    step_size = jax.nn.softplus(step_pre + channel[N + CONV + 1][None, :])
    rates = -jnp.exp(channel[:N])
    scanned = selective_scan(rates, step_size, values, bsel, csel, restart)
    scanned = scanned + channel[N + CONV + 2][None, :] * values
    return scanned * jax.nn.silu(gate_half)


def contract(left, right, left_dim, right_dim):
    return lax.dot_general(
        left, right, (((left_dim,), (right_dim,)), ((), ())), preferred_element_type=jnp.float32
    )


def channel_decay(rows_total):
    places = jnp.arange(rows_total, dtype=jnp.int32)[:, None]
    return ((places >= N) & (places < N + CONV)).astype(jnp.float32)


def adam_direction(weight, grad, first, second, factor, decay):
    clipped = grad * factor
    first = beta_one * first + (1.0 - beta_one) * clipped
    second = beta_two * second + (1.0 - beta_two) * clipped * clipped
    first_hat = first / (1.0 - beta_one**adam_step)
    second_hat = second / (1.0 - beta_two**adam_step)
    return first_hat / (jnp.sqrt(second_hat) + adam_eps) + decay_rate * decay * weight


def local(
    tokens,
    lengths,
    cotangent,
    norm_gain,
    input_weight,
    select_weight,
    step_weight,
    channel_params,
    output_weight,
    moment_gain,
    moment_input,
    moment_select,
    moment_step,
    moment_channel,
    moment_output,
    square_gain,
    square_input,
    square_select,
    square_step,
    square_channel,
    square_output,
):
    row_count = tokens.shape[0]
    live_mask, offset = block_layout(lengths[0], row_count)
    restart = (offset == 0).astype(jnp.float32)
    full_input, full_select, full_step, full_output = (
        lax.all_gather(input_weight.astype(jnp.bfloat16), "fsdp", axis=0, tiled=True),
        lax.all_gather(select_weight.astype(jnp.bfloat16), "fsdp", axis=1, tiled=True),
        lax.all_gather(step_weight.astype(jnp.bfloat16), "fsdp", axis=1, tiled=True),
        lax.all_gather(output_weight.astype(jnp.bfloat16), "fsdp", axis=0, tiled=True),
    )
    gain, channel = (
        lax.all_gather(norm_gain, "fsdp", axis=0, tiled=True),
        lax.all_gather(channel_params, "fsdp", axis=1, tiled=True),
    )
    inputs = tokens.astype(jnp.float32)
    normed_value, norm_pull = jax.vjp(rms_scale, inputs, gain)
    normed = normed_value.astype(jnp.bfloat16)
    projected = jnp.dot(normed, full_input, preferred_element_type=jnp.float32)
    conv_input = projected[:, :DI]
    gate_half = projected[:, DI:]

    def conv_piece(values, kernel, shift):
        return jax.nn.silu(causal_conv(values, kernel, shift, offset))

    conv_value, conv_pull = jax.vjp(
        conv_piece, conv_input, channel[N : N + CONV], channel[N + CONV]
    )
    mixed = conv_value.astype(jnp.bfloat16)
    mixed_values = mixed.astype(jnp.float32)
    selection = contract(mixed, full_select, 1, 1)
    step_low = selection[:, :R].astype(jnp.bfloat16)
    step_pre = jnp.dot(step_low, full_step, preferred_element_type=jnp.float32)

    def core_piece(values, bsel, csel, pre, gates, params):
        return mixer_core(values, bsel, csel, pre, gates, params, restart)

    core_value, core_pull = jax.vjp(
        core_piece,
        mixed_values,
        selection[:, R : R + N],
        selection[:, R + N :],
        step_pre,
        gate_half,
        channel,
    )
    gated = core_value.astype(jnp.bfloat16)
    branch = jnp.dot(gated, full_output, preferred_element_type=jnp.float32)
    layer_output = (inputs + live_mask[:, None] * branch).astype(jnp.bfloat16)
    back_input, back_select, back_step, back_output = (
        lax.all_gather(input_weight.astype(jnp.bfloat16), "fsdp", axis=0, tiled=True),
        lax.all_gather(select_weight.astype(jnp.bfloat16), "fsdp", axis=1, tiled=True),
        lax.all_gather(step_weight.astype(jnp.bfloat16), "fsdp", axis=1, tiled=True),
        lax.all_gather(output_weight.astype(jnp.bfloat16), "fsdp", axis=0, tiled=True),
    )
    upstream = cotangent.astype(jnp.float32)
    grad_branch = (upstream * live_mask[:, None]).astype(jnp.bfloat16)
    grad_output = contract(gated, grad_branch, 0, 0)
    grad_gated = contract(grad_branch, back_output, 1, 1)
    grad_mixed, grad_bsel, grad_csel, grad_pre, grad_gate, grad_channel = core_pull(grad_gated)
    grad_pre_low = grad_pre.astype(jnp.bfloat16)
    grad_step = contract(step_low, grad_pre_low, 0, 0)
    grad_step_low = contract(grad_pre_low, back_step, 1, 1)
    grad_selection = jnp.concatenate([grad_step_low, grad_bsel, grad_csel], axis=1).astype(
        jnp.bfloat16
    )
    grad_select = contract(grad_selection, mixed, 0, 0)
    grad_mixed = grad_mixed + jnp.dot(
        grad_selection, back_select, preferred_element_type=jnp.float32
    )
    grad_conv_input, grad_kernel, grad_shift = conv_pull(grad_mixed)
    grad_projected = jnp.concatenate([grad_conv_input, grad_gate], axis=1).astype(jnp.bfloat16)
    grad_input = contract(normed, grad_projected, 0, 0)
    grad_normed = contract(grad_projected, back_input, 1, 1)
    grad_inputs, grad_gain = norm_pull(grad_normed)
    input_grad = (upstream + grad_inputs).astype(jnp.bfloat16)
    grad_channel = grad_channel.at[N : N + CONV].add(grad_kernel).at[N + CONV].add(grad_shift)
    owned_gain, owned_input, owned_select, owned_step, owned_channel, owned_output = (
        lax.psum_scatter(grad_gain, "fsdp", scatter_dimension=0, tiled=True),
        lax.psum_scatter(grad_input, "fsdp", scatter_dimension=0, tiled=True),
        lax.psum_scatter(grad_select, "fsdp", scatter_dimension=1, tiled=True),
        lax.psum_scatter(grad_step, "fsdp", scatter_dimension=1, tiled=True),
        lax.psum_scatter(grad_channel, "fsdp", scatter_dimension=1, tiled=True),
        lax.psum_scatter(grad_output, "fsdp", scatter_dimension=0, tiled=True),
    )
    sum_gain, sum_input, sum_select, sum_step, sum_channel, sum_output = lax.psum(
        (owned_gain, owned_input, owned_select, owned_step, owned_channel, owned_output), "dp"
    )
    grads = (sum_gain, sum_input, sum_select, sum_step, sum_channel, sum_output)
    local_square = sum([jnp.sum(grad * grad) for grad in grads])
    total_square = lax.psum(local_square, "fsdp")
    grad_norm = jnp.sqrt(total_square)
    factor = jnp.minimum(1.0, clip_norm / (grad_norm + 1e-06))
    params = (norm_gain, input_weight, select_weight, step_weight, channel_params, output_weight)
    firsts = (moment_gain, moment_input, moment_select, moment_step, moment_channel, moment_output)
    seconds = (square_gain, square_input, square_select, square_step, square_channel, square_output)
    decays = (0.0, 1.0, 1.0, 1.0, channel_decay(channel_params.shape[0]), 1.0)
    updates = [
        adam_direction(
            params[which], grads[which], firsts[which], seconds[which], factor, decays[which]
        )
        for which in range(6)
    ]
    return (
        layer_output,
        input_grad,
        grad_norm,
        updates[0],
        updates[1],
        updates[2],
        updates[3],
        updates[4],
        updates[5],
        grads[0],
        grads[1],
        grads[2],
        grads[3],
        grads[4],
        grads[5],
    )


def solution(mesh):
    in_specs = (
        P(("dp", "fsdp"), None),
        P(("dp", "fsdp"), None),
        P(("dp", "fsdp"), None),
        P("fsdp"),
        P("fsdp", None),
        P(None, "fsdp"),
        P(None, "fsdp"),
        P(None, "fsdp"),
        P("fsdp", None),
        P("fsdp"),
        P("fsdp", None),
        P(None, "fsdp"),
        P(None, "fsdp"),
        P(None, "fsdp"),
        P("fsdp", None),
        P("fsdp"),
        P("fsdp", None),
        P(None, "fsdp"),
        P(None, "fsdp"),
        P(None, "fsdp"),
        P("fsdp", None),
    )
    out_specs = (
        P(("dp", "fsdp"), None),
        P(("dp", "fsdp"), None),
        P(),
        P("fsdp"),
        P("fsdp", None),
        P(None, "fsdp"),
        P(None, "fsdp"),
        P(None, "fsdp"),
        P("fsdp", None),
        P("fsdp"),
        P("fsdp", None),
        P(None, "fsdp"),
        P(None, "fsdp"),
        P(None, "fsdp"),
        P("fsdp", None),
    )
    return jax.shard_map(local, mesh=mesh, in_specs=in_specs, out_specs=out_specs, check_vma=False)
```

profile of v0, /device:TPU:0, one launch (start us, length us, event | category | flops | bytes accessed | tf_op | source)
XLA Modules:
  0.0 6957.9 jit_solution(13265659499785784374)
XLA Ops:
  15.1 12.6 all-gather
  27.8 17.2 all_gather.22
  45.0 20.2 all_gather.26
  65.8 23.6 all_gather.25
  91.2 85.8 %all-gather.4.cloned.1.call-done = bf16[1024,4096]{1,0:T(8,128)(2,1)} async-done(((bf16[256,4096]{1,0:T(8,128)(2,1)}), bf16[1024,4096]{1,0:T(8,128)(2,1)}) %all-gather.4.cloned.1.call-update) | async-done | bytes 8388624 | tf_op jit(solution)/shard_map/all_gather | solution.py:139
  194.3 64.3 all-gather.6.cloned.1.call-done
  258.6 26.9 multiply_reduce_fusion.324
  304.1 886.2 %while.42 = (s32[]{:T(128)}, f32[16,2048]{1,0:T(8,128)S(1)}, f32[12,64,2048]{2,1,0:T(8,128)}, f32[12,16,2048]{2,1,0:T(8,128)}, f32[12,64,2048]{2,1,0:T(8,128)}, ...) while((s32[]{:T(128)}, f32[16,2048]{1,0:T(8,128)S(1)}, ...), condition=%wide.region_68.69_spmd.clone, body=%wide.region_3.68_spmd.clone.sunk | while | flops 20021376 | bytes 19167756 | solution.py:76
  1198.5 5076.9 %while.43 = (s32[]{:T(128)}, f32[16,2048]{1,0:T(8,128)}, f32[16,2048]{1,0:T(8,128)}, f32[12,64,2048]{2,1,0:T(8,128)}, f32[12,64,2048]{2,1,0:T(8,128)}, /*index=5...) while((s32[]{:T(128)}, f32[16,2048]{1,0:T(8,128)}, ...), condition=%wide.region_326.327_spmd.clone, body=%wide.region_69.326_spmd.clone.sunk | while | flops 76150848 | bytes 111636064 | solution.py:76
  1578.1 12.3 concatenate.64
  1590.3 12.3 concatenate.65
  1998.8 12.3 concatenate.64
  2011.1 12.3 concatenate.65
  2419.6 12.3 concatenate.64
  2431.9 12.3 concatenate.65
  2840.5 12.3 concatenate.64
  2852.7 12.3 concatenate.65
  3261.3 12.3 concatenate.64
  3273.5 12.3 concatenate.65
  3682.1 12.3 concatenate.64
  4102.9 12.3 concatenate.64
  4523.7 12.3 concatenate.64
  4944.5 12.3 concatenate.64
  5365.3 12.3 concatenate.64
  5786.1 12.3 concatenate.64
  6207.0 12.3 concatenate.64
  6294.7 33.5 multiply_reduce_fusion.323
  6362.3 117.3 %reduce-scatter.14.cloned.1.call-done = f32[512,1024]{1,0:T(8,128)} async-done(((f32[2048,1024]{1,0:T(8,128)}), f32[512,1024]{1,0:T(8,128)}) %reduce-scatter.14.cloned.1.call-update) | async-done | bytes 2097168 | tf_op jit(solution)/shard_map/reduce_scatter | solution.py:216
  6479.6 283.3 %reduce-scatter.6.cloned.1.call-done = f32[256,4096]{1,0:T(8,128)} async-done(((f32[1024,4096]{1,0:T(8,128)}), f32[256,4096]{1,0:T(8,128)}) %reduce-scatter.6.cloned.1.call-update) | async-done | bytes 4194320 | tf_op jit(solution)/shard_map/reduce_scatter | solution.py:212
  6764.2 12.8 fusion.154
  6796.0 26.0 all-reduce.14
  6823.3 74.1 %all-reduce.18.cloned.1.call-done = (f32[256,4096]{1,0:T(8,128)}, f32[96,512]{1,0:T(8,128)}, f32[64,512]{1,0:T(8,128)}, f32[512,1024]{1,0:T(8,128)}) async-done(((f32[256,4096]{1,0:T(8,128)}, f32[96,512]{1,0:T(8,128)}, f32[64,512]{1,0:T(8,128)}, f32[512,1024]{1,0:T(8,128)}), (f32[256,4096]{1,0:T(8,128)}, f32[96,512]{1,0:T(8,128)}, f32[64,512]{1,0:T(8,128)}, ...) | async-done | bytes 6619152 | tf_op jit(solution)/shard_map/psum | solution.py:218
  (6855 shorter events, 4923.1 us)
Async XLA Ops:
  7.2 169.7 %all-gather.4.cloned.1.call-start = ((), (), s32[]{:S(2)}) async-start(), calls=%async_computation.5 | async-start | bytes 10485760 | tf_op jit(solution)/shard_map/all_gather | solution.py:139
  11.3 247.3 %all-gather.6.cloned.1.call-start = ((), (), s32[]{:S(2)}) async-start(), calls=%async_computation.6 | async-start | bytes 5242880 | tf_op jit(solution)/shard_map/all_gather | solution.py:142
  14.1 6348.2 %reduce-scatter.10.cloned.1.call-start = ((), (), s32[]{:S(2)}) async-start(), calls=%async_computation.9 | async-start | bytes 655360 | tf_op jit(solution)/shard_map/reduce_scatter | solution.py:214
  27.8 158.5 %copy-start.131 = (f32[4,1,256]{2,1,0:T(1,128)}, f32[4,1,256]{2,1,0:T(1,128)S(1)}, u32[]{:S(2)}) copy-start(f32[4,1,256]{2,1,0:T(1,128)S(1)} %all-gather) | copy-start | bytes 12292
  45.0 141.3 %copy-start.121 = (f32[23,2048]{1,0:T(8,128)}, f32[23,2048]{1,0:T(8,128)S(1)}, u32[]{:S(2)}) copy-start(f32[23,2048]{1,0:T(8,128)S(1)} %all_gather.22) | copy-start | bytes 565252
  65.8 192.7 %copy-start.157 = (f32[768]{0:T(1024)}, f32[768]{0:T(1024)S(1)}, u32[]{:S(2)}) copy-start(f32[768]{0:T(1024)S(1)} %fusion.204) | copy-start | bytes 9220
  89.8 168.7 %copy-start.161 = (f32[768]{0:T(1024)}, f32[768]{0:T(1024)S(1)}, u32[]{:S(2)}) copy-start(f32[768]{0:T(1024)S(1)} %get-tuple-element.2015) | copy-start | bytes 9220
  89.8 168.7 %copy-start.162 = (f32[768]{0:T(1024)}, f32[768]{0:T(1024)S(1)}, u32[]{:S(2)}) copy-start(f32[768]{0:T(1024)S(1)} %get-tuple-element.2016) | copy-start | bytes 9220
  89.9 168.7 %copy-start.163 = (f32[768]{0:T(1024)}, f32[768]{0:T(1024)S(1)}, u32[]{:S(2)}) copy-start(f32[768]{0:T(1024)S(1)} %get-tuple-element.2017) | copy-start | bytes 9220
  91.1 167.4 %copy-start.149 = (f32[1,2048]{1,0:T(1,128)}, f32[1,2048]{1,0:T(1,128)S(1)}, u32[]{:S(2)}) copy-start(f32[1,2048]{1,0:T(1,128)S(1)} %get-tuple-element.2013) | copy-start | bytes 24580
  91.1 167.4 %copy-start.152 = (f32[1,2048]{1,0:T(1,128)}, f32[1,2048]{1,0:T(1,128)S(1)}, u32[]{:S(2)}) copy-start(f32[1,2048]{1,0:T(1,128)S(1)} %get-tuple-element.2010) | copy-start | bytes 24580
  91.1 167.4 %copy-start.154 = (f32[1,2048]{1,0:T(1,128)}, f32[1,2048]{1,0:T(1,128)S(1)}, u32[]{:S(2)}) copy-start(f32[1,2048]{1,0:T(1,128)S(1)} %get-tuple-element.2011) | copy-start | bytes 24580
  91.1 167.4 %copy-start.155 = (f32[1,2048]{1,0:T(1,128)}, f32[1,2048]{1,0:T(1,128)S(1)}, u32[]{:S(2)}) copy-start(f32[1,2048]{1,0:T(1,128)S(1)} %get-tuple-element.2012) | copy-start | bytes 24580
  91.1 201.5 %copy-start.148 = (f32[1,2048]{1,0:T(1,128)}, f32[1,2048]{1,0:T(1,128)S(1)}, u32[]{:S(2)}) copy-start(f32[1,2048]{1,0:T(1,128)S(1)} %get-tuple-element.2008) | copy-start | bytes 24580
  1290.7 176.5 %copy-start = (f32[16,2048]{1,0:T(8,128)}, f32[16,2048]{1,0:T(8,128)S(1)}, u32[]{:S(2)}) copy-start(f32[16,2048]{1,0:T(8,128)S(1)} %get-tuple-element.4235) | copy-start | bytes 393220 | tf_op jit(solution)/shard_map/transpose(jvp())/while
  1711.5 176.5 %copy-start = (f32[16,2048]{1,0:T(8,128)}, f32[16,2048]{1,0:T(8,128)S(1)}, u32[]{:S(2)}) copy-start(f32[16,2048]{1,0:T(8,128)S(1)} %get-tuple-element.4235) | copy-start | bytes 393220 | tf_op jit(solution)/shard_map/transpose(jvp())/while
  2132.3 176.5 %copy-start = (f32[16,2048]{1,0:T(8,128)}, f32[16,2048]{1,0:T(8,128)S(1)}, u32[]{:S(2)}) copy-start(f32[16,2048]{1,0:T(8,128)S(1)} %get-tuple-element.4235) | copy-start | bytes 393220 | tf_op jit(solution)/shard_map/transpose(jvp())/while
  2553.1 176.5 %copy-start = (f32[16,2048]{1,0:T(8,128)}, f32[16,2048]{1,0:T(8,128)S(1)}, u32[]{:S(2)}) copy-start(f32[16,2048]{1,0:T(8,128)S(1)} %get-tuple-element.4235) | copy-start | bytes 393220 | tf_op jit(solution)/shard_map/transpose(jvp())/while
  2973.9 176.5 %copy-start = (f32[16,2048]{1,0:T(8,128)}, f32[16,2048]{1,0:T(8,128)S(1)}, u32[]{:S(2)}) copy-start(f32[16,2048]{1,0:T(8,128)S(1)} %get-tuple-element.4235) | copy-start | bytes 393220 | tf_op jit(solution)/shard_map/transpose(jvp())/while
  3394.8 176.5 %copy-start = (f32[16,2048]{1,0:T(8,128)}, f32[16,2048]{1,0:T(8,128)S(1)}, u32[]{:S(2)}) copy-start(f32[16,2048]{1,0:T(8,128)S(1)} %get-tuple-element.4235) | copy-start | bytes 393220 | tf_op jit(solution)/shard_map/transpose(jvp())/while
  3815.6 176.5 %copy-start = (f32[16,2048]{1,0:T(8,128)}, f32[16,2048]{1,0:T(8,128)S(1)}, u32[]{:S(2)}) copy-start(f32[16,2048]{1,0:T(8,128)S(1)} %get-tuple-element.4235) | copy-start | bytes 393220 | tf_op jit(solution)/shard_map/transpose(jvp())/while
  4236.4 176.5 %copy-start = (f32[16,2048]{1,0:T(8,128)}, f32[16,2048]{1,0:T(8,128)S(1)}, u32[]{:S(2)}) copy-start(f32[16,2048]{1,0:T(8,128)S(1)} %get-tuple-element.4235) | copy-start | bytes 393220 | tf_op jit(solution)/shard_map/transpose(jvp())/while
  4657.2 176.5 %copy-start = (f32[16,2048]{1,0:T(8,128)}, f32[16,2048]{1,0:T(8,128)S(1)}, u32[]{:S(2)}) copy-start(f32[16,2048]{1,0:T(8,128)S(1)} %get-tuple-element.4235) | copy-start | bytes 393220 | tf_op jit(solution)/shard_map/transpose(jvp())/while
  5078.0 176.5 %copy-start = (f32[16,2048]{1,0:T(8,128)}, f32[16,2048]{1,0:T(8,128)S(1)}, u32[]{:S(2)}) copy-start(f32[16,2048]{1,0:T(8,128)S(1)} %get-tuple-element.4235) | copy-start | bytes 393220 | tf_op jit(solution)/shard_map/transpose(jvp())/while
  5498.8 176.5 %copy-start = (f32[16,2048]{1,0:T(8,128)}, f32[16,2048]{1,0:T(8,128)S(1)}, u32[]{:S(2)}) copy-start(f32[16,2048]{1,0:T(8,128)S(1)} %get-tuple-element.4235) | copy-start | bytes 393220 | tf_op jit(solution)/shard_map/transpose(jvp())/while
  5919.6 176.5 %copy-start = (f32[16,2048]{1,0:T(8,128)}, f32[16,2048]{1,0:T(8,128)S(1)}, u32[]{:S(2)}) copy-start(f32[16,2048]{1,0:T(8,128)S(1)} %get-tuple-element.4235) | copy-start | bytes 393220 | tf_op jit(solution)/shard_map/transpose(jvp())/while
  6287.0 75.3 %reduce-scatter.8.cloned.1.call-start = ((), (), s32[]{:S(2)}) async-start(), calls=%async_computation.8 | async-start | bytes 983040 | tf_op jit(solution)/shard_map/reduce_scatter | solution.py:213
  6294.6 185.0 %reduce-scatter.14.cloned.1.call-start = ((), (), s32[]{:S(2)}) async-start(), calls=%async_computation.11 | async-start | bytes 10485760 | tf_op jit(solution)/shard_map/reduce_scatter | solution.py:216
  6336.0 426.8 %reduce-scatter.6.cloned.1.call-start = ((), (), s32[]{:S(2)}) async-start(), calls=%async_computation.7 | async-start | bytes 20971520 | tf_op jit(solution)/shard_map/reduce_scatter | solution.py:212
  6360.1 402.8 %copy-start.168 = (u32[32]{0:T(128)S(1)}, u32[32]{0:T(128)}, u32[]{:S(2)}) copy-start(u32[32]{0:T(128)} %constant.412) | copy-start | bytes 388
  6360.1 435.9 %reduce-scatter.12.cloned.1.call-start = ((), (), s32[]{:S(2)}) async-start(), calls=%async_computation.10 | async-start | bytes 245760 | tf_op jit(solution)/shard_map/reduce_scatter | solution.py:215
  6362.2 535.3 %all-reduce.18.cloned.1.call-start = ((), (), s32[]{:S(2)}) async-start(), calls=%async_computation.12 | async-start | bytes 13238272 | tf_op jit(solution)/shard_map/psum | solution.py:218
  (1278 other events, 17128.6 us)
Sparse Core Ops, SparseCore 0:
  11.4 165.5 all-gather.3
  179.1 79.3 all-gather.5
  6287.1 20.1 reduce-scatter.9
  6310.0 21.6 reduce-scatter.7
  6336.2 143.3 reduce-scatter.13
  6481.8 281.0 reduce-scatter.5
  6765.8 20.1 reduce-scatter.11
  6789.6 107.7 all-reduce.17
where the time goes:
time: 7050 us; the launch traced here: 6960 us
  local copies, waits for them, and re-layouts  3010 us (43%)
  other arithmetic  2050 us (29%)
  loops' own time  1010 us (14%)
  waiting for transfers between devices  625 us (9%)
  matrix products  125 us (2%)
  blocking collectives  123 us (2%)
    broadcast_in_dim x1536, local copies, waits for them, and re-layouts, one_block(): return lax.scan(scan_token(rates), carried, slices, unroll=True)  2000 us
    another operation x2, loops' own time, selective_scan(): lax.scan(one_block, start, (shaped(step_size), shaped(values), shaped(bse...  1010 us
    reduce_sum x348, other arithmetic, advance(): step_size[None, :] * rates  918 us
    concatenate x60, local copies, waits for them, and re-layouts, one_block(): return lax.scan(scan_token(rates), carried, slices, unroll=True)  346 us
    slice x276, local copies, waits for them, and re-layouts, one_block(): return lax.scan(scan_token(rates), carried, slices, unroll=True)  284 us
    reduce_scatter x1, waiting for transfers between devices, local(): lax.psum_scatter(grad_input, 'fsdp', scatter_dimension=0, tiled=True)  283 us
    reduce_sum x252, other arithmetic, advance(): return (carried, jnp.sum(csel[:, None] * carried, axis=0))  230 us
    mul x948, other arithmetic, advance(): step_size * values  209 us

commit v1 on v0

--- a/solution.py
+++ b/solution.py
@@ -1,14 +1,22 @@
+import functools
+import math
+
 import jax
 import jax.numpy as jnp
 from jax import lax
+from jax.experimental import pallas as pl
+from jax.experimental.pallas import tpu as pltpu
 from jax.sharding import PartitionSpec as P
 
 DI = 2048
 N = 16
 R = 64
 CONV = 4
-SPAN = 64
-
+LANES = 128
+COLS = DI // LANES
+HALVES = COLS // 8
+BLOCK = 64
+GROUP = 8
 
 norm_eps = 1e-05
 beta_one = 0.9
@@ -17,19 +25,18 @@
 decay_rate = 0.1
 adam_step = 10.0
 clip_norm = 1.0
+RESET = 1e30
 
 
 def block_layout(lengths_row, count):
-    ends = jnp.cumsum(lengths_row, dtype=jnp.int32)
-    starts = ends - lengths_row
     places = jnp.arange(count, dtype=jnp.int32)
-    live_mask = (places < ends[-1]).astype(jnp.float32)
-    begun = jnp.where(
-        starts[None, :] <= places[:, None], starts[None, :], jnp.zeros_like(starts)[None, :]
-    )
-    offset = places - jnp.max(begun, axis=1)
-    return (live_mask, offset)
-
+    begun = jnp.zeros((count,), jnp.int32)
+    end = jnp.zeros((), jnp.int32)
+    for cluster in range(lengths_row.shape[0]):
+        begun = jnp.where(end <= places, jnp.maximum(begun, end), begun)
+        end = end + lengths_row[cluster]
+    live_mask = (places < end).astype(jnp.float32)
+    return live_mask, places - begun
 
 def rms_scale(values, scales):
     return (
@@ -48,45 +55,239 @@
     return total
 
 
-def scan_token(rates):
-
-    def advance(carried, token_row):
-        step_size, values, bsel, csel, restart = token_row
-        carried = (
-            jnp.exp(step_size[None, :] * rates) * (1.0 - restart) * carried
-            + bsel[:, None] * (step_size * values)[None, :]
-        )
-        return (carried, jnp.sum(csel[:, None] * carried, axis=0))
-
-    return advance
-
-
-def selective_scan(rates, step_size, values, bsel, csel, restart):
-    length = step_size.shape[0]
-    blocks = length // SPAN
-
-    def shaped(array):
-        return array.reshape((blocks, SPAN) + array.shape[1:])
-
-    @jax.checkpoint
-    def one_block(carried, slices):
-        return lax.scan(scan_token(rates), carried, slices, unroll=True)
-
-    start = jnp.zeros(rates.shape, jnp.float32)
-    _, scanned = lax.scan(
-        one_block,
-        start,
-        (shaped(step_size), shaped(values), shaped(bsel), shaped(csel), shaped(restart)),
-    )
-    return scanned.reshape(length, rates.shape[1])
-
-
-def mixer_core(values, bsel, csel, step_pre, gate_half, channel, restart):
-    step_size = jax.nn.softplus(step_pre + channel[N + CONV + 1][None, :])
-    rates = -jnp.exp(channel[:N])
-    scanned = selective_scan(rates, step_size, values, bsel, csel, restart)
-    scanned = scanned + channel[N + CONV + 2][None, :] * values
-    return scanned * jax.nn.silu(gate_half)
+def spread(ref, value, first):
+    for col in range(COLS):
+        ref[pl.ds(first + 8 * col, 8), :] = value[:, LANES * col : LANES * (col + 1)]
+
+
+def token_rows(ref, first, half, token):
+    return ref[pl.ds(first + 64 * half + token, 8, stride=8), :]
+
+
+def splat(ref, row):
+    return ref[pl.ds(row, 8, stride=0), :]
+
+
+def prepare(rows, sel, dt_ref, mixed_ref, dts, us, bb):
+    first = rows * 16
+    step = dt_ref[pl.ds(rows, 8), :]
+    chosen = sel[pl.ds(rows, 8), :]
+    fresh = chosen[:, 2 * N : 2 * N + 1] > 0.5
+    spread(dts, jnp.where(fresh, RESET, step), first)
+    spread(us, step * mixed_ref[pl.ds(rows, 8), :], first)
+    for k in range(2 * N):
+        bb[pl.ds(rows * 2 * N + 8 * k, 8), :] = jnp.broadcast_to(chosen[:, k : k + 1], (8, LANES))
+
+
+def forward_kernel(dt_ref, mixed_ref, sel, rates, y_ref, hs_ref, state, dts, us, bb, ys):
+    @pl.when(pl.program_id(0) == 0)
+    def _():
+        state[...] = jnp.zeros_like(state)
+
+    def stage(g, _):
+        prepare(pl.multiple_of(g * 8, 8), sel, dt_ref, mixed_ref, dts, us, bb)
+        return 0
+
+    lax.fori_loop(0, BLOCK // 8, stage, 0)
+    for low in range(0, N, GROUP):
+        names = [(n, half) for n in range(low, low + GROUP) for half in range(HALVES)]
+
+        def steps(g, carried):
+            rows = pl.multiple_of(g * 8, 8)
+            first = rows * 16
+            kept = dict(zip(names, carried))
+            for token in range(8):
+                dt = [token_rows(dts, first, half, token) for half in range(HALVES)]
+                u = [token_rows(us, first, half, token) for half in range(HALVES)]
+                total = [None] * HALVES
+                for n in range(low, low + GROUP):
+                    b = splat(bb, rows * 2 * N + 8 * n + token)
+                    c = splat(bb, rows * 2 * N + 8 * (N + n) + token)
+                    for half in range(HALVES):
+                        h = jnp.exp2(dt[half] * rates[2 * n + half]) * kept[n, half] + b * u[half]
+                        kept[n, half] = h
+                        hs_ref[rows + token, 2 * n + half] = h
+                        part = c * h
+                        total[half] = part if total[half] is None else total[half] + part
+                for half in range(HALVES):
+                    at = pl.ds(first + 64 * half + token, 8, stride=8)
+                    ys[at, :] = total[half] if low == 0 else ys[at, :] + total[half]
+            return tuple(kept[name] for name in names)
+
+        start = tuple(state[2 * n + half] for n, half in names)
+        for name, value in zip(names, lax.fori_loop(0, BLOCK // 8, steps, start)):
+            state[2 * name[0] + name[1]] = value
+
+    def finish(g, _):
+        rows = pl.multiple_of(g * 8, 8)
+        for col in range(COLS):
+            y_ref[pl.ds(rows, 8), LANES * col : LANES * (col + 1)] = ys[pl.ds(rows * 16 + 8 * col, 8), :]
+        return 0
+
+    lax.fori_loop(0, BLOCK // 8, finish, 0)
+
+
+def backward_kernel(
+    dt_ref, mixed_ref, gs_ref, sel, rates, hs_ref, last_ref,
+    sum_in, sum_decay, parts, grad_rates,
+    carry, dts, us, gss, bb, s1, s2, prods,
+):
+    @pl.when(pl.program_id(0) == 0)
+    def _():
+        carry[...] = jnp.zeros_like(carry)
+        grad_rates[...] = jnp.zeros_like(grad_rates)
+
+    def stage(g, _):
+        rows = pl.multiple_of(g * 8, 8)
+        prepare(rows, sel, dt_ref, mixed_ref, dts, us, bb)
+        spread(gss, gs_ref[pl.ds(rows, 8), :], rows * 16)
+        return 0
+
+    lax.fori_loop(0, BLOCK // 8, stage, 0)
+    for low in range(0, N, GROUP):
+        names = [(n, half) for n in range(low, low + GROUP) for half in range(HALVES)]
+
+        def steps(step, carried):
+            g = BLOCK // 8 - 1 - step
+            rows = pl.multiple_of(g * 8, 8)
+            first = rows * 16
+            kept = dict(zip(names, carried[: len(names)]))
+            total = dict(zip(names, carried[len(names) :]))
+            for token in reversed(range(8)):
+                dt = [token_rows(dts, first, half, token) for half in range(HALVES)]
+                u = [token_rows(us, first, half, token) for half in range(HALVES)]
+                gs = [token_rows(gss, first, half, token) for half in range(HALVES)]
+                in_sum = [None] * HALVES
+                decay_sum = [None] * HALVES
+                for n in range(low, low + GROUP):
+                    b = splat(bb, rows * 2 * N + 8 * n + token)
+                    c = splat(bb, rows * 2 * N + 8 * (N + n) + token)
+                    for_b = for_c = None
+                    for half in range(HALVES):
+                        at = 2 * n + half
+                        if token > 0:
+                            before = hs_ref[rows + token - 1, at]
+                        else:
+                            before = jnp.where(g == 0, last_ref[0, at], hs_ref[jnp.maximum(rows - 1, 0), at])
+                        rate = rates[at]
+                        adjoint = c * gs[half] + kept[n, half]
+                        part_c = gs[half] * hs_ref[rows + token, at]
+                        part_b = adjoint * u[half]
+                        for_c = part_c if for_c is None else for_c + part_c
+                        for_b = part_b if for_b is None else for_b + part_b
+                        part = b * adjoint
+                        in_sum[half] = part if in_sum[half] is None else in_sum[half] + part
+                        later = jnp.exp2(dt[half] * rate) * adjoint
+                        kept[n, half] = later
+                        slope = later * before
+                        part = rate * slope
+                        decay_sum[half] = part if decay_sum[half] is None else decay_sum[half] + part
+                        total[n, half] = total[n, half] + dt[half] * slope
+                    prods[pl.ds(8 * (n - low), 8), :] = for_b
+                    prods[pl.ds(8 * (GROUP + n - low), 8), :] = for_c
+                for half in range(HALVES):
+                    at = pl.ds(first + 64 * half + token, 8, stride=8)
+                    s1[at, :] = in_sum[half] if low == 0 else s1[at, :] + in_sum[half]
+                    s2[at, :] = decay_sum[half] if low == 0 else s2[at, :] + decay_sum[half]
+                for kind in range(2):
+                    rows_of = [prods[pl.ds(8 * GROUP * kind + s, GROUP, stride=8), :] for s in range(8)]
+                    while len(rows_of) > 1:
+                        rows_of = [a + b for a, b in zip(rows_of[::2], rows_of[1::2])]
+                    parts[rows + token, pl.ds(N * kind + low, GROUP), :] = rows_of[0]
+            return tuple(kept[name] for name in names) + tuple(total[name] for name in names)
+
+        start = tuple(carry[2 * n + half] for n, half in names)
+        start = start + tuple(grad_rates[2 * n + half] for n, half in names)
+        ended = lax.fori_loop(0, BLOCK // 8, steps, start)
+        for name, value, sums in zip(names, ended[: len(names)], ended[len(names) :]):
+            carry[2 * name[0] + name[1]] = value
+            grad_rates[2 * name[0] + name[1]] = sums
+
+    def finish(g, _):
+        rows = pl.multiple_of(g * 8, 8)
+        for col in range(COLS):
+            lanes = slice(LANES * col, LANES * (col + 1))
+            sum_in[pl.ds(rows, 8), lanes] = s1[pl.ds(rows * 16 + 8 * col, 8), :]
+            sum_decay[pl.ds(rows, 8), lanes] = s2[pl.ds(rows * 16 + 8 * col, 8), :]
+        return 0
+
+    lax.fori_loop(0, BLOCK // 8, finish, 0)
+
+
+def scan_forward(dt, mixed, sel, rates):
+    count = dt.shape[0]
+    rows = pl.BlockSpec((BLOCK, DI), lambda i: (i, 0))
+    return pl.pallas_call(
+        forward_kernel,
+        grid=(count // BLOCK,),
+        in_specs=[
+            rows,
+            rows,
+            pl.BlockSpec((BLOCK, LANES), lambda i: (i, 0)),
+            pl.BlockSpec((2 * N, 8, LANES), lambda i: (0, 0, 0)),
+        ],
+        out_specs=[rows, pl.BlockSpec((BLOCK, 2 * N, 8, LANES), lambda i: (i, 0, 0, 0))],
+        out_shape=[
+            jax.ShapeDtypeStruct((count, DI), jnp.float32),
+            jax.ShapeDtypeStruct((count, 2 * N, 8, LANES), jnp.float32),
+        ],
+        scratch_shapes=[
+            pltpu.VMEM((2 * N, 8, LANES), jnp.float32),
+            pltpu.VMEM((BLOCK * COLS, LANES), jnp.float32),
+            pltpu.VMEM((BLOCK * COLS, LANES), jnp.float32),
+            pltpu.VMEM((BLOCK * 2 * N, LANES), jnp.float32),
+            pltpu.VMEM((BLOCK * COLS, LANES), jnp.float32),
+        ],
+        compiler_params=pltpu.CompilerParams(vmem_limit_bytes=48 << 20),
+        cost_estimate=pl.CostEstimate(
+            flops=6 * count * N * DI, bytes_accessed=4 * count * N * DI, transcendentals=count * N * DI
+        ),
+        name="scan_forward",
+    )(dt, mixed, sel, rates)
+
+
+def scan_backward(dt, mixed, gs, sel, rates, states):
+    count = dt.shape[0]
+    blocks = count // BLOCK
+    rows = pl.BlockSpec((BLOCK, DI), lambda i: (blocks - 1 - i, 0))
+    return pl.pallas_call(
+        backward_kernel,
+        grid=(blocks,),
+        in_specs=[
+            rows,
+            rows,
+            rows,
+            pl.BlockSpec((BLOCK, LANES), lambda i: (blocks - 1 - i, 0)),
+            pl.BlockSpec((2 * N, 8, LANES), lambda i: (0, 0, 0)),
+            pl.BlockSpec((BLOCK, 2 * N, 8, LANES), lambda i: (blocks - 1 - i, 0, 0, 0)),
+            pl.BlockSpec(
+                (1, 2 * N, 8, LANES),
+                lambda i: (jnp.maximum((blocks - 1 - i) * BLOCK - 1, 0), 0, 0, 0),
+            ),
+        ],
+        out_specs=[
+            rows,
+            rows,
+            pl.BlockSpec((BLOCK, 2 * N, LANES), lambda i: (blocks - 1 - i, 0, 0)),
+            pl.BlockSpec((2 * N, 8, LANES), lambda i: (0, 0, 0)),
+        ],
+        out_shape=[
+            jax.ShapeDtypeStruct((count, DI), jnp.float32),
+            jax.ShapeDtypeStruct((count, DI), jnp.float32),
+            jax.ShapeDtypeStruct((count, 2 * N, LANES), jnp.float32),
+            jax.ShapeDtypeStruct((2 * N, 8, LANES), jnp.float32),
+        ],
+        scratch_shapes=[pltpu.VMEM((2 * N, 8, LANES), jnp.float32)]
+        + [pltpu.VMEM((BLOCK * COLS, LANES), jnp.float32)] * 3
+        + [pltpu.VMEM((BLOCK * 2 * N, LANES), jnp.float32)]
+        + [pltpu.VMEM((BLOCK * COLS, LANES), jnp.float32)] * 2
+        + [pltpu.VMEM((16 * GROUP, LANES), jnp.float32)],
+        compiler_params=pltpu.CompilerParams(vmem_limit_bytes=48 << 20),
+        cost_estimate=pl.CostEstimate(
+            flops=15 * count * N * DI, bytes_accessed=4 * count * N * DI, transcendentals=count * N * DI
+        ),
+        name="scan_backward",
+    )(dt, mixed, gs, sel, rates, states, states)
 
 
 def contract(left, right, left_dim, right_dim):
@@ -163,50 +364,56 @@
     selection = contract(mixed, full_select, 1, 1)
     step_low = selection[:, :R].astype(jnp.bfloat16)
     step_pre = jnp.dot(step_low, full_step, preferred_element_type=jnp.float32)
-
-    def core_piece(values, bsel, csel, pre, gates, params):
-        return mixer_core(values, bsel, csel, pre, gates, params, restart)
-
-    core_value, core_pull = jax.vjp(
-        core_piece,
-        mixed_values,
-        selection[:, R : R + N],
-        selection[:, R + N :],
-        step_pre,
-        gate_half,
-        channel,
-    )
-    gated = core_value.astype(jnp.bfloat16)
+    step_in = step_pre + channel[N + CONV + 1][None, :]
+    step_size = jax.nn.softplus(step_in)
+    rates = -jnp.exp(channel[:N])
+    rates_low = (rates * math.log2(math.e)).reshape(2 * N, 8, LANES)
+    chosen = jnp.concatenate(
+        [selection[:, R:], restart[:, None], jnp.zeros((row_count, LANES - 2 * N - 1), jnp.float32)], axis=1
+    )
+    skip = channel[N + CONV + 2][None, :]
+    state_out, states = scan_forward(step_size, mixed_values, chosen, rates_low)
+    scanned = state_out + skip * mixed_values
+    gate_value, gate_pull = jax.vjp(jax.nn.silu, gate_half)
+    gated = (scanned * gate_value).astype(jnp.bfloat16)
     branch = jnp.dot(gated, full_output, preferred_element_type=jnp.float32)
     layer_output = (inputs + live_mask[:, None] * branch).astype(jnp.bfloat16)
-    back_input, back_select, back_step, back_output = (
-        lax.all_gather(input_weight.astype(jnp.bfloat16), "fsdp", axis=0, tiled=True),
-        lax.all_gather(select_weight.astype(jnp.bfloat16), "fsdp", axis=1, tiled=True),
-        lax.all_gather(step_weight.astype(jnp.bfloat16), "fsdp", axis=1, tiled=True),
-        lax.all_gather(output_weight.astype(jnp.bfloat16), "fsdp", axis=0, tiled=True),
-    )
     upstream = cotangent.astype(jnp.float32)
     grad_branch = (upstream * live_mask[:, None]).astype(jnp.bfloat16)
     grad_output = contract(gated, grad_branch, 0, 0)
-    grad_gated = contract(grad_branch, back_output, 1, 1)
-    grad_mixed, grad_bsel, grad_csel, grad_pre, grad_gate, grad_channel = core_pull(grad_gated)
+    grad_gated = contract(grad_branch, full_output, 1, 1)
+    grad_scanned = grad_gated * gate_value
+    (grad_gate,) = gate_pull(grad_gated * scanned)
+    sum_in, sum_decay, parts, sums = scan_backward(
+        step_size, mixed_values, grad_scanned, chosen, rates_low, states
+    )
+    grad_both = jnp.sum(parts, axis=2)
+    grad_mixed = step_size * sum_in + skip * grad_scanned
+    grad_pre = (mixed_values * sum_in + math.log(2.0) * sum_decay) * jax.nn.sigmoid(step_in)
     grad_pre_low = grad_pre.astype(jnp.bfloat16)
     grad_step = contract(step_low, grad_pre_low, 0, 0)
-    grad_step_low = contract(grad_pre_low, back_step, 1, 1)
-    grad_selection = jnp.concatenate([grad_step_low, grad_bsel, grad_csel], axis=1).astype(
-        jnp.bfloat16
-    )
+    grad_step_low = contract(grad_pre_low, full_step, 1, 1)
+    grad_selection = jnp.concatenate([grad_step_low, grad_both], axis=1).astype(jnp.bfloat16)
     grad_select = contract(grad_selection, mixed, 0, 0)
     grad_mixed = grad_mixed + jnp.dot(
-        grad_selection, back_select, preferred_element_type=jnp.float32
+        grad_selection, full_select, preferred_element_type=jnp.float32
     )
     grad_conv_input, grad_kernel, grad_shift = conv_pull(grad_mixed)
     grad_projected = jnp.concatenate([grad_conv_input, grad_gate], axis=1).astype(jnp.bfloat16)
     grad_input = contract(normed, grad_projected, 0, 0)
-    grad_normed = contract(grad_projected, back_input, 1, 1)
+    grad_normed = contract(grad_projected, full_input, 1, 1)
     grad_inputs, grad_gain = norm_pull(grad_normed)
     input_grad = (upstream + grad_inputs).astype(jnp.bfloat16)
-    grad_channel = grad_channel.at[N : N + CONV].add(grad_kernel).at[N + CONV].add(grad_shift)
+    grad_channel = jnp.concatenate(
+        [
+            rates * sums.reshape(N, DI),
+            grad_kernel,
+            grad_shift[None, :],
+            jnp.sum(grad_pre, axis=0, keepdims=True),
+            jnp.sum(grad_scanned * mixed_values, axis=0, keepdims=True),
+        ],
+        axis=0,
+    )
     owned_gain, owned_input, owned_select, owned_step, owned_channel, owned_output = (
         lax.psum_scatter(grad_gain, "fsdp", scatter_dimension=0, tiled=True),
         lax.psum_scatter(grad_input, "fsdp", scatter_dimension=0, tiled=True),

time: 7050 us -> 1130 us (0.16); the launches traced: 6960 us -> 1120 us
  local copies, waits for them, and re-layouts: 3010 us -> 24.2 us
  other arithmetic: 2050 us -> 68.9 us
  loops' own time: 1010 us -> 0 us
  Pallas kernels: 0 us -> 133 us
    broadcast_in_dim x1536 -> x1, local copies, waits for them, and re-layouts: 2000 us -> 0.01 us  [local(): jnp.zeros((row_count, LANES - 2 * N - 1), jnp.float32)]
    reduce_sum x625 -> x2, other arithmetic: 1220 us -> 14.8 us  [the longest x1 8.66 us: local(): grad_both = jnp.sum(parts, axis=2)]
    another operation x2 -> x0, loops' own time: 1010 us -> none  [selective_scan(): lax.scan(one_block, start, (shaped(step_size), shaped(values), shaped(bse...]
    add_any x229 -> x1, other arithmetic: 367 us -> 0.04 us  [causal_conv(): total = shift[None, :] + kernel[CONV - 1][None, :] * values]
    concatenate x60 -> x2, local copies, waits for them, and re-layouts: 346 us -> 1.42 us  [the longest x1 1.34 us: local(): jnp.concatenate([rates * sums.reshape(N, DI), grad_kernel, grad_shift[Non...]
    slice x279 -> x3, local copies, waits for them, and re-layouts: 285 us -> 1.24 us  [the longest x1 0.64 us: local(): skip = channel[N + CONV + 2][None, :]]
    mul x961 -> x2, other arithmetic: 232 us -> 0.05 us  [the longest x1 0.03 us: local(): rates * sums.reshape(N, DI)]
    mul x180 -> x0, local copies, waits for them, and re-layouts: 153 us -> none  [the longest x96 82.6 us: advance(): bsel[:, None] * (step_size * values)[None, :]]
where the time goes in v1:
time: 1130 us; the launch traced here: 1120 us
  waiting for transfers between devices  613 us (54%)
  Pallas kernels  133 us (12%)
  blocking collectives  128 us (11%)
  matrix products  127 us (11%)
  other arithmetic  68.9 us (6%)
  between operations  24.8 us (2%)
  local copies, waits for them, and re-layouts  24.2 us (2%)
    reduce_scatter x1, waiting for transfers between devices, local(): lax.psum_scatter(grad_input, 'fsdp', scatter_dimension=0, tiled=True)  283 us
    reduce_scatter x1, waiting for transfers between devices, local(): lax.psum_scatter(grad_output, 'fsdp', scatter_dimension=0, tiled=True)  117 us
    pallas_call x1, Pallas kernels, scan_backward(): pl.pallas_call(backward_kernel, grid=(blocks,), in_specs=[rows, rows, row...  88.7 us
    all_gather x1, waiting for transfers between devices, local(): lax.all_gather(input_weight.astype(jnp.bfloat16), 'fsdp', axis=0, tiled=T...  74.5 us
    psum x1, waiting for transfers between devices, local(): lax.psum((owned_gain, owned_input, owned_select, owned_step, owned_channe...  73.8 us
    dot_general x8, matrix products, contract(): lax.dot_general(left, right, (((left_dim,), (right_dim,)), ((), ())), pre...  66.9 us
    all_gather x1, waiting for transfers between devices, local(): lax.all_gather(output_weight.astype(jnp.bfloat16), 'fsdp', axis=0, tiled=...  64.5 us
    pallas_call x1, Pallas kernels, scan_forward(): pl.pallas_call(forward_kernel, grid=(count // BLOCK,), in_specs=[rows, ro...  44.5 us
  transfers between devices with their start and end apart: 8, of which 5 were waited for; matrix products, arithmetic and copies ran while one was open for 11% of the time, Pallas kernels for 0%

profile of v1, /device:TPU:0, one launch (start us, length us, event | category | flops | bytes accessed | tf_op | source)
XLA Modules:
  0.0 1119.8 jit_solution(11479430029713372789)
XLA Ops:
  7.3 3.9 convert_element_type.93
  16.7 16.3 %all_gather.18 = f32[23,2048]{1,0:T(8,128)S(1)} all-gather(f32[23,512]{1,0:T(8,128)S(1)} %copy-done.34), channel_id=1, replica_groups=mesh['dp'=8,'fsdp'=4] {'fsdp'}, dimensions={1}, use_global_device_ids=true | all-gather | bytes 235520 | tf_op jit(solution)/shard_map/all_gather | solution.py:347
  34.5 18.1 %all-gather = f32[4,1,256]{2,1,0:T(1,128)S(1)} all-gather(f32[1,1,256]{2,1,0:T(1,128)S(1)} %bitcast.58), channel_id=1, replica_groups=mesh['dp'=8,'fsdp'=4] {'fsdp'}, dimensions={0}, use_global_device_ids=true | all-gather | bytes 5120 | tf_op jit(solution)/shard_map/all_gather | solution.py:346
  52.6 19.0 %all_gather.22 = bf16[64,2048]{1,0:T(8,128)(2,1)} all-gather(bf16[64,512]{1,0:T(8,128)(2,1)S(1)} %convert_element_type.99), channel_id=1, replica_groups=mesh['dp'=8,'fsdp'=4] {'fsdp'}, dimensions={1}, use_global_device_ids=true | all-gather | bytes 327680 | tf_op jit(solution)/shard_map/all_gather | solution.py:342
  74.5 25.4 %all_gather.21 = bf16[96,2048]{1,0:T(8,128)(2,1)} all-gather(bf16[96,512]{1,0:T(8,128)(2,1)S(1)} %convert_element_type.98), channel_id=1, replica_groups=mesh['dp'=8,'fsdp'=4] {'fsdp'}, dimensions={1}, use_global_device_ids=true | all-gather | bytes 491520 | tf_op jit(solution)/shard_map/all_gather | solution.py:341
  100.9 74.5 %all-gather.4.cloned.1.call-done = bf16[1024,4096]{1,0:T(8,128)(2,1)} async-done(((bf16[256,4096]{1,0:T(8,128)(2,1)}), bf16[1024,4096]{1,0:T(8,128)(2,1)}) %all-gather.4.cloned.1.call-update) | async-done | bytes 8388624 | tf_op jit(solution)/shard_map/all_gather | solution.py:340
  175.4 9.2 fusion.46
  184.7 4.5 copy-done.8
  189.2 3.4 slice.91
  192.6 64.5 %all-gather.6.cloned.1.call-done = bf16[2048,1024]{1,0:T(8,128)(2,1)} async-done(((bf16[512,1024]{1,0:T(8,128)(2,1)}), bf16[2048,1024]{1,0:T(8,128)(2,1)}) %all-gather.6.cloned.1.call-update) | async-done | bytes 4194320 | tf_op jit(solution)/shard_map/all_gather | solution.py:343
  257.1 26.4 %multiply_reduce_fusion = (f32[2048]{0:T(1024)}, f32[768,2048]{1,0:T(8,128)}, bf16[768,2048]{1,0:T(8,128)(2,1)S(1)}, f32[768,2048]{1,0:T(8,128)}, f32[768,2048]{1,0:T(8,128)}) fusion(f32[768,4096]{1,0:T(8,128)} %copy-done.8, f32[768]{0:T(1024)S(1)} %get-tuple-element.69, f32[768,2048]{1,0:T(8,128)} %slice.91, f32[2048]{0:T(1024)S(1)} %bitcast.45, ...), kind=kOutput, calls=%fused_computation.20 | convolution fusion | flops 3261331456 | bytes 40431616 | tf_op jit(solution)/shard_map/dot_general | solution.py:294
  283.5 3.4 convert_element_type.100.mixed_ref
  289.7 7.5 compare_select_fusion
  297.4 44.5 %scan_forward.1 = (f32[768,2048]{1,0:T(8,128)}, f32[768,32,8,128]{3,2,1,0:T(8,128)}) custom-call(f32[768,2048]{1,0:T(8,128)} %get-tuple-element.65.dt_ref, f32[768,2048]{1,0:T(8,128)} %convert_element_type.100.mixed_ref, f32[768,128]{1,0:T(8,128)S(1)} %maximum_maximum_fusion.sel, f32[32,8,128]{2,1,0:T(8,128)S(1)} %reshape.165.rates), custom_call_target="tpu_custom_call" | custom-call | flops 150994944 | bytes 100663296 | tf_op jit(solution)/shard_map/scan_forward/pallas_call | solution.py:220
  341.9 88.7 %scan_backward.1 = (f32[768,2048]{1,0:T(8,128)}, f32[768,2048]{1,0:T(8,128)}, f32[768,32,128]{2,1,0:T(8,128)}, f32[32,8,128]{2,1,0:T(8,128)S(1)}) custom-call(f32[768,2048]{1,0:T(8,128)} %get-tuple-element.65.dt_ref, f32[768,2048]{1,0:T(8,128)} %convert_element_type.100.mixed_ref, f32[768,2048]{1,0:T(8,128)} %get-tuple-element.41.gs_ref, ...), custom_call_target="tpu_custom_call" | custom-call | flops 377487360 | bytes 100663296 | tf_op jit(solution)/shard_map/scan_backward/pallas_call | solution.py:253
  430.6 6.1 fusion.85
  439.9 8.7 reduce_sum.149
  456.3 35.2 %multiply_reduce_fusion.4 = (f32[2048]{0:T(1024)S(1)}, f32[2048]{0:T(1024)S(1)}, f32[2048]{0:T(1024)S(1)}, f32[2048]{0:T(1024)S(1)}, f32[2048]{0:T(1024)S(1)}, /...) fusion(f32[768,2048]{1,0:T(8,128)} %slice.91, ...), kind=kOutput, calls=%fused_computation.24 | convolution fusion | flops 373053440 | bytes 91849728 | tf_op jit(solution)/shard_map/dot_general | solution.py:398
  491.5 9.1 fusion.41
  500.7 11.0 fusion.3
  513.5 10.7 fusion.16
  526.6 117.2 %reduce-scatter.14.cloned.1.call-done = f32[512,1024]{1,0:T(8,128)} async-done(((f32[2048,1024]{1,0:T(8,128)}), f32[512,1024]{1,0:T(8,128)}) %reduce-scatter.14.cloned.1.call-update) | async-done | bytes 2097168 | tf_op jit(solution)/shard_map/reduce_scatter | solution.py:423
  643.8 283.2 %reduce-scatter.6.cloned.1.call-done = f32[256,4096]{1,0:T(8,128)} async-done(((f32[1024,4096]{1,0:T(8,128)}), f32[256,4096]{1,0:T(8,128)}) %reduce-scatter.6.cloned.1.call-update) | async-done | bytes 4194320 | tf_op jit(solution)/shard_map/reduce_scatter | solution.py:419
  928.4 12.8 %fusion.21 = (f32[1024]{0:T(1024)S(1)}, f32[768]{0:T(1024)S(1)}, f32[768,1024]{1,0:T(8,128)}) fusion(bf16[768,1024]{1,0:T(8,128)(2,1)S(1)} %copy-done.4, f32[768]{0:T(1024)S(1)} %copy-done.30, f32[1024]{0:T(1024)S(1)} %bitcast.37, bf16[1024,4096]{1,0:T(8,128)(2,1)} %all-gather.4.cloned.1.call-done, bf16[768,2048]{1,0:T(8,128)(2,1)} %get-tuple-element.49, ...), kind=kOutput, calls=%fused_computation.56 | convolution fusion | flops 6460536832 | bytes 19412992 | tf_op jit(solution)/shard_map/dot_general | solution.py:294
  941.2 11.2 all-reduce.10
  952.5 7.7 fusion.25
  960.2 26.4 %all-reduce.11 = (f32[256]{0:T(256)S(1)}, f32[23,512]{1,0:T(8,128)S(1)}) all-reduce(f32[256]{0:T(256)S(1)} %dynamic-slice.1, f32[23,512]{1,0:T(8,128)} %reduce-scatter.12.cloned.1.call-done), channel_id=1, replica_groups=mesh['dp'=8,'fsdp'=4] {'dp'}, use_global_device_ids=true, to_apply=%region_5.6 | all-reduce | flops 12032 | bytes 96256 | tf_op jit(solution)/shard_map/psum | solution.py:425
  987.8 73.8 %all-reduce.15.cloned.1.call-done = (f32[256,4096]{1,0:T(8,128)}, f32[96,512]{1,0:T(8,128)}, f32[64,512]{1,0:T(8,128)}, f32[512,1024]{1,0:T(8,128)}) async-done(((f32[256,4096]{1,0:T(8,128)}, f32[96,512]{1,0:T(8,128)}, f32[64,512]{1,0:T(8,128)}, f32[512,1024]{1,0:T(8,128)}), (f32[256,4096]{1,0:T(8,128)}, f32[96,512]{1,0:T(8,128)}, f32[64,512]{1,0:T(8,128)}, ...) | async-done | bytes 6619152 | tf_op jit(solution)/shard_map/psum | solution.py:425
  1061.6 3.9 multiply_reduce_fusion.5
  1075.3 4.0 fusion.23
  1079.2 12.2 %psum.55 = f32[]{:T(128)} all-reduce(f32[]{:T(128)S(6)} %add.265), channel_id=1, replica_groups=mesh['dp'=8,'fsdp'=4] {'fsdp'}, use_global_device_ids=true, to_apply=%region_29.30 | all-reduce | flops 1 | bytes 8 | tf_op jit(solution)/shard_map/psum | solution.py:430
  1092.9 8.8 fusion.15
  (179 shorter events, 43.8 us)
Async XLA Ops:
  7.2 27.2 %copy-start.52 = (f32[256]{0:T(256)S(1)}, f32[256]{0:T(256)}, u32[]{:S(2)}) copy-start(f32[256]{0:T(256)} %param.24) | copy-start | bytes 3076
  7.2 92.7 %copy-start.3 = (bf16[768,1024]{1,0:T(8,128)(2,1)S(1)}, bf16[768,1024]{1,0:T(8,128)(2,1)}, u32[]{:S(2)}) copy-start(bf16[768,1024]{1,0:T(8,128)(2,1)} %param.21) | copy-start | bytes 4718596
  7.2 168.2 %all-gather.4.cloned.1.call-start = ((), (), s32[]{:S(2)}) async-start(), calls=%async_computation.5 | async-start | bytes 10485760 | tf_op jit(solution)/shard_map/all_gather | solution.py:340
  11.3 245.8 %all-gather.6.cloned.1.call-start = ((), (), s32[]{:S(2)}) async-start(), calls=%async_computation.6 | async-start | bytes 5242880 | tf_op jit(solution)/shard_map/all_gather | solution.py:343
  14.1 512.5 %reduce-scatter.10.cloned.1.call-start = ((), (), s32[]{:S(2)}) async-start(), calls=%async_computation.9 | async-start | bytes 655360 | tf_op jit(solution)/shard_map/reduce_scatter | solution.py:421
  33.0 151.7 %copy-start.18 = (f32[23,2048]{1,0:T(8,128)}, f32[23,2048]{1,0:T(8,128)S(1)}, u32[]{:S(2)}) copy-start(f32[23,2048]{1,0:T(8,128)S(1)} %all_gather.18) | copy-start | bytes 565252
  52.6 132.1 %copy-start.27 = (f32[4,1,256]{2,1,0:T(1,128)}, f32[4,1,256]{2,1,0:T(1,128)S(1)}, u32[]{:S(2)}) copy-start(f32[4,1,256]{2,1,0:T(1,128)S(1)} %all-gather) | copy-start | bytes 12292
  72.2 184.9 %copy-start.49 = (f32[768]{0:T(1024)}, f32[768]{0:T(1024)S(1)}, u32[]{:S(2)}) copy-start(f32[768]{0:T(1024)S(1)} %compare_convert_fusion.2) | copy-start | bytes 9220
  72.2 184.8 %copy-start.47 = (f32[768]{0:T(1024)}, f32[768]{0:T(1024)S(1)}, u32[]{:S(2)}) copy-start(f32[768]{0:T(1024)S(1)} %fusion.75) | copy-start | bytes 9220
  72.9 184.2 %copy-start.50 = (f32[768]{0:T(1024)}, f32[768]{0:T(1024)S(1)}, u32[]{:S(2)}) copy-start(f32[768]{0:T(1024)S(1)} %get-tuple-element.69) | copy-start | bytes 9220
  72.9 184.2 %copy-start.51 = (f32[768]{0:T(1024)}, f32[768]{0:T(1024)S(1)}, u32[]{:S(2)}) copy-start(f32[768]{0:T(1024)S(1)} %get-tuple-element.70) | copy-start | bytes 9220
  100.3 84.4 %copy-start.40 = (f32[768]{0:T(1024)}, f32[768]{0:T(1024)S(1)}, u32[]{:S(2)}) copy-start(f32[768]{0:T(1024)S(1)} %fusion.24) | copy-start | bytes 9220
  100.3 84.4 %copy-start.29 = (f32[768]{0:T(1024)}, f32[768]{0:T(1024)S(1)}, u32[]{:S(2)}) copy-start(f32[768]{0:T(1024)S(1)} %fusion.76) | copy-start | bytes 9220
  100.9 156.1 %copy-start.42 = (f32[1,2048]{1,0:T(1,128)}, f32[1,2048]{1,0:T(1,128)S(1)}, u32[]{:S(2)}) copy-start(f32[1,2048]{1,0:T(1,128)S(1)} %get-tuple-element.55) | copy-start | bytes 24580
  100.9 156.2 %copy-start.43 = (f32[1,2048]{1,0:T(1,128)}, f32[1,2048]{1,0:T(1,128)S(1)}, u32[]{:S(2)}) copy-start(f32[1,2048]{1,0:T(1,128)S(1)} %get-tuple-element.56) | copy-start | bytes 24580
  100.9 156.2 %copy-start.44 = (f32[1,2048]{1,0:T(1,128)}, f32[1,2048]{1,0:T(1,128)S(1)}, u32[]{:S(2)}) copy-start(f32[1,2048]{1,0:T(1,128)S(1)} %get-tuple-element.57) | copy-start | bytes 24580
  439.9 86.8 %reduce-scatter.8.cloned.1.call-start = ((), (), s32[]{:S(2)}) async-start(), calls=%async_computation.8 | async-start | bytes 983040 | tf_op jit(solution)/shard_map/reduce_scatter | solution.py:420
  456.2 187.6 %reduce-scatter.14.cloned.1.call-start = ((), (), s32[]{:S(2)}) async-start(), calls=%async_computation.11 | async-start | bytes 10485760 | tf_op jit(solution)/shard_map/reduce_scatter | solution.py:423
  456.3 35.2 %copy-start.48 = (f32[768]{0:T(1024)S(1)}, f32[768]{0:T(1024)}, u32[]{:S(2)}) copy-start(f32[768]{0:T(1024)} %copy-done.47) | copy-start | bytes 9220
  500.6 426.4 %reduce-scatter.6.cloned.1.call-start = ((), (), s32[]{:S(2)}) async-start(), calls=%async_computation.7 | async-start | bytes 20971520 | tf_op jit(solution)/shard_map/reduce_scatter | solution.py:419
  500.7 12.8 %copy-start.4 = (bf16[768,1024]{1,0:T(8,128)(2,1)S(1)}, bf16[768,1024]{1,0:T(8,128)(2,1)}, u32[]{:S(2)}) copy-start(bf16[768,1024]{1,0:T(8,128)(2,1)} %param.21) | copy-start | bytes 4718596
  500.7 12.8 %copy-start.7 = (bf16[768,2048]{1,0:T(8,128)(2,1)S(1)}, bf16[768,2048]{1,0:T(8,128)(2,1)}, u32[]{:S(2)}) copy-start(bf16[768,2048]{1,0:T(8,128)(2,1)} %get-tuple-element.49) | copy-start | bytes 9437188
  524.2 402.9 %copy-start.57 = (u32[32]{0:T(128)S(1)}, u32[32]{0:T(128)}, u32[]{:S(2)}) copy-start(u32[32]{0:T(128)} %constant.133) | copy-start | bytes 388
  524.2 435.9 %reduce-scatter.12.cloned.1.call-start = ((), (), s32[]{:S(2)}) async-start(), calls=%async_computation.10 | async-start | bytes 245760 | tf_op jit(solution)/shard_map/reduce_scatter | solution.py:422
  526.5 535.1 %all-reduce.15.cloned.1.call-start = ((), (), s32[]{:S(2)}) async-start(), calls=%async_computation.12 | async-start | bytes 13238272 | tf_op jit(solution)/shard_map/psum | solution.py:425
  928.3 24.1 %copy-start.41 = (f32[768]{0:T(1024)S(1)}, f32[768]{0:T(1024)}, u32[]{:S(2)}) copy-start(f32[768]{0:T(1024)} %copy-done.40) | copy-start | bytes 9220
  960.2 115.1 %copy-start.16 = (bf16[768,1024]{1,0:T(8,128)(2,1)S(1)}, bf16[768,1024]{1,0:T(8,128)(2,1)}, u32[]{:S(2)}) copy-start(bf16[768,1024]{1,0:T(8,128)(2,1)} %param.23) | copy-start | bytes 4718596
  986.5 105.6 %copy-start.56 = (f32[256]{0:T(256)}, f32[256]{0:T(256)S(1)}, u32[]{:S(2)}) copy-start(f32[256]{0:T(256)S(1)} %get-tuple-element.82) | copy-start | bytes 3076
  986.6 119.7 %copy-start.33 = (f32[23,512]{1,0:T(8,128)}, f32[23,512]{1,0:T(8,128)S(1)}, u32[]{:S(2)}) copy-start(f32[23,512]{1,0:T(8,128)S(1)} %get-tuple-element.86) | copy-start | bytes 141316
  1061.6 30.6 %copy-start.53 = (f32[256]{0:T(256)S(1)}, f32[256]{0:T(256)}, u32[]{:S(2)}) copy-start(f32[256]{0:T(256)} %param.24) | copy-start | bytes 3076
  1061.6 30.6 %copy-start.54 = (f32[256]{0:T(256)S(1)}, f32[256]{0:T(256)}, u32[]{:S(2)}) copy-start(f32[256]{0:T(256)} %param.36) | copy-start | bytes 3076
  1061.6 30.6 %copy-start.55 = (f32[256]{0:T(256)S(1)}, f32[256]{0:T(256)}, u32[]{:S(2)}) copy-start(f32[256]{0:T(256)} %param.30) | copy-start | bytes 3076
  (34 other events, 244.7 us)
Sparse Core Ops, SparseCore 0:
  11.4 164.0 all-gather.3
  177.6 79.4 all-gather.5
  440.0 20.1 reduce-scatter.9
  462.9 21.6 reduce-scatter.7
  500.7 143.0 reduce-scatter.13
  646.0 280.9 reduce-scatter.5
  930.0 20.1 reduce-scatter.11
  953.8 107.7 all-reduce.14

commit v2 on v1

--- a/solution.py
+++ b/solution.py
@@ -290,6 +290,259 @@
     )(dt, mixed, gs, sel, rates, states, states)
 
 
+def mesh_copy(src, dst, sems, at, device):
+    return pltpu.make_async_remote_copy(
+        src_ref=src,
+        dst_ref=dst,
+        send_sem=sems.at[0, at],
+        recv_sem=sems.at[1, at],
+        device_id=device,
+        device_id_type=pl.DeviceIdType.MESH,
+    )
+
+
+def placed(plan):
+    group = lax.axis_index("dp")
+    return lax.axis_index("fsdp"), group // 2, lax.rem(group, 2)
+
+
+def peers_of(plan):
+    shards, places = plan
+    mine, place, side = placed(plan)
+    along = [(place * 2 + side, lax.rem(mine + k, shards)) for k in range(1, shards)]
+    plane = [((place ^ j) * 2 + side, mine) for j in range(1, places)]
+    return along, plane, (place * 2 + 1 - side, mine)
+
+
+def greet(plan):
+    along, plane, pair = peers_of(plan)
+    barrier = pltpu.get_barrier_semaphore()
+    everyone = along + plane + [pair]
+    for device in everyone:
+        pl.semaphore_signal(barrier, inc=1, device_id=device, device_id_type=pl.DeviceIdType.MESH)
+    pl.semaphore_wait(barrier, len(everyone))
+
+
+def gather_kernel(plan, count, *refs):
+    own, full = refs[:count], refs[count : 2 * count]
+    near, far, wide, cross = refs[2 * count :]
+    shards, places = plan
+    mine, place, side = placed(plan)
+    along, plane, pair = peers_of(plan)
+    greet(plan)
+    local, first, second, third = [], [], [], []
+    for s in range(count):
+        keep = pltpu.make_async_copy(own[s], full[s].at[mine, place, side], near.at[s])
+        keep.start()
+        local.append(keep)
+        sends = [
+            mesh_copy(own[s], full[s].at[mine, place, side], far, s * (shards - 1) + k, device)
+            for k, device in enumerate(along)
+        ]
+        for copy in sends:
+            copy.start()
+        first.append(sends)
+    for s in range(count):
+        local[s].wait()
+        for copy in first[s]:
+            copy.wait_recv()
+        sends = [
+            mesh_copy(
+                full[s].at[:, place, side], full[s].at[:, place, side], wide, s * (places - 1) + k, device
+            )
+            for k, device in enumerate(plane)
+        ]
+        for copy in sends:
+            copy.start()
+        second.append(sends)
+    for s in range(count):
+        for copy in second[s]:
+            copy.wait_recv()
+        copy = mesh_copy(full[s].at[:, :, side], full[s].at[:, :, side], cross, s, pair)
+        copy.start()
+        third.append(copy)
+    for s in range(count):
+        for copy in first[s] + second[s]:
+            copy.wait_send()
+        third[s].wait()
+
+
+def gather_pieces(plan, pieces, name, collective_id):
+    shards, places = plan
+    count = len(pieces)
+    return pl.pallas_call(
+        functools.partial(gather_kernel, plan, count),
+        in_specs=[pl.BlockSpec(memory_space=pl.ANY)] * count,
+        out_specs=[pl.BlockSpec(memory_space=pl.ANY)] * count,
+        out_shape=[jax.ShapeDtypeStruct((shards, places, 2) + piece.shape, piece.dtype) for piece in pieces],
+        scratch_shapes=[
+            pltpu.SemaphoreType.DMA((count,)),
+            pltpu.SemaphoreType.DMA((2, count * (shards - 1))),
+            pltpu.SemaphoreType.DMA((2, count * (places - 1))),
+            pltpu.SemaphoreType.DMA((2, count)),
+        ],
+        compiler_params=pltpu.CompilerParams(collective_id=collective_id, has_side_effects=True),
+        cost_estimate=pl.CostEstimate(flops=0, bytes_accessed=32 << 20, transcendentals=0),
+        name=name,
+    )(*pieces)
+
+
+def wide_sum(values):
+    total = values[0].astype(jnp.float32)
+    for value in values[1:]:
+        total = total + value.astype(jnp.float32)
+    return total.astype(jnp.bfloat16)
+
+
+def reduce_kernel(plan, count, *refs):
+    parts, full = refs[:count], refs[count : 2 * count]
+    held = refs[2 * count : 3 * count]
+    from_pair = refs[3 * count : 4 * count]
+    from_plane = refs[4 * count : 5 * count]
+    from_along = refs[5 * count : 6 * count]
+    near, cross, wide, far, back, over = refs[6 * count :]
+    shards, places = plan
+    mine, place, side = placed(plan)
+    along, plane, pair = peers_of(plan)
+    greet(plan)
+    local, first, second, third, fourth, fifth = [], [], [], [], [], []
+    for s in range(count):
+        keep = pltpu.make_async_copy(parts[s].at[:, :, side], held[s], near.at[s])
+        keep.start()
+        local.append(keep)
+        copy = mesh_copy(parts[s].at[:, :, 1 - side], from_pair[s], cross, s, pair)
+        copy.start()
+        first.append(copy)
+    for s in range(count):
+        local[s].wait()
+        first[s].wait_recv()
+
+        @pl.loop(0, shards * places)
+        def _(i, s=s):
+            a, b = i // places, lax.rem(i, places)
+            held[s][a, b] = wide_sum([held[s][a, b], from_pair[s][a, b]])
+
+        sends = [
+            mesh_copy(held[s].at[:, place ^ (k + 1)], from_plane[s].at[k], wide, s * (places - 1) + k, device)
+            for k, device in enumerate(plane)
+        ]
+        for copy in sends:
+            copy.start()
+        second.append(sends)
+    for s in range(count):
+        for copy in second[s]:
+            copy.wait_recv()
+
+        @pl.loop(0, shards)
+        def _(i, s=s):
+            held[s][i, place] = wide_sum([held[s][i, place]] + [from_plane[s][k, i] for k in range(places - 1)])
+
+        sends = [
+            mesh_copy(
+                held[s].at[lax.rem(mine + k + 1, shards), place],
+                from_along[s].at[k],
+                far,
+                s * (shards - 1) + k,
+                device,
+            )
+            for k, device in enumerate(along)
+        ]
+        for copy in sends:
+            copy.start()
+        third.append(sends)
+    for s in range(count):
+        for copy in third[s]:
+            copy.wait_recv()
+        full[s][place, side] = wide_sum([held[s][mine, place]] + [from_along[s][k] for k in range(shards - 1)])
+        sends = [
+            mesh_copy(full[s].at[place, side], full[s].at[place, side], back, s * (places - 1) + k, device)
+            for k, device in enumerate(plane)
+        ]
+        for copy in sends:
+            copy.start()
+        fourth.append(sends)
+    for s in range(count):
+        for copy in fourth[s]:
+            copy.wait_recv()
+        copy = mesh_copy(full[s].at[:, side], full[s].at[:, side], over, s, pair)
+        copy.start()
+        fifth.append(copy)
+    for s in range(count):
+        first[s].wait_send()
+        for copy in second[s] + third[s] + fourth[s]:
+            copy.wait_send()
+        fifth[s].wait()
+
+
+def reduce_pieces(plan, parts, name, collective_id):
+    shards, places = plan
+    count = len(parts)
+    tails = [part.shape[3:] for part in parts]
+
+    def scratch(*lead):
+        return [pltpu.VMEM(lead + tail, jnp.bfloat16) for tail in tails]
+
+    return pl.pallas_call(
+        functools.partial(reduce_kernel, plan, count),
+        in_specs=[pl.BlockSpec(memory_space=pl.ANY)] * count,
+        out_specs=[pl.BlockSpec(memory_space=pltpu.VMEM)] * count,
+        out_shape=[jax.ShapeDtypeStruct((places, 2) + tail, jnp.bfloat16) for tail in tails],
+        scratch_shapes=scratch(shards, places)
+        + scratch(shards, places)
+        + scratch(places - 1, shards)
+        + scratch(shards - 1)
+        + [
+            pltpu.SemaphoreType.DMA((count,)),
+            pltpu.SemaphoreType.DMA((2, count)),
+            pltpu.SemaphoreType.DMA((2, count * (places - 1))),
+            pltpu.SemaphoreType.DMA((2, count * (shards - 1))),
+            pltpu.SemaphoreType.DMA((2, count * (places - 1))),
+            pltpu.SemaphoreType.DMA((2, count)),
+        ],
+        compiler_params=pltpu.CompilerParams(
+            collective_id=collective_id, has_side_effects=True, vmem_limit_bytes=48 << 20
+        ),
+        cost_estimate=pl.CostEstimate(flops=0, bytes_accessed=32 << 20, transcendentals=0),
+        name=name,
+    )(*parts)
+
+
+def cut_of(rows, columns, dp):
+    best = None
+    across = 1
+    while across <= dp and across * LANES <= columns:
+        down = dp // across
+        tall = -(-rows // (16 * down)) * 16
+        if best is None or down * tall < best[0] * best[2]:
+            best = (down, across, tall)
+        across *= 2
+    return best
+
+
+def to_pieces(shards, array, dp):
+    rows, columns = array.shape[1:]
+    down, across, tall = cut_of(rows, columns, dp)
+    array = jnp.pad(array, ((0, 0), (0, down * tall - rows), (0, 0)))
+    array = array.reshape(shards, down, tall, across, columns // across).transpose(0, 1, 3, 2, 4)
+    return array.reshape(shards, dp // 2, 2, tall, columns // across)
+
+
+def from_pieces(pieces, rows, columns, dp):
+    shards = pieces.shape[0]
+    down, across, tall = cut_of(rows, columns, dp)
+    array = pieces.reshape(shards, down, across, tall, columns // across).transpose(0, 1, 3, 2, 4)
+    return array.reshape(shards, down * tall, columns)[:, :rows]
+
+
+def own_piece(array, dp):
+    rows, columns = array.shape
+    down, across, tall = cut_of(rows, columns, dp)
+    array = jnp.pad(array, ((0, down * tall - rows), (0, 0)))
+    group = lax.axis_index("dp")
+    at = (group // across * tall, lax.rem(group, across) * (columns // across))
+    return lax.dynamic_slice(array, at, (tall, columns // across))
+
+
 def contract(left, right, left_dim, right_dim):
     return lax.dot_general(
         left, right, (((left_dim,), (right_dim,)), ((), ())), preferred_element_type=jnp.float32
@@ -311,6 +564,8 @@
 
 
 def local(
+    shards,
+    dp,
     tokens,
     lengths,
     cotangent,
@@ -336,16 +591,27 @@
     row_count = tokens.shape[0]
     live_mask, offset = block_layout(lengths[0], row_count)
     restart = (offset == 0).astype(jnp.float32)
-    full_input, full_select, full_step, full_output = (
-        lax.all_gather(input_weight.astype(jnp.bfloat16), "fsdp", axis=0, tiled=True),
-        lax.all_gather(select_weight.astype(jnp.bfloat16), "fsdp", axis=1, tiled=True),
-        lax.all_gather(step_weight.astype(jnp.bfloat16), "fsdp", axis=1, tiled=True),
-        lax.all_gather(output_weight.astype(jnp.bfloat16), "fsdp", axis=0, tiled=True),
-    )
-    gain, channel = (
-        lax.all_gather(norm_gain, "fsdp", axis=0, tiled=True),
-        lax.all_gather(channel_params, "fsdp", axis=1, tiled=True),
-    )
+    plan = (shards, dp // 2)
+    low_conv, low_gate, low_output = (
+        own_piece(weight, dp).astype(jnp.bfloat16)
+        for weight in (input_weight[:, :DI], input_weight[:, DI:], output_weight)
+    )
+    low_small = own_piece(jnp.concatenate([select_weight, step_weight], axis=0), dp).astype(jnp.bfloat16)
+    width = channel_params.shape[1]
+    vectors = jnp.concatenate(
+        [channel_params, jnp.pad(norm_gain, (0, width - norm_gain.shape[0]))[None, :]], axis=0
+    )
+    full_conv, full_small, full_vectors, full_gate, full_output = gather_pieces(
+        plan, [low_conv, low_small, own_piece(vectors, dp), low_gate, low_output], "gather_weights", 0
+    )
+    full_input = jnp.concatenate([full_conv.reshape(-1, DI), full_gate.reshape(-1, DI)], axis=1)
+    full_output = full_output.reshape(DI, -1)
+    small_rows = R + 2 * N + R
+    full_small = from_pieces(full_small, small_rows, width, dp).transpose(1, 0, 2).reshape(small_rows, DI)
+    full_select, full_step = full_small[: R + 2 * N], full_small[R + 2 * N :]
+    full_vectors = from_pieces(full_vectors, vectors.shape[0], width, dp)
+    gain = full_vectors[:, -1, : norm_gain.shape[0]].reshape(-1)
+    channel = full_vectors[:, :-1].transpose(1, 0, 2).reshape(-1, DI)
     inputs = tokens.astype(jnp.float32)
     normed_value, norm_pull = jax.vjp(rms_scale, inputs, gain)
     normed = normed_value.astype(jnp.bfloat16)
@@ -380,7 +646,7 @@
     layer_output = (inputs + live_mask[:, None] * branch).astype(jnp.bfloat16)
     upstream = cotangent.astype(jnp.float32)
     grad_branch = (upstream * live_mask[:, None]).astype(jnp.bfloat16)
-    grad_output = contract(gated, grad_branch, 0, 0)
+    grad_output = contract(gated, grad_branch, 0, 0).astype(jnp.bfloat16)
     grad_gated = contract(grad_branch, full_output, 1, 1)
     grad_scanned = grad_gated * gate_value
     (grad_gate,) = gate_pull(grad_gated * scanned)
@@ -400,7 +666,10 @@
     )
     grad_conv_input, grad_kernel, grad_shift = conv_pull(grad_mixed)
     grad_projected = jnp.concatenate([grad_conv_input, grad_gate], axis=1).astype(jnp.bfloat16)
-    grad_input = contract(normed, grad_projected, 0, 0)
+    grad_conv_weight, grad_gate_weight = (
+        contract(normed, half, 0, 0).astype(jnp.bfloat16)
+        for half in (grad_projected[:, :DI], grad_projected[:, DI:])
+    )
     grad_normed = contract(grad_projected, full_input, 1, 1)
     grad_inputs, grad_gain = norm_pull(grad_normed)
     input_grad = (upstream + grad_inputs).astype(jnp.bfloat16)
@@ -414,17 +683,34 @@
         ],
         axis=0,
     )
-    owned_gain, owned_input, owned_select, owned_step, owned_channel, owned_output = (
-        lax.psum_scatter(grad_gain, "fsdp", scatter_dimension=0, tiled=True),
-        lax.psum_scatter(grad_input, "fsdp", scatter_dimension=0, tiled=True),
-        lax.psum_scatter(grad_select, "fsdp", scatter_dimension=1, tiled=True),
-        lax.psum_scatter(grad_step, "fsdp", scatter_dimension=1, tiled=True),
-        lax.psum_scatter(grad_channel, "fsdp", scatter_dimension=1, tiled=True),
-        lax.psum_scatter(grad_output, "fsdp", scatter_dimension=0, tiled=True),
-    )
-    sum_gain, sum_input, sum_select, sum_step, sum_channel, sum_output = lax.psum(
-        (owned_gain, owned_input, owned_select, owned_step, owned_channel, owned_output), "dp"
-    )
+    small = jnp.concatenate([grad_select, grad_step, grad_channel], axis=0)
+    small = small.reshape(-1, shards, width).transpose(1, 0, 2)
+    small_gain = jnp.pad(grad_gain.reshape(shards, 1, -1), ((0, 0), (0, 0), (0, width - grad_gain.shape[0] // shards)))
+    small = jnp.concatenate([small, small_gain], axis=1).astype(jnp.bfloat16)
+    heights = [norm_gain.shape[0], output_weight.shape[0]]
+    sum_output, sum_gate, sum_conv, sum_small = reduce_pieces(
+        plan,
+        [
+            to_pieces(shards, grad_output.reshape(shards, heights[1], -1), dp),
+            to_pieces(shards, grad_gate_weight.reshape(shards, heights[0], -1), dp),
+            to_pieces(shards, grad_conv_weight.reshape(shards, heights[0], -1), dp),
+            to_pieces(shards, small, dp),
+        ],
+        "sum_gradients",
+        1,
+    )
+    sum_output, sum_gate, sum_conv, sum_small = (
+        from_pieces(pieces[None], rows, columns, dp)[0].astype(jnp.float32)
+        for pieces, rows, columns in (
+            (sum_output, heights[1], output_weight.shape[1]),
+            (sum_gate, heights[0], DI),
+            (sum_conv, heights[0], DI),
+            (sum_small, small.shape[1], width),
+        )
+    )
+    sum_input = jnp.concatenate([sum_conv, sum_gate], axis=1)
+    sum_select, sum_step = sum_small[: R + 2 * N], sum_small[R + 2 * N : small_rows]
+    sum_channel, sum_gain = sum_small[small_rows:-1], sum_small[-1, : norm_gain.shape[0]]
     grads = (sum_gain, sum_input, sum_select, sum_step, sum_channel, sum_output)
     local_square = sum([jnp.sum(grad * grad) for grad in grads])
     total_square = lax.psum(local_square, "fsdp")
@@ -500,4 +786,5 @@
         P(None, "fsdp"),
         P("fsdp", None),
     )
-    return jax.shard_map(local, mesh=mesh, in_specs=in_specs, out_specs=out_specs, check_vma=False)
+    shards, dp = mesh.shape["fsdp"], mesh.shape["dp"]
+    return jax.shard_map(functools.partial(local, shards, dp), mesh=mesh, in_specs=in_specs, out_specs=out_specs, check_vma=False)

time: 1130 us -> 578 us (0.51)
  waiting for transfers between devices: 613 us -> 0 us
  Pallas kernels: 133 us -> 341 us
  blocking collectives: 128 us -> 11.3 us
  between operations: 24.8 us -> 11.1 us
    reduce_scatter x5 -> x0, waiting for transfers between devices: 400 us -> none  [the longest x1 283 us: local(): lax.psum_scatter(grad_input, 'fsdp', scatter_dimension=0, tiled=True)]
    pallas_call x0 -> x2, Pallas kernels: none -> 208 us  [the longest x1 112 us: reduce_pieces(): pl.pallas_call(functools.partial(reduce_kernel, plan, count), in_specs=[p...]
    all_gather x2 -> x0, waiting for transfers between devices: 139 us -> none  [the longest x1 74.5 us: local(): lax.all_gather(input_weight.astype(jnp.bfloat16), 'fsdp', axis=0, tiled=T...]
    all_gather x4 -> x0, blocking collectives: 78.7 us -> none  [the longest x1 25.4 us: local(): lax.all_gather(select_weight.astype(jnp.bfloat16), 'fsdp', axis=1, tiled=...]
    psum x1 -> x0, waiting for transfers between devices: 73.8 us -> none  [local(): lax.psum((owned_gain, owned_input, owned_select, owned_step, owned_channe...]
    psum x1 -> x0, blocking collectives: 26.4 us -> none  [local(): lax.psum((owned_gain, owned_input, owned_select, owned_step, owned_channe...]
    dot_general x8 -> x9, matrix products: 66.9 us -> 62.4 us  [contract(): lax.dot_general(left, right, (((left_dim,), (right_dim,)), ((), ())), pre...]
  transfers between devices with their start and end apart: 8 -> 0, of which waited for: 5 -> 0; matrix products, arithmetic and copies ran while one was open for 11% -> 0% of each run, Pallas kernels for 0% -> 0%
where the time goes in v2:
time: 578 us; the launch traced here: 571 us
  Pallas kernels  341 us (59%)
  matrix products  124 us (21%)
  other arithmetic  59.6 us (10%)
  local copies, waits for them, and re-layouts  24.3 us (4%)
  blocking collectives  11.3 us (2%)
  between operations  11.1 us (2%)
    pallas_call x1, Pallas kernels, reduce_pieces(): pl.pallas_call(functools.partial(reduce_kernel, plan, count), in_specs=[p...  112 us
    pallas_call x1, Pallas kernels, gather_pieces(): pl.pallas_call(functools.partial(gather_kernel, plan, count), in_specs=[p...  95.3 us
    pallas_call x1, Pallas kernels, scan_backward(): pl.pallas_call(backward_kernel, grid=(blocks,), in_specs=[rows, rows, row...  88.5 us
    dot_general x9, matrix products, contract(): lax.dot_general(left, right, (((left_dim,), (right_dim,)), ((), ())), pre...  62.4 us
    pallas_call x1, Pallas kernels, scan_forward(): pl.pallas_call(forward_kernel, grid=(count // BLOCK,), in_specs=[rows, ro...  44.7 us
    dot_general x1, matrix products, local(): jnp.dot(grad_selection, full_select, preferred_element_type=jnp.float32)  35.5 us
    add x6, other arithmetic, adam_direction(): first_hat / (jnp.sqrt(second_hat) + adam_eps) + decay_rate * decay * weight  15.4 us

profile of v2, /device:TPU:0, one launch (start us, length us, event | category | flops | bytes accessed | tf_op | source)
XLA Modules:
  0.0 570.7 jit_solution(5338908265622018164)
XLA Ops:
  0.7 3.6 fusion.94
  4.4 1.6 dynamic-slice_convert_fusion.1
  7.3 1.6 dynamic-slice_convert_fusion.refs_4_
  8.9 95.3 %gather_weights.1 = (bf16[4,4,2,32,2048]{4,3,2,1,0:T(8,128)(2,1)}, bf16[4,4,2,80,128]{4,3,2,1,0:T(8,128)(2,1)}, f32[4,4,2,16,128]{4,3,2,1,0:T(8,128)}, bf16[4,4,...) custom-call(bf16[32,2048]{1,0:T(8,128)(2,1)} %get-tuple-element.96.refs_0_, bf16[80,128]{1,0:T(8,128)(2,1)} %fusion.74.refs_1_, ...), custom_call_target="tpu_custom_call" | custom-call | bytes 33554432 | tf_op jit(solution)/shard_map/gather_weights/pallas_call | solution.py:373
  105.9 9.4 %fusion.14 = f32[768,4096]{1,0:T(8,128)S(1)} fusion(bf16[1024,2048]{1,0:T(8,128)(2,1)} %bitcast.139, bf16[1024,2048]{1,0:T(8,128)(2,1)} %bitcast.137, bf16[768,1024]{1,0:T(8,128)(2,1)S(1)} %copy-done.4, f32[1024]{0:T(1024)S(1)} %bitcast.116, f32[768]{0:T(1024)S(1)} %fusion.81), kind=kOutput, calls=%fused_computation.45 | convolution fusion | flops 6462373888 | bytes 22551552 | tf_op jit(solution)/shard_map/dot_general | solution.py:618
  115.4 3.1 slice.177
  118.5 3.2 copy-done.7
  128.2 26.8 %multiply_reduce_fusion = (bf16[2048]{0:T(1024)(128)(2,1)}, f32[768,2048]{1,0:T(8,128)}, bf16[768,2048]{1,0:T(8,128)(2,1)S(1)}, f32[768,2048]{1,0:T(8,128)}, f32[768,2048]{1,0:T(8,128)}) fusion(f32[768,4096]{1,0:T(8,128)} %copy-done.7, f32[768]{0:T(1024)S(1)} %get-tuple-element.97, f32[768,2048]{1,0:T(8,128)} %slice.177, f32[2048]{0:T(1024)S(1)} %bitcast.122, ...), kind=kOutput, calls=%fused_computation.24 | convolution fusion | flops 3261331456 | bytes 40427520 | tf_op jit(solution)/shard_map/dot_general | solution.py:547
  157.1 8.2 %compare_select_fusion = (f32[768,2048]{1,0:T(8,128)}, f32[768,2048]{1,0:T(8,128)}) fusion(f32[2048]{0:T(1024)S(1)} %bitcast.112, bf16[64,2048]{1,0:T(8,128)(2,1)S(1)} %bitcast.105, f32[768,96]{0,1:T(8,128)S(1)} %fusion.97), kind=kOutput, calls=%fused_computation | convolution fusion | flops 212336640 | bytes 12951552 | tf_op jit(solution)/shard_map/dot_general | solution.py:632
  165.3 3.5 convert_element_type.142.mixed_ref
  170.3 44.7 %scan_forward.1 = (f32[768,2048]{1,0:T(8,128)}, f32[768,32,8,128]{3,2,1,0:T(8,128)}) custom-call(f32[768,2048]{1,0:T(8,128)} %get-tuple-element.91.dt_ref, f32[768,2048]{1,0:T(8,128)} %convert_element_type.142.mixed_ref, f32[768,128]{1,0:T(8,128)S(1)} %maximum_maximum_fusion.sel, f32[32,8,128]{2,1,0:T(8,128)S(1)} %mul.569.rates), custom_call_target="tpu_custom_call" | custom-call | flops 150994944 | bytes 100663296 | tf_op jit(solution)/shard_map/scan_forward/pallas_call | solution.py:220
  215.0 88.5 %scan_backward.1 = (f32[768,2048]{1,0:T(8,128)}, f32[768,2048]{1,0:T(8,128)}, f32[768,32,128]{2,1,0:T(8,128)}, f32[32,8,128]{2,1,0:T(8,128)S(1)}) custom-call(f32[768,2048]{1,0:T(8,128)} %get-tuple-element.91.dt_ref, f32[768,2048]{1,0:T(8,128)} %convert_element_type.142.mixed_ref, f32[768,2048]{1,0:T(8,128)} %get-tuple-element.63.gs_ref, ...), custom_call_target="tpu_custom_call" | custom-call | flops 377487360 | bytes 100663296 | tf_op jit(solution)/shard_map/scan_backward/pallas_call | solution.py:253
  303.5 8.8 %reduce_sum.149 = bf16[768,32]{1,0:T(8,128)(2,1)} reduce(f32[768,32,128]{2,1,0:T(8,128)} %get-tuple-element.39, f32[]{:T(128)} %constant.65.clone.1), dimensions={2}, to_apply=%region_1.2 | reduce | flops 3121152 | bytes 12632068 | tf_op jit(solution)/shard_map/reduce_sum | solution.py:656
  312.3 1.7 copy.70
  313.9 8.6 %fusion.93 = (bf16[2048]{0:T(1024)(128)(2,1)}, bf16[768,2048]{1,0:T(8,128)(2,1)S(1)}) fusion(f32[768,2048]{1,0:T(8,128)} %get-tuple-element.92, f32[2048]{0:T(1024)S(1)} %bitcast.113, f32[768,2048]{1,0:T(8,128)} %get-tuple-element.38, f32[768,2048]{1,0:T(8,128)} %get-tuple-element.37, bf16[768,2048]{1,0:T(8,128)(2,1)S(1)} %copy-done.1), kind=kLoop, calls=%fused_computation.180 | loop fusion | flops 17299456 | bytes 25178112 | tf_op jit(solution)/shard_map/reduce_sum | solution.py:681
  322.5 1.6 copy-done.2
  324.1 1.7 fusion.40
  325.9 35.5 %multiply_reduce_fusion.4 = (f32[2048]{0:T(1024)S(1)}, f32[2048]{0:T(1024)}, f32[2048]{0:T(1024)}, bf16[2048]{0:T(1024)(128)(2,1)}, f32[2048]{0:T(1024)}, /*inde...) fusion(f32[768,2048]{1,0:T(8,128)} %slice.177, ...), kind=kOutput, calls=%fused_computation.28 | convolution fusion | flops 373053440 | bytes 91845632 | tf_op jit(solution)/shard_map/dot_general | solution.py:664
  361.4 8.3 %fusion.28 = bf16[768,1024]{1,0:T(8,128)(2,1)} fusion(bf16[768,1024]{1,0:T(8,128)(2,1)} %param.21, bf16[768,2048]{1,0:T(8,128)(2,1)} %get-tuple-element.70, bf16[2048,1024]{1,0:T(8,128)(2,1)} %bitcast.142, f32[768]{0:T(1024)S(1)} %copy-done.53), kind=kOutput, calls=%fused_computation.66 | convolution fusion | flops 3224371200 | bytes 10488832 | tf_op jit(solution)/shard_map/dot_general | solution.py:645
  369.7 1.3 copy-done.6
  371.0 6.8 %fusion.3 = bf16[768,2048]{1,0:T(8,128)(2,1)} fusion(f32[768,2048]{1,0:T(8,128)S(1)} %copy-done.6, f32[768,2048]{1,0:T(8,128)S(1)} %bitcast.93, f32[768,2048]{1,0:T(8,128)S(1)} %bitcast.91, f32[768,2048]{1,0:T(8,128)} %get-tuple-element.93, f32[2048]{0:T(1024)S(1)} %bitcast.115), kind=kLoop, calls=%fused_computation.13 | loop fusion | flops 7864320 | bytes 28319744 | tf_op jit(solution)/shard_map/slice | solution.py:671
  377.8 14.0 %fusion.24 = (bf16[1024]{0:T(1024)(128)(2,1)S(1)}, f32[768]{0:T(1024)S(1)}, f32[768,1024]{1,0:T(8,128)}) fusion(bf16[768,1024]{1,0:T(8,128)(2,1)S(1)} %copy-done.5, f32[768]{0:T(1024)S(1)} %copy-done.41, f32[1024]{0:T(1024)S(1)} %bitcast.117, bf16[1024,2048]{1,0:T(8,128)(2,1)} %bitcast.140, bf16[1024,2048]{1,0:T(8,128)(2,1)} %bitcast.138, ...), kind=kOutput, calls=%fused_computation.62 | convolution fusion | flops 6477314048 | bytes 19410944 | tf_op jit(solution)/shard_map/dot_general | solution.py:547
  391.8 4.1 fusion.26
  395.9 5.2 convolution_convert_fusion.2
  401.2 5.5 convolution_convert_fusion.1
  406.6 5.7 %convolution_convert_fusion = bf16[1024,2048]{1,0:T(8,128)(2,1)} fusion(bf16[768,2048]{1,0:T(8,128)(2,1)S(1)} %copy-done.8, bf16[768,1024]{1,0:T(8,128)(2,1)S(1)} %copy-done.5, f32[1024]{0:T(1024)S(1)} %bitcast.120, f32[768]{0:T(1024)S(1)} %copy-done.41), kind=kOutput, calls=%fused_computation.56 | convolution fusion | flops 3226468352 | bytes 8920064 | tf_op jit(solution)/shard_map/dot_general | solution.py:547
  412.5 1.7 convolution_convert_fusion.3
  416.1 112.2 %sum_gradients.1 = (bf16[4,2,64,1024]{3,2,1,0:T(8,128)(2,1)S(1)}, bf16[4,2,32,2048]{3,2,1,0:T(8,128)(2,1)S(1)}, bf16[4,2,32,2048]{3,2,1,0:T(8,128)(2,1)S(1)}, bf16[4,2,48,256]{3,2,1,0:T(8,128)(2,1)S(1)}) custom-call(bf16[4,4,2,64,1024]{4,3,2,1,0:T(8,128)(2,1)} %bitcast.94, bf16[4,4,2,32,2048]{4,3,2,1,0:T(8,128)(2,1)} %bitcast.95, ...), custom_call_target="tpu_custom_call" | custom-call | bytes 33554432 | tf_op jit(solution)/shard_map/sum_gradients/pallas_call | solution.py:485
  530.9 3.6 multiply_reduce_fusion.5
  541.5 11.3 %psum.7 = f32[]{:T(128)} all-reduce(f32[]{:T(128)S(6)} %add.276), channel_id=1, replica_groups=mesh['dp'=8,'fsdp'=4] {'fsdp'}, use_global_device_ids=true, to_apply=%region_17.18 | all-reduce | flops 1 | bytes 8 | tf_op jit(solution)/shard_map/psum | solution.py:716
  554.3 8.8 %fusion.20 = f32[256,4096]{1,0:T(8,128)} fusion(f32[256,4096]{1,0:T(8,128)} %param.25, f32[256,4096]{1,0:T(8,128)} %param.37, f32[256,4096]{1,0:T(8,128)} %get-tuple-element.61, f32[256,4096]{1,0:T(8,128)} %param.31, f32[]{:T(128)S(6)} %min.3), kind=kLoop, calls=%fused_computation.52 | loop fusion | flops 14680064 | bytes 20971524 | tf_op jit(solution)/shard_map/add | solution.py:563
  565.5 3.7 fusion.35
  (194 shorter events, 20.0 us)
Async XLA Ops:
  0.6 104.8 %copy-start.4 = (bf16[768,1024]{1,0:T(8,128)(2,1)S(1)}, bf16[768,1024]{1,0:T(8,128)(2,1)}, u32[]{:S(2)}) copy-start(bf16[768,1024]{1,0:T(8,128)(2,1)} %param.21) | copy-start | bytes 4718596
  105.5 9.8 %copy-start.38 = (f32[4,1,256]{2,1,0:T(1,128)}, f32[4,1,256]{2,1,0:T(1,128)S(1)}, u32[]{:S(2)}) copy-start(f32[4,1,256]{2,1,0:T(1,128)S(1)} %slice.176) | copy-start | bytes 12292
  115.4 12.3 %copy-start.21 = (bf16[4,4,2,80,128]{4,3,2,1,0:T(8,128)(2,1)S(1)}, bf16[4,4,2,80,128]{4,3,2,1,0:T(8,128)(2,1)}, u32[]{:S(2)}) copy-start(bf16[4,4,2,80,128]{4,3,2,1,0:T(8,128)(2,1)} %get-tuple-element.33) | copy-start | bytes 1966084
  125.6 29.5 %copy-start.54 = (f32[768]{0:T(1024)}, f32[768]{0:T(1024)S(1)}, u32[]{:S(2)}) copy-start(f32[768]{0:T(1024)S(1)} %get-tuple-element.97) | copy-start | bytes 9220
  125.6 29.5 %copy-start.55 = (f32[768]{0:T(1024)}, f32[768]{0:T(1024)S(1)}, u32[]{:S(2)}) copy-start(f32[768]{0:T(1024)S(1)} %get-tuple-element.98) | copy-start | bytes 9220
  126.9 28.2 %copy-start.52 = (f32[768]{0:T(1024)}, f32[768]{0:T(1024)S(1)}, u32[]{:S(2)}) copy-start(f32[768]{0:T(1024)S(1)} %get-tuple-element.99) | copy-start | bytes 9220
  126.9 28.1 %copy-start.56 = (f32[768]{0:T(1024)}, f32[768]{0:T(1024)S(1)}, u32[]{:S(2)}) copy-start(f32[768]{0:T(1024)S(1)} %get-tuple-element.100) | copy-start | bytes 9220
  126.9 43.2 %copy-start.16 = (f32[23,4,512]{2,0,1:T(8,128)}, f32[23,4,512]{2,0,1:T(8,128)S(1)}, u32[]{:S(2)}) copy-start(f32[23,4,512]{2,0,1:T(8,128)S(1)} %slice_bitcast_fusion.3) | copy-start | bytes 565252
  127.6 27.5 %copy-start.43 = (f32[1,4,512]{2,0,1:T(1,128)}, f32[1,4,512]{2,0,1:T(1,128)S(1)}, u32[]{:S(2)}) copy-start(f32[1,4,512]{2,0,1:T(1,128)S(1)} %get-tuple-element.81) | copy-start | bytes 24580
  127.6 27.5 %copy-start.44 = (f32[1,4,512]{2,0,1:T(1,128)}, f32[1,4,512]{2,0,1:T(1,128)S(1)}, u32[]{:S(2)}) copy-start(f32[1,4,512]{2,0,1:T(1,128)S(1)} %get-tuple-element.82) | copy-start | bytes 24580
  127.6 27.5 %copy-start.45 = (f32[1,4,512]{2,0,1:T(1,128)}, f32[1,4,512]{2,0,1:T(1,128)S(1)}, u32[]{:S(2)}) copy-start(f32[1,4,512]{2,0,1:T(1,128)S(1)} %get-tuple-element.83) | copy-start | bytes 24580
  155.1 10.2 %copy-start = (bf16[768,2048]{1,0:T(8,128)(2,1)}, bf16[768,2048]{1,0:T(8,128)(2,1)S(1)}, u32[]{:S(2)}) copy-start(bf16[768,2048]{1,0:T(8,128)(2,1)S(1)} %get-tuple-element.64) | copy-start | bytes 9437188
  157.1 12.6 %copy-start.12 = (f32[768,96]{0,1:T(8,128)}, f32[768,96]{0,1:T(8,128)S(1)}, u32[]{:S(2)}) copy-start(f32[768,96]{0,1:T(8,128)S(1)} %fusion.97) | copy-start | bytes 884740
  303.5 10.4 %copy-start.1 = (bf16[768,2048]{1,0:T(8,128)(2,1)S(1)}, bf16[768,2048]{1,0:T(8,128)(2,1)}, u32[]{:S(2)}) copy-start(bf16[768,2048]{1,0:T(8,128)(2,1)} %copy-done) | copy-start | bytes 9437188
  325.9 35.5 %copy-start.53 = (f32[768]{0:T(1024)S(1)}, f32[768]{0:T(1024)}, u32[]{:S(2)}) copy-start(f32[768]{0:T(1024)} %copy-done.52) | copy-start | bytes 9220
  377.8 14.0 %copy-start.36 = (f32[768]{0:T(1024)S(1)}, f32[768]{0:T(1024)}, u32[]{:S(2)}) copy-start(f32[768]{0:T(1024)} %copy-done.35) | copy-start | bytes 9220
  377.8 14.0 %copy-start.15 = (bf16[768,1024]{1,0:T(8,128)(2,1)S(1)}, bf16[768,1024]{1,0:T(8,128)(2,1)}, u32[]{:S(2)}) copy-start(bf16[768,1024]{1,0:T(8,128)(2,1)} %param.23) | copy-start | bytes 4718596
  530.3 23.3 %copy-start.58 = (f32[256]{0:T(256)S(1)}, f32[256]{0:T(256)}, u32[]{:S(2)}) copy-start(f32[256]{0:T(256)} %param.24) | copy-start | bytes 3076
  530.3 23.3 %copy-start.60 = (f32[256]{0:T(256)S(1)}, f32[256]{0:T(256)}, u32[]{:S(2)}) copy-start(f32[256]{0:T(256)} %param.36) | copy-start | bytes 3076
  530.3 23.3 %copy-start.61 = (f32[256]{0:T(256)S(1)}, f32[256]{0:T(256)}, u32[]{:S(2)}) copy-start(f32[256]{0:T(256)} %param.30) | copy-start | bytes 3076
  530.3 32.8 %copy-start.59 = (f32[1,256]{1,0:T(1,128)}, f32[1,256]{1,0:T(1,128)S(1)}, u32[]{:S(2)}) copy-start(f32[1,256]{1,0:T(1,128)S(1)} %slice.190) | copy-start | bytes 3076
  536.5 26.6 %copy-start.18 = (f32[96,512]{1,0:T(8,128)}, f32[96,512]{1,0:T(8,128)S(1)}, u32[]{:S(2)}) copy-start(f32[96,512]{1,0:T(8,128)S(1)} %get-tuple-element.59) | copy-start | bytes 589828
  537.8 26.2 %copy-start.24 = (f32[64,512]{1,0:T(8,128)}, f32[64,512]{1,0:T(8,128)S(1)}, u32[]{:S(2)}) copy-start(f32[64,512]{1,0:T(8,128)S(1)} %get-tuple-element.57) | copy-start | bytes 393220
  539.1 25.7 %copy-start.28 = (f32[23,512]{1,0:T(8,128)}, f32[23,512]{1,0:T(8,128)S(1)}, u32[]{:S(2)}) copy-start(f32[23,512]{1,0:T(8,128)S(1)} %get-tuple-element.55) | copy-start | bytes 141316
  554.2 9.8 %copy-start.23 = (f32[64,512]{1,0:T(8,128)S(1)}, f32[64,512]{1,0:T(8,128)}, u32[]{:S(2)}) copy-start(f32[64,512]{1,0:T(8,128)} %param.27) | copy-start | bytes 393220
  554.2 9.8 %copy-start.31 = (f32[64,512]{1,0:T(8,128)S(1)}, f32[64,512]{1,0:T(8,128)}, u32[]{:S(2)}) copy-start(f32[64,512]{1,0:T(8,128)} %param.39) | copy-start | bytes 393220
  554.2 10.6 %copy-start.30 = (f32[23,512]{1,0:T(8,128)S(1)}, f32[23,512]{1,0:T(8,128)}, u32[]{:S(2)}) copy-start(f32[23,512]{1,0:T(8,128)} %param.28) | copy-start | bytes 141316
  554.2 10.6 %copy-start.33 = (f32[23,512]{1,0:T(8,128)S(1)}, f32[23,512]{1,0:T(8,128)}, u32[]{:S(2)}) copy-start(f32[23,512]{1,0:T(8,128)} %param.40) | copy-start | bytes 141316
  554.2 10.6 %copy-start.34 = (f32[23,512]{1,0:T(8,128)S(1)}, f32[23,512]{1,0:T(8,128)}, u32[]{:S(2)}) copy-start(f32[23,512]{1,0:T(8,128)} %param.34) | copy-start | bytes 141316
  554.2 11.3 %copy-start.9 = (f32[512,1024]{1,0:T(8,128)S(1)}, f32[512,1024]{1,0:T(8,128)}, u32[]{:S(2)}) copy-start(f32[512,1024]{1,0:T(8,128)} %param.29) | copy-start | bytes 6291460
  554.2 11.2 %copy-start.10 = (f32[512,1024]{1,0:T(8,128)S(1)}, f32[512,1024]{1,0:T(8,128)}, u32[]{:S(2)}) copy-start(f32[512,1024]{1,0:T(8,128)} %param.41) | copy-start | bytes 6291460
  554.2 11.2 %copy-start.11 = (f32[512,1024]{1,0:T(8,128)S(1)}, f32[512,1024]{1,0:T(8,128)}, u32[]{:S(2)}) copy-start(f32[512,1024]{1,0:T(8,128)} %param.35) | copy-start | bytes 6291460
  (36 other events, 198.6 us)

commit v3 on v2

--- a/solution.py
+++ b/solution.py
@@ -17,6 +17,9 @@
 HALVES = COLS // 8
 BLOCK = 64
 GROUP = 8
+BACK = 4
+WIDE = 512
+TAIL = 4
 
 norm_eps = 1e-05
 beta_one = 0.9
@@ -55,167 +58,200 @@
     return total
 
 
-def spread(ref, value, first):
+def spread(ref, value, g):
     for col in range(COLS):
-        ref[pl.ds(first + 8 * col, 8), :] = value[:, LANES * col : LANES * (col + 1)]
-
-
-def token_rows(ref, first, half, token):
-    return ref[pl.ds(first + 64 * half + token, 8, stride=8), :]
-
-
-def splat(ref, row):
-    return ref[pl.ds(row, 8, stride=0), :]
-
-
-def prepare(rows, sel, dt_ref, mixed_ref, dts, us, bb):
-    first = rows * 16
-    step = dt_ref[pl.ds(rows, 8), :]
-    chosen = sel[pl.ds(rows, 8), :]
+        ref[pl.ds(g * 8 * COLS + col, 8, stride=COLS), :] = value[:, LANES * col : LANES * (col + 1)]
+
+
+def unspread(out, ref, g):
+    rows = pl.multiple_of(g * 8, 8)
+    for col in range(COLS):
+        out[pl.ds(rows, 8), LANES * col : LANES * (col + 1)] = ref[pl.ds(g * 8 * COLS + col, 8, stride=COLS), :]
+
+
+def token_rows(g, token):
+    return pl.ds(pl.multiple_of(g * 8 * COLS, 8 * COLS) + token * COLS, COLS)
+
+
+def prepare(g, sel, step, mixed, dts, us, bb):
+    chosen = sel[pl.ds(pl.multiple_of(g * 8, 8), 8), :]
     fresh = chosen[:, 2 * N : 2 * N + 1] > 0.5
-    spread(dts, jnp.where(fresh, RESET, step), first)
-    spread(us, step * mixed_ref[pl.ds(rows, 8), :], first)
+    spread(dts, jnp.where(fresh, RESET, step), g)
+    spread(us, step * mixed, g)
     for k in range(2 * N):
-        bb[pl.ds(rows * 2 * N + 8 * k, 8), :] = jnp.broadcast_to(chosen[:, k : k + 1], (8, LANES))
-
-
-def forward_kernel(dt_ref, mixed_ref, sel, rates, y_ref, hs_ref, state, dts, us, bb, ys):
+        bb[g, k] = jnp.broadcast_to(chosen[:, k : k + 1], (8, LANES))
+
+
+def splat(bb, g, first, count, token):
+    return jnp.stack([bb[g, first + n, pl.ds(token, COLS, stride=0), :] for n in range(count)])
+
+
+def softplus(v):
+    small = jnp.exp(-jnp.abs(v))
+    series = small * (1.0 - small * (1 / 2 - small * (1 / 3 - small * (1 / 4 - small * (1 / 5)))))
+    return jnp.maximum(v, 0.0) + jnp.where(small < 1 / 32, series, jnp.log(1.0 + small))
+
+
+def forward_kernel(v_ref, mixed_ref, sel, rates, y_ref, dt_ref, hs_ref, state, dts, us, bb, ys):
     @pl.when(pl.program_id(0) == 0)
     def _():
         state[...] = jnp.zeros_like(state)
 
-    def stage(g, _):
-        prepare(pl.multiple_of(g * 8, 8), sel, dt_ref, mixed_ref, dts, us, bb)
-        return 0
-
-    lax.fori_loop(0, BLOCK // 8, stage, 0)
+    @pl.loop(0, BLOCK // 8)
+    def _(g):
+        rows = pl.ds(pl.multiple_of(g * 8, 8), 8)
+        dt_ref[rows, :] = softplus(v_ref[rows, :])
+
+    @pl.loop(0, BLOCK // 16)
+    def _(pair):
+        mixed = mixed_ref[pl.ds(pl.multiple_of(pair * 16, 16), 16), :].astype(jnp.float32)
+        for side in range(2):
+            g = pair * 2 + side
+            step = dt_ref[pl.ds(pl.multiple_of(g * 8, 8), 8), :]
+            prepare(g, sel, step, mixed[8 * side : 8 * side + 8], dts, us, bb)
+
     for low in range(0, N, GROUP):
-        names = [(n, half) for n in range(low, low + GROUP) for half in range(HALVES)]
-
-        def steps(g, carried):
-            rows = pl.multiple_of(g * 8, 8)
-            first = rows * 16
-            kept = dict(zip(names, carried))
+        part = pl.ds(low, GROUP)
+
+        def steps(g, kept):
             for token in range(8):
-                dt = [token_rows(dts, first, half, token) for half in range(HALVES)]
-                u = [token_rows(us, first, half, token) for half in range(HALVES)]
-                total = [None] * HALVES
-                for n in range(low, low + GROUP):
-                    b = splat(bb, rows * 2 * N + 8 * n + token)
-                    c = splat(bb, rows * 2 * N + 8 * (N + n) + token)
-                    for half in range(HALVES):
-                        h = jnp.exp2(dt[half] * rates[2 * n + half]) * kept[n, half] + b * u[half]
-                        kept[n, half] = h
-                        hs_ref[rows + token, 2 * n + half] = h
-                        part = c * h
-                        total[half] = part if total[half] is None else total[half] + part
-                for half in range(HALVES):
-                    at = pl.ds(first + 64 * half + token, 8, stride=8)
-                    ys[at, :] = total[half] if low == 0 else ys[at, :] + total[half]
-            return tuple(kept[name] for name in names)
-
-        start = tuple(state[2 * n + half] for n, half in names)
-        for name, value in zip(names, lax.fori_loop(0, BLOCK // 8, steps, start)):
-            state[2 * name[0] + name[1]] = value
-
-    def finish(g, _):
-        rows = pl.multiple_of(g * 8, 8)
-        for col in range(COLS):
-            y_ref[pl.ds(rows, 8), LANES * col : LANES * (col + 1)] = ys[pl.ds(rows * 16 + 8 * col, 8), :]
-        return 0
-
-    lax.fori_loop(0, BLOCK // 8, finish, 0)
+                at = token_rows(g, token)
+                decay = jnp.exp2(dts[at, :][None] * rates[part])
+                kept = decay * kept + splat(bb, g, low, GROUP, token) * us[at, :][None]
+                hs_ref[g * 8 + token, part] = kept
+                total = jnp.sum(splat(bb, g, N + low, GROUP, token) * kept, axis=0)
+                ys[at, :] = total if low == 0 else ys[at, :] + total
+            return kept
+
+        state[part] = lax.fori_loop(0, BLOCK // 8, steps, state[part])
+
+    @pl.loop(0, BLOCK // 8)
+    def _(g):
+        unspread(y_ref, ys, g)
+
+
+def fold(value):
+    return jnp.sum(value.reshape(value.shape[0] // 8, 8, value.shape[1]), axis=0)
 
 
 def backward_kernel(
-    dt_ref, mixed_ref, gs_ref, sel, rates, hs_ref, last_ref,
-    sum_in, sum_decay, parts, grad_rates,
-    carry, dts, us, gss, bb, s1, s2, prods,
+    v_ref, dt_ref, mixed_ref, gs_ref, sel, rates, vectors,
+    step_weight, select_weight, hs_ref, last_ref, conv_ref, slope_ref, flags,
+    grad_conv_in, pre_low, chosen, grad_rows, grad_rates,
+    carry, dts, us, gss, bb, s1, s2, prods, parts, nat1, nat2, grad_mixed, taps,
 ):
+    turn = lax.rem(pl.program_id(0), TAIL)
+    tall = BLOCK * TAIL
+    own = pl.ds(pl.multiple_of((TAIL - 1 - turn) * BLOCK, BLOCK), BLOCK)
+
     @pl.when(pl.program_id(0) == 0)
     def _():
-        carry[...] = jnp.zeros_like(carry)
-        grad_rates[...] = jnp.zeros_like(grad_rates)
-
-    def stage(g, _):
-        rows = pl.multiple_of(g * 8, 8)
-        prepare(rows, sel, dt_ref, mixed_ref, dts, us, bb)
-        spread(gss, gs_ref[pl.ds(rows, 8), :], rows * 16)
-        return 0
-
-    lax.fori_loop(0, BLOCK // 8, stage, 0)
-    for low in range(0, N, GROUP):
-        names = [(n, half) for n in range(low, low + GROUP) for half in range(HALVES)]
+        for ref in (carry, grad_rates, grad_rows, parts):
+            ref[...] = jnp.zeros_like(ref)
+        taps[:, tall:, :] = jnp.zeros_like(taps[:, tall:, :])
+
+    @pl.loop(0, BLOCK // 16)
+    def _(pair):
+        mixed = mixed_ref[pl.ds(pl.multiple_of(pair * 16, 16), 16), :].astype(jnp.float32)
+        for side in range(2):
+            g = pair * 2 + side
+            rows = pl.ds(pl.multiple_of(g * 8, 8), 8)
+            prepare(g, sel, dt_ref[rows, :], mixed[8 * side : 8 * side + 8], dts, us, bb)
+            spread(gss, gs_ref[rows, :], g)
+
+    spot = lax.broadcasted_iota(jnp.int32, (8, LANES), 1)
+    for low in range(0, N, BACK):
+        part = pl.ds(low, BACK)
 
         def steps(step, carried):
             g = BLOCK // 8 - 1 - step
-            rows = pl.multiple_of(g * 8, 8)
-            first = rows * 16
-            kept = dict(zip(names, carried[: len(names)]))
-            total = dict(zip(names, carried[len(names) :]))
+            kept, total, sums = carried
             for token in reversed(range(8)):
-                dt = [token_rows(dts, first, half, token) for half in range(HALVES)]
-                u = [token_rows(us, first, half, token) for half in range(HALVES)]
-                gs = [token_rows(gss, first, half, token) for half in range(HALVES)]
-                in_sum = [None] * HALVES
-                decay_sum = [None] * HALVES
-                for n in range(low, low + GROUP):
-                    b = splat(bb, rows * 2 * N + 8 * n + token)
-                    c = splat(bb, rows * 2 * N + 8 * (N + n) + token)
-                    for_b = for_c = None
-                    for half in range(HALVES):
-                        at = 2 * n + half
-                        if token > 0:
-                            before = hs_ref[rows + token - 1, at]
-                        else:
-                            before = jnp.where(g == 0, last_ref[0, at], hs_ref[jnp.maximum(rows - 1, 0), at])
-                        rate = rates[at]
-                        adjoint = c * gs[half] + kept[n, half]
-                        part_c = gs[half] * hs_ref[rows + token, at]
-                        part_b = adjoint * u[half]
-                        for_c = part_c if for_c is None else for_c + part_c
-                        for_b = part_b if for_b is None else for_b + part_b
-                        part = b * adjoint
-                        in_sum[half] = part if in_sum[half] is None else in_sum[half] + part
-                        later = jnp.exp2(dt[half] * rate) * adjoint
-                        kept[n, half] = later
-                        slope = later * before
-                        part = rate * slope
-                        decay_sum[half] = part if decay_sum[half] is None else decay_sum[half] + part
-                        total[n, half] = total[n, half] + dt[half] * slope
-                    prods[pl.ds(8 * (n - low), 8), :] = for_b
-                    prods[pl.ds(8 * (GROUP + n - low), 8), :] = for_c
-                for half in range(HALVES):
-                    at = pl.ds(first + 64 * half + token, 8, stride=8)
-                    s1[at, :] = in_sum[half] if low == 0 else s1[at, :] + in_sum[half]
-                    s2[at, :] = decay_sum[half] if low == 0 else s2[at, :] + decay_sum[half]
-                for kind in range(2):
-                    rows_of = [prods[pl.ds(8 * GROUP * kind + s, GROUP, stride=8), :] for s in range(8)]
+                at = token_rows(g, token)
+                dt, u, gs = dts[at, :][None], us[at, :][None], gss[at, :][None]
+                if token > 0:
+                    before = hs_ref[g * 8 + token - 1, part]
+                else:
+                    before = jnp.where(g == 0, last_ref[0, part], hs_ref[jnp.maximum(g * 8 - 1, 0), part])
+                rate = rates[part]
+                adjoint = splat(bb, g, N + low, BACK, token) * gs + kept
+                for_c = gs * hs_ref[g * 8 + token, part]
+                for_b = adjoint * u
+                in_sum = jnp.sum(splat(bb, g, low, BACK, token) * adjoint, axis=0)
+                kept = jnp.exp2(dt * rate) * adjoint
+                slope = kept * before
+                decay_sum = jnp.sum(rate * slope, axis=0)
+                total = total + dt * slope
+                for kind, value in enumerate((for_b, for_c)):
+                    prods[token % 2, pl.ds(8 * BACK * kind, 8 * BACK), :] = (value[:, :8] + value[:, 8:]).reshape(8 * BACK, LANES)
+                here = spot == g * 8 + token
+                new = []
+                for first in range(0, 2 * BACK, 8):
+                    rows_of = [prods[token % 2, pl.ds(8 * first + s, 8, stride=8), :] for s in range(8)]
                     while len(rows_of) > 1:
                         rows_of = [a + b for a, b in zip(rows_of[::2], rows_of[1::2])]
-                    parts[rows + token, pl.ds(N * kind + low, GROUP), :] = rows_of[0]
-            return tuple(kept[name] for name in names) + tuple(total[name] for name in names)
-
-        start = tuple(carry[2 * n + half] for n, half in names)
-        start = start + tuple(grad_rates[2 * n + half] for n, half in names)
-        ended = lax.fori_loop(0, BLOCK // 8, steps, start)
-        for name, value, sums in zip(names, ended[: len(names)], ended[len(names) :]):
-            carry[2 * name[0] + name[1]] = value
-            grad_rates[2 * name[0] + name[1]] = sums
-
-    def finish(g, _):
-        rows = pl.multiple_of(g * 8, 8)
-        for col in range(COLS):
-            lanes = slice(LANES * col, LANES * (col + 1))
-            sum_in[pl.ds(rows, 8), lanes] = s1[pl.ds(rows * 16 + 8 * col, 8), :]
-            sum_decay[pl.ds(rows, 8), lanes] = s2[pl.ds(rows * 16 + 8 * col, 8), :]
-        return 0
-
-    lax.fori_loop(0, BLOCK // 8, finish, 0)
-
-
-def scan_forward(dt, mixed, sel, rates):
-    count = dt.shape[0]
+                    new.append(jnp.where(here, jnp.sum(rows_of[0], axis=1, keepdims=True), sums[first // 8]))
+                sums = tuple(new)
+                s1[at, :] = in_sum if low == 0 else s1[at, :] + in_sum
+                s2[at, :] = decay_sum if low == 0 else s2[at, :] + decay_sum
+            return kept, total, sums
+
+        nothing = tuple(jnp.zeros((8, LANES), jnp.float32) for _ in range(2 * BACK // 8))
+        carry[part], grad_rates[part], sums = lax.fori_loop(
+            0, BLOCK // 8, steps, (carry[part], grad_rates[part], nothing)
+        )
+        sums = jnp.concatenate(sums, axis=0)
+        parts[pl.ds(low, BACK), :] = sums[:BACK]
+        parts[pl.ds(N + low, BACK), :] = sums[BACK:]
+
+    @pl.loop(0, BLOCK // 8)
+    def _(g):
+        unspread(nat1, s1, g)
+        unspread(nat2, s2, g)
+
+    @pl.loop(0, DI // WIDE)
+    def _(c):
+        lanes = pl.ds(pl.multiple_of(c * WIDE, WIDE), WIDE)
+        mixed = mixed_ref[:, lanes].astype(jnp.float32)
+        step, gs, in_sum = dt_ref[:, lanes], gs_ref[:, lanes], nat1[:, lanes]
+        pre = (mixed * in_sum + math.log(2.0) * nat2[:, lanes]) * jnp.exp(v_ref[:, lanes] - step)
+        pre_low[own, lanes] = pre.astype(jnp.bfloat16)
+        grad_mixed[own, lanes] = step * in_sum + vectors[CONV + 2 : CONV + 3, lanes] * gs
+        grad_rows[CONV + 1, :, lanes] += fold(pre)
+        grad_rows[CONV + 2, :, lanes] += fold(gs * mixed)
+
+    chosen[own, R:] = parts[...].T[:BLOCK, : 2 * N].astype(jnp.bfloat16)
+
+    @pl.when(turn == TAIL - 1)
+    def _():
+        chosen[:, :R] = dot(pre_low[...], step_weight[...], 1, 1).astype(jnp.bfloat16)
+
+        @pl.loop(0, DI // WIDE)
+        def _(c):
+            lanes = pl.ds(pl.multiple_of(c * WIDE, WIDE), WIDE)
+            total = grad_mixed[:, lanes] + dot(chosen[...], select_weight[:, lanes], 1, 0)
+            grad_conv = total * slope_ref[:, lanes]
+            value = conv_ref[:, lanes]
+            grad_rows[CONV, :, lanes] += fold(grad_conv)
+            result = vectors[CONV - 1 : CONV, lanes] * grad_conv
+            grad_rows[CONV - 1, :, lanes] += fold(grad_conv * value)
+            for j in range(1, CONV):
+                taps[j - 1, :tall, lanes] = grad_conv * flags[:, 2 * N + j : 2 * N + j + 1]
+                later = taps[j - 1, :, lanes][j : j + tall]
+                grad_rows[CONV - 1 - j, :, lanes] += fold(later * value)
+                result = result + vectors[CONV - 1 - j : CONV - j, lanes] * later
+                taps[j - 1, tall:, lanes] = taps[j - 1, :8, lanes]
+            grad_conv_in[:, lanes] = result.astype(jnp.bfloat16)
+
+
+def dot(left, right, left_dim, right_dim):
+    return lax.dot_general(
+        left, right, (((left_dim,), (right_dim,)), ((), ())), preferred_element_type=jnp.float32
+    )
+
+
+def scan_forward(v, mixed, sel, rates):
+    count = v.shape[0]
     rows = pl.BlockSpec((BLOCK, DI), lambda i: (i, 0))
     return pl.pallas_call(
         forward_kernel,
@@ -224,18 +260,19 @@
             rows,
             rows,
             pl.BlockSpec((BLOCK, LANES), lambda i: (i, 0)),
-            pl.BlockSpec((2 * N, 8, LANES), lambda i: (0, 0, 0)),
+            pl.BlockSpec((N, COLS, LANES), lambda i: (0, 0, 0)),
         ],
-        out_specs=[rows, pl.BlockSpec((BLOCK, 2 * N, 8, LANES), lambda i: (i, 0, 0, 0))],
+        out_specs=[rows, rows, pl.BlockSpec((BLOCK, N, COLS, LANES), lambda i: (i, 0, 0, 0))],
         out_shape=[
             jax.ShapeDtypeStruct((count, DI), jnp.float32),
-            jax.ShapeDtypeStruct((count, 2 * N, 8, LANES), jnp.float32),
+            jax.ShapeDtypeStruct((count, DI), jnp.float32),
+            jax.ShapeDtypeStruct((count, N, COLS, LANES), jnp.float32),
         ],
         scratch_shapes=[
-            pltpu.VMEM((2 * N, 8, LANES), jnp.float32),
+            pltpu.VMEM((N, COLS, LANES), jnp.float32),
             pltpu.VMEM((BLOCK * COLS, LANES), jnp.float32),
             pltpu.VMEM((BLOCK * COLS, LANES), jnp.float32),
-            pltpu.VMEM((BLOCK * 2 * N, LANES), jnp.float32),
+            pltpu.VMEM((BLOCK // 8, 2 * N, 8, LANES), jnp.float32),
             pltpu.VMEM((BLOCK * COLS, LANES), jnp.float32),
         ],
         compiler_params=pltpu.CompilerParams(vmem_limit_bytes=48 << 20),
@@ -243,13 +280,21 @@
             flops=6 * count * N * DI, bytes_accessed=4 * count * N * DI, transcendentals=count * N * DI
         ),
         name="scan_forward",
-    )(dt, mixed, sel, rates)
-
-
-def scan_backward(dt, mixed, gs, sel, rates, states):
+    )(v, mixed, sel, rates)
+
+
+def scan_backward(v, dt, mixed, gs, conv_input, slope, sel, rates, vectors, step_weight, select_weight, states):
     count = dt.shape[0]
     blocks = count // BLOCK
     rows = pl.BlockSpec((BLOCK, DI), lambda i: (blocks - 1 - i, 0))
+
+    def tall(width):
+        return pl.BlockSpec((BLOCK * TAIL, width), lambda i: (blocks // TAIL - 1 - i // TAIL, 0))
+
+    def whole(*shape):
+        return pl.BlockSpec(shape, lambda i: (0,) * len(shape))
+
+    state = (N, COLS, LANES)
     return pl.pallas_call(
         backward_kernel,
         grid=(blocks,),
@@ -257,37 +302,44 @@
             rows,
             rows,
             rows,
+            rows,
             pl.BlockSpec((BLOCK, LANES), lambda i: (blocks - 1 - i, 0)),
-            pl.BlockSpec((2 * N, 8, LANES), lambda i: (0, 0, 0)),
-            pl.BlockSpec((BLOCK, 2 * N, 8, LANES), lambda i: (blocks - 1 - i, 0, 0, 0)),
-            pl.BlockSpec(
-                (1, 2 * N, 8, LANES),
-                lambda i: (jnp.maximum((blocks - 1 - i) * BLOCK - 1, 0), 0, 0, 0),
-            ),
+            whole(*state),
+            whole(8, DI),
+            whole(R, DI),
+            whole(R + 2 * N, DI),
+            pl.BlockSpec((BLOCK,) + state, lambda i: (blocks - 1 - i, 0, 0, 0)),
+            pl.BlockSpec((1,) + state, lambda i: (jnp.maximum((blocks - 1 - i) * BLOCK - 1, 0), 0, 0, 0)),
+            tall(DI),
+            tall(DI),
+            tall(LANES),
         ],
-        out_specs=[
-            rows,
-            rows,
-            pl.BlockSpec((BLOCK, 2 * N, LANES), lambda i: (blocks - 1 - i, 0, 0)),
-            pl.BlockSpec((2 * N, 8, LANES), lambda i: (0, 0, 0)),
+        out_specs=[tall(DI), tall(DI), tall(R + 2 * N), whole(8, 8, DI), whole(*state)],
+        out_shape=[
+            jax.ShapeDtypeStruct((count, DI), jnp.bfloat16),
+            jax.ShapeDtypeStruct((count, DI), jnp.bfloat16),
+            jax.ShapeDtypeStruct((count, R + 2 * N), jnp.bfloat16),
+            jax.ShapeDtypeStruct((8, 8, DI), jnp.float32),
+            jax.ShapeDtypeStruct(state, jnp.float32),
         ],
-        out_shape=[
-            jax.ShapeDtypeStruct((count, DI), jnp.float32),
-            jax.ShapeDtypeStruct((count, DI), jnp.float32),
-            jax.ShapeDtypeStruct((count, 2 * N, LANES), jnp.float32),
-            jax.ShapeDtypeStruct((2 * N, 8, LANES), jnp.float32),
-        ],
-        scratch_shapes=[pltpu.VMEM((2 * N, 8, LANES), jnp.float32)]
+        scratch_shapes=[pltpu.VMEM(state, jnp.float32)]
         + [pltpu.VMEM((BLOCK * COLS, LANES), jnp.float32)] * 3
-        + [pltpu.VMEM((BLOCK * 2 * N, LANES), jnp.float32)]
+        + [pltpu.VMEM((BLOCK // 8, 2 * N, 8, LANES), jnp.float32)]
         + [pltpu.VMEM((BLOCK * COLS, LANES), jnp.float32)] * 2
-        + [pltpu.VMEM((16 * GROUP, LANES), jnp.float32)],
-        compiler_params=pltpu.CompilerParams(vmem_limit_bytes=48 << 20),
+        + [pltpu.VMEM((2, 16 * BACK, LANES), jnp.float32)]
+        + [pltpu.VMEM((LANES, LANES), jnp.float32)]
+        + [pltpu.VMEM((BLOCK, DI), jnp.float32)] * 2
+        + [pltpu.VMEM((BLOCK * TAIL, DI), jnp.float32)]
+        + [pltpu.VMEM((CONV - 1, BLOCK * TAIL + 8, DI), jnp.float32)],
+        compiler_params=pltpu.CompilerParams(vmem_limit_bytes=60 << 20),
         cost_estimate=pl.CostEstimate(
-            flops=15 * count * N * DI, bytes_accessed=4 * count * N * DI, transcendentals=count * N * DI
+            flops=20 * count * N * DI, bytes_accessed=4 * count * N * DI, transcendentals=count * N * DI
         ),
         name="scan_backward",
-    )(dt, mixed, gs, sel, rates, states, states)
+    )(
+        v, dt, mixed, gs, sel, rates, vectors, step_weight, select_weight,
+        states, states, conv_input, slope, sel,
+    )
 
 
 def mesh_copy(src, dst, sems, at, device):
@@ -604,7 +656,7 @@
     full_conv, full_small, full_vectors, full_gate, full_output = gather_pieces(
         plan, [low_conv, low_small, own_piece(vectors, dp), low_gate, low_output], "gather_weights", 0
     )
-    full_input = jnp.concatenate([full_conv.reshape(-1, DI), full_gate.reshape(-1, DI)], axis=1)
+    full_conv, full_gate = full_conv.reshape(-1, DI), full_gate.reshape(-1, DI)
     full_output = full_output.reshape(DI, -1)
     small_rows = R + 2 * N + R
     full_small = from_pieces(full_small, small_rows, width, dp).transpose(1, 0, 2).reshape(small_rows, DI)
@@ -615,30 +667,25 @@
     inputs = tokens.astype(jnp.float32)
     normed_value, norm_pull = jax.vjp(rms_scale, inputs, gain)
     normed = normed_value.astype(jnp.bfloat16)
-    projected = jnp.dot(normed, full_input, preferred_element_type=jnp.float32)
-    conv_input = projected[:, :DI]
-    gate_half = projected[:, DI:]
-
-    def conv_piece(values, kernel, shift):
-        return jax.nn.silu(causal_conv(values, kernel, shift, offset))
-
-    conv_value, conv_pull = jax.vjp(
-        conv_piece, conv_input, channel[N : N + CONV], channel[N + CONV]
-    )
-    mixed = conv_value.astype(jnp.bfloat16)
+    conv_input = jnp.dot(normed, full_conv, preferred_element_type=jnp.float32)
+    gate_half = jnp.dot(normed, full_gate, preferred_element_type=jnp.float32)
+    conv_out = causal_conv(conv_input, channel[N : N + CONV], channel[N + CONV], offset)
+    sigmoid = jax.nn.sigmoid(conv_out)
+    mixed, conv_slope = lax.optimization_barrier(
+        ((conv_out * sigmoid).astype(jnp.bfloat16), sigmoid * (1.0 + conv_out * (1.0 - sigmoid)))
+    )
     mixed_values = mixed.astype(jnp.float32)
     selection = contract(mixed, full_select, 1, 1)
     step_low = selection[:, :R].astype(jnp.bfloat16)
-    step_pre = jnp.dot(step_low, full_step, preferred_element_type=jnp.float32)
-    step_in = step_pre + channel[N + CONV + 1][None, :]
-    step_size = jax.nn.softplus(step_in)
+    step_in = jnp.dot(step_low, full_step, preferred_element_type=jnp.float32) + channel[N + CONV + 1][None, :]
     rates = -jnp.exp(channel[:N])
-    rates_low = (rates * math.log2(math.e)).reshape(2 * N, 8, LANES)
+    rates_low = (rates * math.log2(math.e)).reshape(N, COLS, LANES)
+    kept = [restart] + [(offset >= j).astype(jnp.float32) for j in range(1, CONV)]
     chosen = jnp.concatenate(
-        [selection[:, R:], restart[:, None], jnp.zeros((row_count, LANES - 2 * N - 1), jnp.float32)], axis=1
+        [selection[:, R:], jnp.stack(kept, axis=1), jnp.zeros((row_count, LANES - 2 * N - CONV), jnp.float32)], axis=1
     )
     skip = channel[N + CONV + 2][None, :]
-    state_out, states = scan_forward(step_size, mixed_values, chosen, rates_low)
+    state_out, step_size, states = scan_forward(step_in, mixed, chosen, rates_low)
     scanned = state_out + skip * mixed_values
     gate_value, gate_pull = jax.vjp(jax.nn.silu, gate_half)
     gated = (scanned * gate_value).astype(jnp.bfloat16)
@@ -650,38 +697,32 @@
     grad_gated = contract(grad_branch, full_output, 1, 1)
     grad_scanned = grad_gated * gate_value
     (grad_gate,) = gate_pull(grad_gated * scanned)
-    sum_in, sum_decay, parts, sums = scan_backward(
-        step_size, mixed_values, grad_scanned, chosen, rates_low, states
-    )
-    grad_both = jnp.sum(parts, axis=2)
-    grad_mixed = step_size * sum_in + skip * grad_scanned
-    grad_pre = (mixed_values * sum_in + math.log(2.0) * sum_decay) * jax.nn.sigmoid(step_in)
-    grad_pre_low = grad_pre.astype(jnp.bfloat16)
+    grad_conv_input, grad_pre_low, grad_selection, grad_rows, sums = scan_backward(
+        step_in,
+        step_size,
+        mixed,
+        grad_scanned,
+        conv_input,
+        conv_slope,
+        chosen,
+        rates_low,
+        jnp.pad(channel[N:], ((0, 1), (0, 0))),
+        full_step,
+        full_select,
+        states,
+    )
+    grad_gate = grad_gate.astype(jnp.bfloat16)
     grad_step = contract(step_low, grad_pre_low, 0, 0)
-    grad_step_low = contract(grad_pre_low, full_step, 1, 1)
-    grad_selection = jnp.concatenate([grad_step_low, grad_both], axis=1).astype(jnp.bfloat16)
     grad_select = contract(grad_selection, mixed, 0, 0)
-    grad_mixed = grad_mixed + jnp.dot(
-        grad_selection, full_select, preferred_element_type=jnp.float32
-    )
-    grad_conv_input, grad_kernel, grad_shift = conv_pull(grad_mixed)
-    grad_projected = jnp.concatenate([grad_conv_input, grad_gate], axis=1).astype(jnp.bfloat16)
     grad_conv_weight, grad_gate_weight = (
         contract(normed, half, 0, 0).astype(jnp.bfloat16)
-        for half in (grad_projected[:, :DI], grad_projected[:, DI:])
-    )
-    grad_normed = contract(grad_projected, full_input, 1, 1)
+        for half in (grad_conv_input, grad_gate)
+    )
+    grad_normed = contract(grad_conv_input, full_conv, 1, 1) + contract(grad_gate, full_gate, 1, 1)
     grad_inputs, grad_gain = norm_pull(grad_normed)
     input_grad = (upstream + grad_inputs).astype(jnp.bfloat16)
     grad_channel = jnp.concatenate(
-        [
-            rates * sums.reshape(N, DI),
-            grad_kernel,
-            grad_shift[None, :],
-            jnp.sum(grad_pre, axis=0, keepdims=True),
-            jnp.sum(grad_scanned * mixed_values, axis=0, keepdims=True),
-        ],
-        axis=0,
+        [rates * sums.reshape(N, DI), jnp.sum(grad_rows[: CONV + 3], axis=1)], axis=0
     )
     small = jnp.concatenate([grad_select, grad_step, grad_channel], axis=0)
     small = small.reshape(-1, shards, width).transpose(1, 0, 2)

time: 578 us -> 536 us (0.927)
  matrix products: 124 us -> 66.2 us
  Pallas kernels: 341 us -> 370 us
  other arithmetic: 59.6 us -> 48.2 us
    dot_general x3, matrix products: 53 us -> 22 us  [the longest x1 11.6 us: local(): gate_half = jnp.dot(normed, full_gate, preferred_element_type=jnp.float32)]
    pallas_call x1, Pallas kernels: 88.5 us -> 115 us  [scan_backward(): pl.pallas_call(backward_kernel, grid=(blocks,), in_specs=[rows, rows, row...]
    dot_general x9, matrix products: 62.4 us -> 37.4 us  [contract(): lax.dot_general(left, right, (((left_dim,), (right_dim,)), ((), ())), pre...]
    reduce_sum x2 -> x1, other arithmetic: 17.3 us -> 0.12 us  [local(): jnp.sum(grad_rows[:CONV + 3], axis=1)]
    mul x1, other arithmetic: 0.03 us -> 6.99 us  [local(): sigmoid * (1.0 + conv_out * (1.0 - sigmoid))]
    slice x1 -> x0, other arithmetic: 6.77 us -> none  [local(): grad_projected[:, :DI]]
where the time goes in v3:
time: 536 us; the launch traced here: 526 us
  Pallas kernels  370 us (69%)
  matrix products  66.2 us (12%)
  other arithmetic  48.2 us (9%)
  local copies, waits for them, and re-layouts  19.7 us (4%)
  blocking collectives  11.3 us (2%)
  between operations  10.6 us (2%)
    pallas_call x1, Pallas kernels, scan_backward(): pl.pallas_call(backward_kernel, grid=(blocks,), in_specs=[rows, rows, row...  115 us
    pallas_call x1, Pallas kernels, reduce_pieces(): pl.pallas_call(functools.partial(reduce_kernel, plan, count), in_specs=[p...  112 us
    pallas_call x1, Pallas kernels, gather_pieces(): pl.pallas_call(functools.partial(gather_kernel, plan, count), in_specs=[p...  95.3 us
    pallas_call x1, Pallas kernels, scan_forward(): pl.pallas_call(forward_kernel, grid=(count // BLOCK,), in_specs=[rows, ro...  47.2 us
    dot_general x9, matrix products, contract(): lax.dot_general(left, right, (((left_dim,), (right_dim,)), ((), ())), pre...  37.4 us
    add x6, other arithmetic, adam_direction(): first_hat / (jnp.sqrt(second_hat) + adam_eps) + decay_rate * decay * weight  18.5 us
    dot_general x1, matrix products, local(): gate_half = jnp.dot(normed, full_gate, preferred_element_type=jnp.float32)  11.6 us
    psum x1, blocking collectives, local(): total_square = lax.psum(local_square, 'fsdp')  11.3 us

profile of v3, /device:TPU:0, one launch (start us, length us, event | category | flops | bytes accessed | tf_op | source)
XLA Modules:
  0.0 526.1 jit_solution(7840886273879429234)
XLA Ops:
  1.9 1.4 fusion.81
  6.6 1.8 fusion.25
  11.1 1.4 fusion.63.refs_1_
  12.5 1.6 dynamic-slice_convert_fusion.refs_4_
  14.1 1.7 compare_convert_fusion.2
  15.9 1.7 compare_convert_fusion
  17.6 2.5 fusion.80
  20.9 95.3 %gather_weights.1 = (bf16[4,4,2,32,2048]{4,3,2,1,0:T(8,128)(2,1)}, bf16[4,4,2,80,128]{4,3,2,1,0:T(8,128)(2,1)}, f32[4,4,2,16,128]{4,3,2,1,0:T(8,128)}, bf16[4,4,...) custom-call(bf16[32,2048]{1,0:T(8,128)(2,1)} %get-tuple-element.89.refs_0_, bf16[80,128]{1,0:T(8,128)(2,1)} %fusion.63.refs_1_, ...), custom_call_target="tpu_custom_call" | custom-call | bytes 33554432 | tf_op jit(solution)/shard_map/gather_weights/pallas_call | solution.py:425
  122.0 5.7 %fusion.77.conv_ref = f32[768,2048]{1,0:T(8,128)S(1)} fusion(bf16[1024,2048]{1,0:T(8,128)(2,1)} %bitcast.148, bf16[768,1024]{1,0:T(8,128)(2,1)S(1)} %copy-done.7, f32[1024]{0:T(1024)S(1)} %bitcast.135, f32[768]{0:T(1024)S(1)} %fusion.69), kind=kOutput, calls=%fused_computation.163 | convolution fusion | flops 3224371200 | bytes 12065792 | tf_op jit(solution)/shard_map/dot_general | solution.py:670
  127.8 5.6 %fusion.38 = f32[768,2048]{1,0:T(8,128)} fusion(bf16[2048,1024]{1,0:T(8,128)(2,1)S(1)} %bitcast.150, bf16[768,1024]{1,0:T(8,128)(2,1)S(1)} %copy-done.15, f32[768]{0:T(1024)S(1)} %fusion.68), kind=kOutput, calls=%fused_computation.71 | convolution fusion | flops 3223584768 | bytes 12061696 | tf_op jit(solution)/shard_map/dot_general | solution.py:599
  133.3 7.0 %add_multiply_fusion = (f32[768,2048]{1,0:T(8,128)}, f32[768,2048]{1,0:T(8,128)S(1)}) fusion(f32[768]{0:T(1024)S(1)} %get-tuple-element.94, f32[768,2048]{1,0:T(8,128)S(1)} %fusion.77.conv_ref, f32[2048]{0:T(1024)S(1)} %bitcast.130, f32[768]{0:T(1024)S(1)} %get-tuple-element.95, f32[2048]{0:T(1024)S(1)} %bitcast.131, f32[768]{0:T(1024)S(1)} %compare_convert_fusion.6, ...), kind=kLoop, calls=%fused_computation.21 | loop fusion | flops 28311552 | bytes 18924544 | tf_op jit(solution)/shard_map/mul | solution.py:675
  140.3 1.7 multiply_convert_fusion.1.mixed_ref
  145.6 2.1 concatenate.25.sel.flags
  147.7 4.8 convolution_add_fusion.v_ref
  152.6 47.2 %scan_forward.1 = (f32[768,2048]{1,0:T(8,128)}, f32[768,2048]{1,0:T(8,128)}, f32[768,16,16,128]{3,2,1,0:T(8,128)}) custom-call(f32[768,2048]{1,0:T(8,128)} %convolution_add_fusion.v_ref, bf16[768,2048]{1,0:T(8,128)(2,1)S(1)} %multiply_convert_fusion.1.mixed_ref, f32[768,128]{1,0:T(8,128)S(1)} %concatenate.25.sel.flags, f32[16,16,128]{2,1,0:T(8,128)S(1)} %copy-done.3), custom_call_target="tpu_custom_call" | custom-call | flops 150994944 | bytes 100663296 | tf_op jit(solution)/shard_map/scan_forward/pallas_call | solution.py:256
  199.8 11.6 %fusion.11 = (bf16[768,2048]{1,0:T(8,128)(2,1)}, bf16[768,2048]{1,0:T(8,128)(2,1)}, f32[768,2048]{1,0:T(8,128)}) fusion(f32[768,2048]{1,0:T(8,128)S(1)} %bitcast.153, f32[768,2048]{1,0:T(8,128)} %get-tuple-element.38, bf16[768,2048]{1,0:T(8,128)(2,1)S(1)} %multiply_convert_fusion.1.mixed_ref, f32[2048]{0:T(1024)S(1)} %bitcast.141, ...), kind=kOutput, calls=%fused_computation.15 | convolution fusion | flops 3252682752 | bytes 34094080 | tf_op jit(solution)/shard_map/dot_general | solution.py:671
  211.4 6.8 %fusion.26 = bf16[768,1024]{1,0:T(8,128)(2,1)} fusion(bf16[768,1024]{1,0:T(8,128)(2,1)S(1)} %copy-done.8, bf16[768,2048]{1,0:T(8,128)(2,1)} %get-tuple-element.68, bf16[2048,1024]{1,0:T(8,128)(2,1)S(1)} %bitcast.151, f32[768]{0:T(1024)S(1)} %copy-done.28), kind=kOutput, calls=%fused_computation.50 | convolution fusion | flops 3224371200 | bytes 10488832 | tf_op jit(solution)/shard_map/dot_general | solution.py:692
  218.2 115.4 %scan_backward.1 = (bf16[768,2048]{1,0:T(8,128)(2,1)}, bf16[768,2048]{1,0:T(8,128)(2,1)}, bf16[768,96]{1,0:T(8,128)(2,1)}, f32[8,8,2048]{2,1,0:T(8,128)}, f32[16,16,128]{2,1,0:T(8,128)}) custom-call(f32[768,2048]{1,0:T(8,128)} %convolution_add_fusion.v_ref, f32[768,2048]{1,0:T(8,128)} %get-tuple-element.41.dt_ref, bf16[768,2048]{1,0:T(8,128)(2,1)} %copy-done, ...), custom_call_target="tpu_custom_call" | custom-call | flops 503316480 | bytes 100663296 | tf_op jit(solution)/shard_map/scan_backward/pallas_call | solution.py:298
  333.7 6.4 %fusion.83 = f32[768,1024]{1,0:T(8,128)S(1)} fusion(bf16[768,2048]{1,0:T(8,128)(2,1)} %get-tuple-element.44, bf16[1024,2048]{1,0:T(8,128)(2,1)} %bitcast.149), kind=kOutput, calls=%fused_computation.167 | convolution fusion | flops 3221225472 | bytes 10485760 | tf_op jit(solution)/shard_map/dot_general | solution.py:599
  340.1 4.0 fusion.22
  344.2 2.1 fusion.24
  350.3 8.1 %convolution_convert_fusion.2 = bf16[2048,1024]{1,0:T(8,128)(2,1)} fusion(bf16[768,2048]{1,0:T(8,128)(2,1)} %get-tuple-element.68, bf16[768,1024]{1,0:T(8,128)(2,1)} %param.23, f32[768]{0:T(1024)S(1)} %copy-done.28), kind=kOutput, calls=%fused_computation.42 | convolution fusion | flops 3225681920 | bytes 8915968 | tf_op jit(solution)/shard_map/dot_general | solution.py:599
  358.3 5.3 %convolution_convert_fusion.1 = bf16[1024,2048]{1,0:T(8,128)(2,1)} fusion(bf16[768,2048]{1,0:T(8,128)(2,1)S(1)} %copy-done.39, bf16[768,1024]{1,0:T(8,128)(2,1)S(1)} %copy-done.9, f32[1024]{0:T(1024)S(1)} %bitcast.139, f32[768]{0:T(1024)S(1)} %fusion.69), kind=kOutput, calls=%fused_computation.41 | convolution fusion | flops 3226468352 | bytes 8920064 | tf_op jit(solution)/shard_map/dot_general | solution.py:599
  363.7 5.5 %convolution_convert_fusion = bf16[1024,2048]{1,0:T(8,128)(2,1)} fusion(bf16[768,2048]{1,0:T(8,128)(2,1)S(1)} %copy-done.37, bf16[768,1024]{1,0:T(8,128)(2,1)S(1)} %copy-done.9, f32[1024]{0:T(1024)S(1)} %bitcast.140, f32[768]{0:T(1024)S(1)} %fusion.69), kind=kOutput, calls=%fused_computation.40 | convolution fusion | flops 3226468352 | bytes 8920064 | tf_op jit(solution)/shard_map/dot_general | solution.py:599
  369.2 112.2 %sum_gradients.1 = (bf16[4,2,64,1024]{3,2,1,0:T(8,128)(2,1)S(1)}, bf16[4,2,32,2048]{3,2,1,0:T(8,128)(2,1)S(1)}, bf16[4,2,32,2048]{3,2,1,0:T(8,128)(2,1)S(1)}, bf16[4,2,48,256]{3,2,1,0:T(8,128)(2,1)S(1)}) custom-call(bf16[4,4,2,64,1024]{4,3,2,1,0:T(8,128)(2,1)} %bitcast.111, bf16[4,4,2,32,2048]{4,3,2,1,0:T(8,128)(2,1)} %bitcast.112, ...), custom_call_target="tpu_custom_call" | custom-call | bytes 33554432 | tf_op jit(solution)/shard_map/sum_gradients/pallas_call | solution.py:537
  486.7 3.6 multiply_reduce_fusion
  494.2 11.3 %psum.7 = f32[]{:T(128)} all-reduce(f32[]{:T(128)S(6)} %add.251), channel_id=1, replica_groups=mesh['dp'=8,'fsdp'=4] {'fsdp'}, use_global_device_ids=true, to_apply=%region_10.11 | all-reduce | flops 1 | bytes 8 | tf_op jit(solution)/shard_map/psum | solution.py:757
  506.9 1.6 fusion.61
  508.4 2.0 fusion.52
  510.4 1.9 fusion.46
  512.3 6.6 %fusion.33 = (f32[512,1024]{1,0:T(8,128)}, f32[512,1024]{1,0:T(8,128)}) fusion(f32[512,1024]{1,0:T(8,128)} %param.29, f32[512,1024]{1,0:T(8,128)} %param.41, f32[512,1024]{1,0:T(8,128)} %param.35, f32[]{:T(128)S(6)} %min.3, bf16[4,2,64,1024]{3,2,1,0:T(8,128)(2,1)S(1)} %get-tuple-element.52), kind=kLoop, calls=%fused_computation.60 | loop fusion | flops 7864320 | bytes 11534340 | tf_op jit(solution)/shard_map/add | solution.py:615
  518.9 5.9 %fusion.18 = f32[256,4096]{1,0:T(8,128)} fusion(f32[256,4096]{1,0:T(8,128)S(1)} %copy-done.6, f32[256,4096]{1,0:T(8,128)S(1)} %copy-done.10, f32[256,4096]{1,0:T(8,128)S(1)} %copy-done.5, f32[256,4096]{1,0:T(8,128)} %param.31, f32[]{:T(128)S(6)} %min.3), kind=kLoop, calls=%fused_computation.35 | loop fusion | flops 14680064 | bytes 20971524 | tf_op jit(solution)/shard_map/add | solution.py:615
  (145 shorter events, 23.8 us)
Async XLA Ops:
  6.6 121.1 %copy-start.27 = (f32[768]{0:T(1024)}, f32[768]{0:T(1024)S(1)}, u32[]{:S(2)}) copy-start(f32[768]{0:T(1024)S(1)} %fusion.68) | copy-start | bytes 9220
  116.2 4.2 copy-start.19
  117.5 4.5 copy-start.24
  121.2 20.8 %copy-start.11 = (bf16[12,8,4,512]{3,1,2,0:T(8,128)(2,1)}, bf16[12,8,4,512]{3,1,2,0:T(8,128)(2,1)S(1)}, u32[]{:S(2)}) copy-start(bf16[12,8,4,512]{3,1,2,0:T(8,128)(2,1)S(1)} %copy.60) | copy-start | bytes 1179652
  122.0 5.7 %copy-start.15 = (bf16[768,1024]{1,0:T(8,128)(2,1)S(1)}, bf16[768,1024]{1,0:T(8,128)(2,1)}, u32[]{:S(2)}) copy-start(bf16[768,1024]{1,0:T(8,128)(2,1)} %param.23) | copy-start | bytes 4718596
  122.0 5.7 %copy-start.35 = (bf16[4,4,2,64,1024]{4,3,2,1,0:T(8,128)(2,1)S(1)}, bf16[4,4,2,64,1024]{4,3,2,1,0:T(8,128)(2,1)}, u32[]{:S(2)}) copy-start(bf16[4,4,2,64,1024]{4,3,2,1,0:T(8,128)(2,1)} %get-tuple-element.40) | copy-start | bytes 12582916
  127.7 5.6 %copy-start.4 = (f32[768,2048]{1,0:T(8,128)}, f32[768,2048]{1,0:T(8,128)S(1)}, u32[]{:S(2)}) copy-start(f32[768,2048]{1,0:T(8,128)S(1)} %fusion.77.conv_ref) | copy-start | bytes 18874372
  142.1 57.7 %copy-start = (bf16[768,2048]{1,0:T(8,128)(2,1)}, bf16[768,2048]{1,0:T(8,128)(2,1)S(1)}, u32[]{:S(2)}) copy-start(bf16[768,2048]{1,0:T(8,128)(2,1)S(1)} %multiply_convert_fusion.1.mixed_ref) | copy-start | bytes 9437188
  147.7 4.8 copy-start.2
  147.7 4.8 copy-start.3
  147.7 52.0 %slice-start = ((s8[6291456]{0:T(1024)(128)(4,1)}), s8[4194304]{0:T(1024)(128)(4,1)S(1)}, s32[]{:S(2)}) async-start(s8[6291456]{0:T(1024)(128)(4,1)} %bitcast.152), calls=%async_computation | async-start | bytes 8388608
  152.6 47.2 %copy-start.8 = (bf16[768,1024]{1,0:T(8,128)(2,1)S(1)}, bf16[768,1024]{1,0:T(8,128)(2,1)}, u32[]{:S(2)}) copy-start(bf16[768,1024]{1,0:T(8,128)(2,1)} %param.21) | copy-start | bytes 4718596
  152.6 47.2 %copy-start.25 = (f32[1,2,4,128]{3,1,2,0:T(2,128)S(1)}, f32[1,2,4,128]{3,1,2,0:T(2,128)}, u32[]{:S(2)}) copy-start(f32[1,2,4,128]{3,1,2,0:T(2,128)} %copy-done.24) | copy-start | bytes 12292
  152.6 47.2 %copy-start.26 = (f32[1,4,4,128]{3,1,2,0:T(4,128)S(1)}, f32[1,4,4,128]{3,1,2,0:T(4,128)}, u32[]{:S(2)}) copy-start(f32[1,4,4,128]{3,1,2,0:T(4,128)} %copy.63) | copy-start | bytes 24580
  152.6 47.2 %copy-start.33 = (bf16[4,4,2,32,2048]{4,3,2,1,0:T(8,128)(2,1)S(1)}, bf16[4,4,2,32,2048]{4,3,2,1,0:T(8,128)(2,1)}, u32[]{:S(2)}) copy-start(bf16[4,4,2,32,2048]{4,3,2,1,0:T(8,128)(2,1)} %get-tuple-element.39) | copy-start | bytes 12582916
  152.6 47.2 %slice-start.1 = ((s8[6291456]{0:T(1024)(128)(4,1)}), s8[2097152]{0:T(1024)(128)(4,1)S(1)}, s32[]{:S(2)}) async-start(s8[6291456]{0:T(1024)(128)(4,1)} %bitcast.152), calls=%async_computation.1 | async-start | bytes 4194304
  199.8 11.6 %copy-start.28 = (f32[768]{0:T(1024)S(1)}, f32[768]{0:T(1024)}, u32[]{:S(2)}) copy-start(f32[768]{0:T(1024)} %copy-done.27) | copy-start | bytes 9220
  199.8 11.6 %copy-start.36 = (bf16[4,4,2,64,1024]{4,3,2,1,0:T(8,128)(2,1)S(1)}, bf16[4,4,2,64,1024]{4,3,2,1,0:T(8,128)(2,1)}, u32[]{:S(2)}) copy-start(bf16[4,4,2,64,1024]{4,3,2,1,0:T(8,128)(2,1)} %get-tuple-element.40) | copy-start | bytes 12582916
  333.6 6.4 %copy-start.9 = (bf16[768,1024]{1,0:T(8,128)(2,1)S(1)}, bf16[768,1024]{1,0:T(8,128)(2,1)}, u32[]{:S(2)}) copy-start(bf16[768,1024]{1,0:T(8,128)(2,1)} %param.21) | copy-start | bytes 4718596
  333.6 6.4 %copy-start.34 = (bf16[4,4,2,32,2048]{4,3,2,1,0:T(8,128)(2,1)S(1)}, bf16[4,4,2,32,2048]{4,3,2,1,0:T(8,128)(2,1)}, u32[]{:S(2)}) copy-start(bf16[4,4,2,32,2048]{4,3,2,1,0:T(8,128)(2,1)} %get-tuple-element.39) | copy-start | bytes 12582916
  333.7 6.4 %copy-start.38 = (bf16[768,2048]{1,0:T(8,128)(2,1)S(1)}, bf16[768,2048]{1,0:T(8,128)(2,1)}, u32[]{:S(2)}) copy-start(bf16[768,2048]{1,0:T(8,128)(2,1)} %get-tuple-element.67) | copy-start | bytes 9437188
  350.2 8.1 %copy-start.39 = (bf16[768,2048]{1,0:T(8,128)(2,1)S(1)}, bf16[768,2048]{1,0:T(8,128)(2,1)}, u32[]{:S(2)}) copy-start(bf16[768,2048]{1,0:T(8,128)(2,1)} %get-tuple-element.67) | copy-start | bytes 9437188
  358.3 5.4 %copy-start.37 = (bf16[768,2048]{1,0:T(8,128)(2,1)S(1)}, bf16[768,2048]{1,0:T(8,128)(2,1)}, u32[]{:S(2)}) copy-start(bf16[768,2048]{1,0:T(8,128)(2,1)} %get-tuple-element.44) | copy-start | bytes 9437188
  482.9 23.3 %copy-start.30 = (f32[1,256]{1,0:T(1,128)}, f32[1,256]{1,0:T(1,128)S(1)}, u32[]{:S(2)}) copy-start(f32[1,256]{1,0:T(1,128)S(1)} %slice.182) | copy-start | bytes 3076
  486.7 23.8 %copy-start.17 = (f32[96,512]{1,0:T(8,128)}, f32[96,512]{1,0:T(8,128)S(1)}, u32[]{:S(2)}) copy-start(f32[96,512]{1,0:T(8,128)S(1)} %get-tuple-element.62) | copy-start | bytes 589828
  486.7 19.6 %copy-start.29 = (f32[256]{0:T(256)S(1)}, f32[256]{0:T(256)}, u32[]{:S(2)}) copy-start(f32[256]{0:T(256)} %param.24) | copy-start | bytes 3076
  486.7 19.6 %copy-start.31 = (f32[256]{0:T(256)S(1)}, f32[256]{0:T(256)}, u32[]{:S(2)}) copy-start(f32[256]{0:T(256)} %param.36) | copy-start | bytes 3076
  486.7 19.6 %copy-start.32 = (f32[256]{0:T(256)S(1)}, f32[256]{0:T(256)}, u32[]{:S(2)}) copy-start(f32[256]{0:T(256)} %param.30) | copy-start | bytes 3076
  486.7 23.7 %copy-start.18 = (f32[96,512]{1,0:T(8,128)S(1)}, f32[96,512]{1,0:T(8,128)}, u32[]{:S(2)}) copy-start(f32[96,512]{1,0:T(8,128)} %param.26) | copy-start | bytes 589828
  508.4 10.4 %copy-start.10 = (f32[256,4096]{1,0:T(8,128)S(1)}, f32[256,4096]{1,0:T(8,128)}, u32[]{:S(2)}) copy-start(f32[256,4096]{1,0:T(8,128)} %param.37) | copy-start | bytes 12582916
  512.3 6.6 %copy-start.5 = (f32[256,4096]{1,0:T(8,128)S(1)}, f32[256,4096]{1,0:T(8,128)}, u32[]{:S(2)}) copy-start(f32[256,4096]{1,0:T(8,128)} %get-tuple-element.64) | copy-start | bytes 12582916
  512.3 6.6 %copy-start.6 = (f32[256,4096]{1,0:T(8,128)S(1)}, f32[256,4096]{1,0:T(8,128)}, u32[]{:S(2)}) copy-start(f32[256,4096]{1,0:T(8,128)} %param.25) | copy-start | bytes 12582916
  (10 other events, 22.3 us)

commit v4 on v3

--- a/solution.py
+++ b/solution.py
@@ -19,7 +19,7 @@
 GROUP = 8
 BACK = 4
 WIDE = 512
-TAIL = 4
+TAIL = 2
 
 norm_eps = 1e-05
 beta_one = 0.9
@@ -58,6 +58,335 @@
     return total
 
 
+def mesh_copy(src, dst, sems, at, device):
+    return pltpu.make_async_remote_copy(
+        src_ref=src,
+        dst_ref=dst,
+        send_sem=sems.at[0, at],
+        recv_sem=sems.at[1, at],
+        device_id=device,
+        device_id_type=pl.DeviceIdType.MESH,
+    )
+
+
+def placed(plan):
+    group = lax.axis_index("dp")
+    return lax.axis_index("fsdp"), group // 2, lax.rem(group, 2)
+
+
+def peers_of(plan):
+    shards, places = plan
+    mine, place, side = placed(plan)
+    along = [(place * 2 + side, lax.rem(mine + k, shards)) for k in range(1, shards)]
+    plane = [((place ^ j) * 2 + side, mine) for j in range(1, places)]
+    return along, plane, (place * 2 + 1 - side, mine)
+
+
+def greet(plan):
+    along, plane, pair = peers_of(plan)
+    barrier = pltpu.get_barrier_semaphore()
+    everyone = along + plane + [pair]
+    for device in everyone:
+        pl.semaphore_signal(barrier, inc=1, device_id=device, device_id_type=pl.DeviceIdType.MESH)
+    pl.semaphore_wait(barrier, len(everyone))
+
+
+class Gather:
+    def __init__(self, plan, own, full, near, far, wide, cross):
+        self.plan, self.own, self.full = plan, own, full
+        self.near, self.far, self.wide, self.cross = near, far, wide, cross
+        self.count = len(own)
+
+    @staticmethod
+    def scratch(plan, count):
+        shards, places = plan
+        return [
+            pltpu.SemaphoreType.DMA((count,)),
+            pltpu.SemaphoreType.DMA((2, count * (shards - 1))),
+            pltpu.SemaphoreType.DMA((2, count * (places - 1))),
+            pltpu.SemaphoreType.DMA((2, count)),
+        ]
+
+    @staticmethod
+    def shapes(plan, pieces):
+        return [jax.ShapeDtypeStruct(plan + (2,) + piece.shape, piece.dtype) for piece in pieces]
+
+    def keep(self, s):
+        mine, place, side = placed(self.plan)
+        return pltpu.make_async_copy(self.own[s], self.full[s].at[mine, place, side], self.near.at[s])
+
+    def along(self, s):
+        mine, place, side = placed(self.plan)
+        return [
+            mesh_copy(
+                self.own[s], self.full[s].at[mine, place, side], self.far, s * (self.plan[0] - 1) + k, device
+            )
+            for k, device in enumerate(peers_of(self.plan)[0])
+        ]
+
+    def plane(self, s):
+        _, place, side = placed(self.plan)
+        part = self.full[s].at[:, place, side]
+        return [
+            mesh_copy(part, part, self.wide, s * (self.plan[1] - 1) + k, device)
+            for k, device in enumerate(peers_of(self.plan)[1])
+        ]
+
+    def pair(self, s):
+        part = self.full[s].at[:, :, placed(self.plan)[2]]
+        return mesh_copy(part, part, self.cross, s, peers_of(self.plan)[2])
+
+    def start(self, s):
+        self.keep(s).start()
+        for copy in self.along(s):
+            copy.start()
+
+    def spread(self, s):
+        self.keep(s).wait()
+        for copy in self.along(s):
+            copy.wait_recv()
+        for copy in self.plane(s):
+            copy.start()
+
+    def share(self, s):
+        for copy in self.plane(s):
+            copy.wait_recv()
+        self.pair(s).start()
+
+    def end(self, s):
+        for copy in self.along(s) + self.plane(s):
+            copy.wait_send()
+        self.pair(s).wait()
+
+
+def gather_kernel(plan, count, *refs):
+    gather = Gather(plan, refs[:count], refs[count : 2 * count], *refs[2 * count :])
+    greet(plan)
+    for stage in (gather.start, gather.spread, gather.share, gather.end):
+        for s in range(count):
+            stage(s)
+
+
+def gather_pieces(plan, pieces, name, collective_id):
+    count = len(pieces)
+    return pl.pallas_call(
+        functools.partial(gather_kernel, plan, count),
+        in_specs=[pl.BlockSpec(memory_space=pl.ANY)] * count,
+        out_specs=[pl.BlockSpec(memory_space=pl.ANY)] * count,
+        out_shape=Gather.shapes(plan, pieces),
+        scratch_shapes=Gather.scratch(plan, count),
+        compiler_params=pltpu.CompilerParams(collective_id=collective_id, has_side_effects=True),
+        cost_estimate=pl.CostEstimate(flops=0, bytes_accessed=32 << 20, transcendentals=0),
+        name=name,
+    )(*pieces)
+
+
+def wide_sum(values):
+    total = values[0].astype(jnp.float32)
+    for value in values[1:]:
+        total = total + value.astype(jnp.float32)
+    return total.astype(jnp.bfloat16)
+
+
+class Reduce:
+    def __init__(self, plan, parts, full, scratch):
+        count = len(parts)
+        self.plan, self.parts, self.full, self.count = plan, parts, full, count
+        self.held, self.from_pair, self.from_plane, self.from_along, self.piece = (
+            scratch[k * count : (k + 1) * count] for k in range(5)
+        )
+        self.near, self.cross, self.wide, self.far, self.back, self.over = scratch[5 * count :]
+
+    @staticmethod
+    def scratch(plan, parts):
+        shards, places = plan
+        count = len(parts)
+        leads = [(shards, places), (shards, places), (places - 1, shards), (shards - 1,), ()]
+        return [pltpu.VMEM(lead + part.shape[3:], jnp.bfloat16) for lead in leads for part in parts] + [
+            pltpu.SemaphoreType.DMA((2, count)),
+            pltpu.SemaphoreType.DMA((2, count)),
+            pltpu.SemaphoreType.DMA((2, count * (places - 1))),
+            pltpu.SemaphoreType.DMA((2, count * (shards - 1))),
+            pltpu.SemaphoreType.DMA((2, count * (places - 1))),
+            pltpu.SemaphoreType.DMA((2, count)),
+        ]
+
+    @staticmethod
+    def shapes(plan, parts):
+        return [jax.ShapeDtypeStruct((plan[1], 2) + part.shape[3:], jnp.bfloat16) for part in parts]
+
+    def keep(self, s):
+        side = placed(self.plan)[2]
+        return pltpu.make_async_copy(self.parts[s].at[:, :, side], self.held[s], self.near.at[0, s])
+
+    def pair(self, s):
+        side = placed(self.plan)[2]
+        return mesh_copy(
+            self.parts[s].at[:, :, 1 - side], self.from_pair[s], self.cross, s, peers_of(self.plan)[2]
+        )
+
+    def plane(self, s):
+        place = placed(self.plan)[1]
+        return [
+            mesh_copy(
+                self.held[s].at[:, place ^ (k + 1)],
+                self.from_plane[s].at[k],
+                self.wide,
+                s * (self.plan[1] - 1) + k,
+                device,
+            )
+            for k, device in enumerate(peers_of(self.plan)[1])
+        ]
+
+    def along(self, s):
+        mine, place, _ = placed(self.plan)
+        shards = self.plan[0]
+        return [
+            mesh_copy(
+                self.held[s].at[lax.rem(mine + k + 1, shards), place],
+                self.from_along[s].at[k],
+                self.far,
+                s * (shards - 1) + k,
+                device,
+            )
+            for k, device in enumerate(peers_of(self.plan)[0])
+        ]
+
+    def put(self, s):
+        _, place, side = placed(self.plan)
+        return pltpu.make_async_copy(self.piece[s], self.full[s].at[place, side], self.near.at[1, s])
+
+    def home(self, s):
+        _, place, side = placed(self.plan)
+        return [
+            mesh_copy(self.piece[s], self.full[s].at[place, side], self.back, s * (self.plan[1] - 1) + k, device)
+            for k, device in enumerate(peers_of(self.plan)[1])
+        ]
+
+    def other(self, s):
+        part = self.full[s].at[:, placed(self.plan)[2]]
+        return mesh_copy(part, part, self.over, s, peers_of(self.plan)[2])
+
+    def start(self, s):
+        self.keep(s).start()
+        self.pair(s).start()
+
+    def sum_pair(self, s):
+        self.keep(s).wait()
+        self.pair(s).wait_recv()
+        held, other = self.held[s], self.from_pair[s]
+
+        @pl.loop(0, self.plan[0] * self.plan[1])
+        def _(i):
+            a, b = i // self.plan[1], lax.rem(i, self.plan[1])
+            held[a, b] = wide_sum([held[a, b], other[a, b]])
+
+        for copy in self.plane(s):
+            copy.start()
+
+    def sum_plane(self, s):
+        place = placed(self.plan)[1]
+        for copy in self.plane(s):
+            copy.wait_recv()
+        held, others = self.held[s], self.from_plane[s]
+
+        @pl.loop(0, self.plan[0])
+        def _(i):
+            held[i, place] = wide_sum([held[i, place]] + [others[k, i] for k in range(self.plan[1] - 1)])
+
+        for copy in self.along(s):
+            copy.start()
+
+    def sum_along(self, s):
+        mine, place, _ = placed(self.plan)
+        for copy in self.along(s):
+            copy.wait_recv()
+        others = self.from_along[s]
+        self.piece[s][...] = wide_sum([self.held[s][mine, place]] + [others[k] for k in range(self.plan[0] - 1)])
+        self.put(s).start()
+        for copy in self.home(s):
+            copy.start()
+
+    def share(self, s):
+        self.put(s).wait()
+        for copy in self.home(s):
+            copy.wait_recv()
+        self.other(s).start()
+
+    def end(self, s):
+        self.pair(s).wait_send()
+        for copy in self.plane(s) + self.along(s) + self.home(s):
+            copy.wait_send()
+        self.other(s).wait()
+
+
+def reduce_kernel(plan, count, *refs):
+    reduce = Reduce(plan, refs[:count], refs[count : 2 * count], refs[2 * count :])
+    greet(plan)
+    stages = (reduce.start, reduce.sum_pair, reduce.sum_plane, reduce.sum_along, reduce.share, reduce.end)
+    for stage in stages:
+        for s in range(count):
+            stage(s)
+
+
+def reduce_pieces(plan, parts, name, collective_id):
+    count = len(parts)
+    return pl.pallas_call(
+        functools.partial(reduce_kernel, plan, count),
+        in_specs=[pl.BlockSpec(memory_space=pl.ANY)] * count,
+        out_specs=[pl.BlockSpec(memory_space=pl.ANY)] * count,
+        out_shape=Reduce.shapes(plan, parts),
+        scratch_shapes=Reduce.scratch(plan, parts),
+        compiler_params=pltpu.CompilerParams(
+            collective_id=collective_id, has_side_effects=True, vmem_limit_bytes=48 << 20
+        ),
+        cost_estimate=pl.CostEstimate(flops=0, bytes_accessed=32 << 20, transcendentals=0),
+        name=name,
+    )(*parts)
+
+
+def at_steps(stages, count, steps):
+    for stage, when in zip(stages, steps):
+        for s in range(count):
+            pl.when(pl.program_id(0) == when[s])(functools.partial(stage, s))
+
+
+def cut_of(rows, columns, dp):
+    best = None
+    across = 1
+    while across <= dp and across * LANES <= columns:
+        down = dp // across
+        tall = -(-rows // (16 * down)) * 16
+        if best is None or down * tall < best[0] * best[2]:
+            best = (down, across, tall)
+        across *= 2
+    return best
+
+
+def to_pieces(shards, array, dp):
+    rows, columns = array.shape[1:]
+    down, across, tall = cut_of(rows, columns, dp)
+    array = jnp.pad(array, ((0, 0), (0, down * tall - rows), (0, 0)))
+    array = array.reshape(shards, down, tall, across, columns // across).transpose(0, 1, 3, 2, 4)
+    return array.reshape(shards, dp // 2, 2, tall, columns // across)
+
+
+def from_pieces(pieces, rows, columns, dp):
+    shards = pieces.shape[0]
+    down, across, tall = cut_of(rows, columns, dp)
+    array = pieces.reshape(shards, down, across, tall, columns // across).transpose(0, 1, 3, 2, 4)
+    return array.reshape(shards, down * tall, columns)[:, :rows]
+
+
+def own_piece(array, dp):
+    rows, columns = array.shape
+    down, across, tall = cut_of(rows, columns, dp)
+    array = jnp.pad(array, ((0, down * tall - rows), (0, 0)))
+    group = lax.axis_index("dp")
+    at = (group // across * tall, lax.rem(group, across) * (columns // across))
+    return lax.dynamic_slice(array, at, (tall, columns // across))
+
+
 def spread(ref, value, g):
     for col in range(COLS):
         ref[pl.ds(g * 8 * COLS + col, 8, stride=COLS), :] = value[:, LANES * col : LANES * (col + 1)]
@@ -92,10 +421,18 @@
     return jnp.maximum(v, 0.0) + jnp.where(small < 1 / 32, series, jnp.log(1.0 + small))
 
 
-def forward_kernel(v_ref, mixed_ref, sel, rates, y_ref, dt_ref, hs_ref, state, dts, us, bb, ys):
+def forward_kernel(plan, count, v_ref, mixed_ref, sel, rates, *refs):
+    own, refs = refs[:count], refs[count:]
+    (y_ref, dt_ref, hs_ref), full, refs = refs[:3], refs[3 : 3 + count], refs[3 + count :]
+    state, dts, us, bb, ys = refs[:5]
+    gather = Gather(plan, own, full, *refs[5:])
+
     @pl.when(pl.program_id(0) == 0)
     def _():
         state[...] = jnp.zeros_like(state)
+        greet(plan)
+
+    at_steps((gather.start, gather.spread, gather.share), count, ((0, 0), (3, 6), (8, 11)))
 
     @pl.loop(0, BLOCK // 8)
     def _(g):
@@ -129,17 +466,23 @@
     def _(g):
         unspread(y_ref, ys, g)
 
+    at_steps((gather.end,), count, ((11, 11),))
+
 
 def fold(value):
     return jnp.sum(value.reshape(value.shape[0] // 8, 8, value.shape[1]), axis=0)
 
 
 def backward_kernel(
-    v_ref, dt_ref, mixed_ref, gs_ref, sel, rates, vectors,
+    plan, count, v_ref, dt_ref, mixed_ref, gs_ref, sel, rates, vectors,
     step_weight, select_weight, hs_ref, last_ref, conv_ref, slope_ref, flags,
-    grad_conv_in, pre_low, chosen, grad_rows, grad_rates,
-    carry, dts, us, gss, bb, s1, s2, prods, parts, nat1, nat2, grad_mixed, taps,
+    *refs,
 ):
+    given, refs = refs[:count], refs[count:]
+    (grad_conv_in, pre_low, chosen, grad_rows, grad_rates), refs = refs[:5], refs[5:]
+    full, refs = refs[:count], refs[count:]
+    (carry, dts, us, gss, bb, s1, s2, prods, parts, nat1, nat2, grad_mixed, taps), refs = refs[:13], refs[13:]
+    reduce = Reduce(plan, given, full, refs)
     turn = lax.rem(pl.program_id(0), TAIL)
     tall = BLOCK * TAIL
     own = pl.ds(pl.multiple_of((TAIL - 1 - turn) * BLOCK, BLOCK), BLOCK)
@@ -149,6 +492,13 @@
         for ref in (carry, grad_rates, grad_rows, parts):
             ref[...] = jnp.zeros_like(ref)
         taps[:, tall:, :] = jnp.zeros_like(taps[:, tall:, :])
+        greet(plan)
+
+    at_steps(
+        (reduce.start, reduce.sum_pair, reduce.sum_plane, reduce.sum_along, reduce.share),
+        count,
+        ((0, 0), (1, 2), (4, 6), (7, 9), (9, 11)),
+    )
 
     @pl.loop(0, BLOCK // 16)
     def _(pair):
@@ -243,6 +593,8 @@
                 taps[j - 1, tall:, lanes] = taps[j - 1, :8, lanes]
             grad_conv_in[:, lanes] = result.astype(jnp.bfloat16)
 
+    at_steps((reduce.end,), count, ((11, 11),))
+
 
 def dot(left, right, left_dim, right_dim):
     return lax.dot_general(
@@ -250,42 +602,49 @@
     )
 
 
-def scan_forward(v, mixed, sel, rates):
+def scan_forward(v, mixed, sel, rates, plan, pieces):
     count = v.shape[0]
+    anywhere = [pl.BlockSpec(memory_space=pl.ANY)] * len(pieces)
     rows = pl.BlockSpec((BLOCK, DI), lambda i: (i, 0))
     return pl.pallas_call(
-        forward_kernel,
+        functools.partial(forward_kernel, plan, len(pieces)),
         grid=(count // BLOCK,),
         in_specs=[
             rows,
             rows,
             pl.BlockSpec((BLOCK, LANES), lambda i: (i, 0)),
             pl.BlockSpec((N, COLS, LANES), lambda i: (0, 0, 0)),
-        ],
-        out_specs=[rows, rows, pl.BlockSpec((BLOCK, N, COLS, LANES), lambda i: (i, 0, 0, 0))],
+        ]
+        + anywhere,
+        out_specs=[rows, rows, pl.BlockSpec((BLOCK, N, COLS, LANES), lambda i: (i, 0, 0, 0))] + anywhere,
         out_shape=[
             jax.ShapeDtypeStruct((count, DI), jnp.float32),
             jax.ShapeDtypeStruct((count, DI), jnp.float32),
             jax.ShapeDtypeStruct((count, N, COLS, LANES), jnp.float32),
-        ],
+        ]
+        + Gather.shapes(plan, pieces),
         scratch_shapes=[
             pltpu.VMEM((N, COLS, LANES), jnp.float32),
             pltpu.VMEM((BLOCK * COLS, LANES), jnp.float32),
             pltpu.VMEM((BLOCK * COLS, LANES), jnp.float32),
             pltpu.VMEM((BLOCK // 8, 2 * N, 8, LANES), jnp.float32),
             pltpu.VMEM((BLOCK * COLS, LANES), jnp.float32),
-        ],
-        compiler_params=pltpu.CompilerParams(vmem_limit_bytes=48 << 20),
+        ]
+        + Gather.scratch(plan, len(pieces)),
+        compiler_params=pltpu.CompilerParams(
+            vmem_limit_bytes=48 << 20, collective_id=2, has_side_effects=True
+        ),
         cost_estimate=pl.CostEstimate(
             flops=6 * count * N * DI, bytes_accessed=4 * count * N * DI, transcendentals=count * N * DI
         ),
         name="scan_forward",
-    )(v, mixed, sel, rates)
-
-
-def scan_backward(v, dt, mixed, gs, conv_input, slope, sel, rates, vectors, step_weight, select_weight, states):
+    )(v, mixed, sel, rates, *pieces)
+
+
+def scan_backward(v, dt, mixed, gs, conv_input, slope, sel, rates, vectors, step_weight, select_weight, states, plan, summed):
     count = dt.shape[0]
     blocks = count // BLOCK
+    anywhere = [pl.BlockSpec(memory_space=pl.ANY)] * len(summed)
     rows = pl.BlockSpec((BLOCK, DI), lambda i: (blocks - 1 - i, 0))
 
     def tall(width):
@@ -296,7 +655,7 @@
 
     state = (N, COLS, LANES)
     return pl.pallas_call(
-        backward_kernel,
+        functools.partial(backward_kernel, plan, len(summed)),
         grid=(blocks,),
         in_specs=[
             rows,
@@ -313,15 +672,17 @@
             tall(DI),
             tall(DI),
             tall(LANES),
-        ],
-        out_specs=[tall(DI), tall(DI), tall(R + 2 * N), whole(8, 8, DI), whole(*state)],
+        ]
+        + anywhere,
+        out_specs=[tall(DI), tall(DI), tall(R + 2 * N), whole(8, 8, DI), whole(*state)] + anywhere,
         out_shape=[
             jax.ShapeDtypeStruct((count, DI), jnp.bfloat16),
             jax.ShapeDtypeStruct((count, DI), jnp.bfloat16),
             jax.ShapeDtypeStruct((count, R + 2 * N), jnp.bfloat16),
             jax.ShapeDtypeStruct((8, 8, DI), jnp.float32),
             jax.ShapeDtypeStruct(state, jnp.float32),
-        ],
+        ]
+        + Reduce.shapes(plan, summed),
         scratch_shapes=[pltpu.VMEM(state, jnp.float32)]
         + [pltpu.VMEM((BLOCK * COLS, LANES), jnp.float32)] * 3
         + [pltpu.VMEM((BLOCK // 8, 2 * N, 8, LANES), jnp.float32)]
@@ -330,269 +691,19 @@
         + [pltpu.VMEM((LANES, LANES), jnp.float32)]
         + [pltpu.VMEM((BLOCK, DI), jnp.float32)] * 2
         + [pltpu.VMEM((BLOCK * TAIL, DI), jnp.float32)]
-        + [pltpu.VMEM((CONV - 1, BLOCK * TAIL + 8, DI), jnp.float32)],
-        compiler_params=pltpu.CompilerParams(vmem_limit_bytes=60 << 20),
+        + [pltpu.VMEM((CONV - 1, BLOCK * TAIL + 8, DI), jnp.float32)]
+        + Reduce.scratch(plan, summed),
+        compiler_params=pltpu.CompilerParams(
+            vmem_limit_bytes=60 << 20, collective_id=3, has_side_effects=True
+        ),
         cost_estimate=pl.CostEstimate(
             flops=20 * count * N * DI, bytes_accessed=4 * count * N * DI, transcendentals=count * N * DI
         ),
         name="scan_backward",
     )(
         v, dt, mixed, gs, sel, rates, vectors, step_weight, select_weight,
-        states, states, conv_input, slope, sel,
-    )
-
-
-def mesh_copy(src, dst, sems, at, device):
-    return pltpu.make_async_remote_copy(
-        src_ref=src,
-        dst_ref=dst,
-        send_sem=sems.at[0, at],
-        recv_sem=sems.at[1, at],
-        device_id=device,
-        device_id_type=pl.DeviceIdType.MESH,
-    )
-
-
-def placed(plan):
-    group = lax.axis_index("dp")
-    return lax.axis_index("fsdp"), group // 2, lax.rem(group, 2)
-
-
-def peers_of(plan):
-    shards, places = plan
-    mine, place, side = placed(plan)
-    along = [(place * 2 + side, lax.rem(mine + k, shards)) for k in range(1, shards)]
-    plane = [((place ^ j) * 2 + side, mine) for j in range(1, places)]
-    return along, plane, (place * 2 + 1 - side, mine)
-
-
-def greet(plan):
-    along, plane, pair = peers_of(plan)
-    barrier = pltpu.get_barrier_semaphore()
-    everyone = along + plane + [pair]
-    for device in everyone:
-        pl.semaphore_signal(barrier, inc=1, device_id=device, device_id_type=pl.DeviceIdType.MESH)
-    pl.semaphore_wait(barrier, len(everyone))
-
-
-def gather_kernel(plan, count, *refs):
-    own, full = refs[:count], refs[count : 2 * count]
-    near, far, wide, cross = refs[2 * count :]
-    shards, places = plan
-    mine, place, side = placed(plan)
-    along, plane, pair = peers_of(plan)
-    greet(plan)
-    local, first, second, third = [], [], [], []
-    for s in range(count):
-        keep = pltpu.make_async_copy(own[s], full[s].at[mine, place, side], near.at[s])
-        keep.start()
-        local.append(keep)
-        sends = [
-            mesh_copy(own[s], full[s].at[mine, place, side], far, s * (shards - 1) + k, device)
-            for k, device in enumerate(along)
-        ]
-        for copy in sends:
-            copy.start()
-        first.append(sends)
-    for s in range(count):
-        local[s].wait()
-        for copy in first[s]:
-            copy.wait_recv()
-        sends = [
-            mesh_copy(
-                full[s].at[:, place, side], full[s].at[:, place, side], wide, s * (places - 1) + k, device
-            )
-            for k, device in enumerate(plane)
-        ]
-        for copy in sends:
-            copy.start()
-        second.append(sends)
-    for s in range(count):
-        for copy in second[s]:
-            copy.wait_recv()
-        copy = mesh_copy(full[s].at[:, :, side], full[s].at[:, :, side], cross, s, pair)
-        copy.start()
-        third.append(copy)
-    for s in range(count):
-        for copy in first[s] + second[s]:
-            copy.wait_send()
-        third[s].wait()
-
-
-def gather_pieces(plan, pieces, name, collective_id):
-    shards, places = plan
-    count = len(pieces)
-    return pl.pallas_call(
-        functools.partial(gather_kernel, plan, count),
-        in_specs=[pl.BlockSpec(memory_space=pl.ANY)] * count,
-        out_specs=[pl.BlockSpec(memory_space=pl.ANY)] * count,
-        out_shape=[jax.ShapeDtypeStruct((shards, places, 2) + piece.shape, piece.dtype) for piece in pieces],
-        scratch_shapes=[
-            pltpu.SemaphoreType.DMA((count,)),
-            pltpu.SemaphoreType.DMA((2, count * (shards - 1))),
-            pltpu.SemaphoreType.DMA((2, count * (places - 1))),
-            pltpu.SemaphoreType.DMA((2, count)),
-        ],
-        compiler_params=pltpu.CompilerParams(collective_id=collective_id, has_side_effects=True),
-        cost_estimate=pl.CostEstimate(flops=0, bytes_accessed=32 << 20, transcendentals=0),
-        name=name,
-    )(*pieces)
-
-
-def wide_sum(values):
-    total = values[0].astype(jnp.float32)
-    for value in values[1:]:
-        total = total + value.astype(jnp.float32)
-    return total.astype(jnp.bfloat16)
-
-
-def reduce_kernel(plan, count, *refs):
-    parts, full = refs[:count], refs[count : 2 * count]
-    held = refs[2 * count : 3 * count]
-    from_pair = refs[3 * count : 4 * count]
-    from_plane = refs[4 * count : 5 * count]
-    from_along = refs[5 * count : 6 * count]
-    near, cross, wide, far, back, over = refs[6 * count :]
-    shards, places = plan
-    mine, place, side = placed(plan)
-    along, plane, pair = peers_of(plan)
-    greet(plan)
-    local, first, second, third, fourth, fifth = [], [], [], [], [], []
-    for s in range(count):
-        keep = pltpu.make_async_copy(parts[s].at[:, :, side], held[s], near.at[s])
-        keep.start()
-        local.append(keep)
-        copy = mesh_copy(parts[s].at[:, :, 1 - side], from_pair[s], cross, s, pair)
-        copy.start()
-        first.append(copy)
-    for s in range(count):
-        local[s].wait()
-        first[s].wait_recv()
-
-        @pl.loop(0, shards * places)
-        def _(i, s=s):
-            a, b = i // places, lax.rem(i, places)
-            held[s][a, b] = wide_sum([held[s][a, b], from_pair[s][a, b]])
-
-        sends = [
-            mesh_copy(held[s].at[:, place ^ (k + 1)], from_plane[s].at[k], wide, s * (places - 1) + k, device)
-            for k, device in enumerate(plane)
-        ]
-        for copy in sends:
-            copy.start()
-        second.append(sends)
-    for s in range(count):
-        for copy in second[s]:
-            copy.wait_recv()
-
-        @pl.loop(0, shards)
-        def _(i, s=s):
-            held[s][i, place] = wide_sum([held[s][i, place]] + [from_plane[s][k, i] for k in range(places - 1)])
-
-        sends = [
-            mesh_copy(
-                held[s].at[lax.rem(mine + k + 1, shards), place],
-                from_along[s].at[k],
-                far,
-                s * (shards - 1) + k,
-                device,
-            )
-            for k, device in enumerate(along)
-        ]
-        for copy in sends:
-            copy.start()
-        third.append(sends)
-    for s in range(count):
-        for copy in third[s]:
-            copy.wait_recv()
-        full[s][place, side] = wide_sum([held[s][mine, place]] + [from_along[s][k] for k in range(shards - 1)])
-        sends = [
-            mesh_copy(full[s].at[place, side], full[s].at[place, side], back, s * (places - 1) + k, device)
-            for k, device in enumerate(plane)
-        ]
-        for copy in sends:
-            copy.start()
-        fourth.append(sends)
-    for s in range(count):
-        for copy in fourth[s]:
-            copy.wait_recv()
-        copy = mesh_copy(full[s].at[:, side], full[s].at[:, side], over, s, pair)
-        copy.start()
-        fifth.append(copy)
-    for s in range(count):
-        first[s].wait_send()
-        for copy in second[s] + third[s] + fourth[s]:
-            copy.wait_send()
-        fifth[s].wait()
-
-
-def reduce_pieces(plan, parts, name, collective_id):
-    shards, places = plan
-    count = len(parts)
-    tails = [part.shape[3:] for part in parts]
-
-    def scratch(*lead):
-        return [pltpu.VMEM(lead + tail, jnp.bfloat16) for tail in tails]
-
-    return pl.pallas_call(
-        functools.partial(reduce_kernel, plan, count),
-        in_specs=[pl.BlockSpec(memory_space=pl.ANY)] * count,
-        out_specs=[pl.BlockSpec(memory_space=pltpu.VMEM)] * count,
-        out_shape=[jax.ShapeDtypeStruct((places, 2) + tail, jnp.bfloat16) for tail in tails],
-        scratch_shapes=scratch(shards, places)
-        + scratch(shards, places)
-        + scratch(places - 1, shards)
-        + scratch(shards - 1)
-        + [
-            pltpu.SemaphoreType.DMA((count,)),
-            pltpu.SemaphoreType.DMA((2, count)),
-            pltpu.SemaphoreType.DMA((2, count * (places - 1))),
-            pltpu.SemaphoreType.DMA((2, count * (shards - 1))),
-            pltpu.SemaphoreType.DMA((2, count * (places - 1))),
-            pltpu.SemaphoreType.DMA((2, count)),
-        ],
-        compiler_params=pltpu.CompilerParams(
-            collective_id=collective_id, has_side_effects=True, vmem_limit_bytes=48 << 20
-        ),
-        cost_estimate=pl.CostEstimate(flops=0, bytes_accessed=32 << 20, transcendentals=0),
-        name=name,
-    )(*parts)
-
-
-def cut_of(rows, columns, dp):
-    best = None
-    across = 1
-    while across <= dp and across * LANES <= columns:
-        down = dp // across
-        tall = -(-rows // (16 * down)) * 16
-        if best is None or down * tall < best[0] * best[2]:
-            best = (down, across, tall)
-        across *= 2
-    return best
-
-
-def to_pieces(shards, array, dp):
-    rows, columns = array.shape[1:]
-    down, across, tall = cut_of(rows, columns, dp)
-    array = jnp.pad(array, ((0, 0), (0, down * tall - rows), (0, 0)))
-    array = array.reshape(shards, down, tall, across, columns // across).transpose(0, 1, 3, 2, 4)
-    return array.reshape(shards, dp // 2, 2, tall, columns // across)
-
-
-def from_pieces(pieces, rows, columns, dp):
-    shards = pieces.shape[0]
-    down, across, tall = cut_of(rows, columns, dp)
-    array = pieces.reshape(shards, down, across, tall, columns // across).transpose(0, 1, 3, 2, 4)
-    return array.reshape(shards, down * tall, columns)[:, :rows]
-
-
-def own_piece(array, dp):
-    rows, columns = array.shape
-    down, across, tall = cut_of(rows, columns, dp)
-    array = jnp.pad(array, ((0, down * tall - rows), (0, 0)))
-    group = lax.axis_index("dp")
-    at = (group // across * tall, lax.rem(group, across) * (columns // across))
-    return lax.dynamic_slice(array, at, (tall, columns // across))
+        states, states, conv_input, slope, sel, *summed,
+    )
 
 
 def contract(left, right, left_dim, right_dim):
@@ -653,11 +764,10 @@
     vectors = jnp.concatenate(
         [channel_params, jnp.pad(norm_gain, (0, width - norm_gain.shape[0]))[None, :]], axis=0
     )
-    full_conv, full_small, full_vectors, full_gate, full_output = gather_pieces(
-        plan, [low_conv, low_small, own_piece(vectors, dp), low_gate, low_output], "gather_weights", 0
-    )
-    full_conv, full_gate = full_conv.reshape(-1, DI), full_gate.reshape(-1, DI)
-    full_output = full_output.reshape(DI, -1)
+    full_conv, full_small, full_vectors = gather_pieces(
+        plan, [low_conv, low_small, own_piece(vectors, dp)], "gather_weights", 0
+    )
+    full_conv = from_pieces(full_conv, norm_gain.shape[0], DI, dp).reshape(-1, DI)
     small_rows = R + 2 * N + R
     full_small = from_pieces(full_small, small_rows, width, dp).transpose(1, 0, 2).reshape(small_rows, DI)
     full_select, full_step = full_small[: R + 2 * N], full_small[R + 2 * N :]
@@ -668,7 +778,6 @@
     normed_value, norm_pull = jax.vjp(rms_scale, inputs, gain)
     normed = normed_value.astype(jnp.bfloat16)
     conv_input = jnp.dot(normed, full_conv, preferred_element_type=jnp.float32)
-    gate_half = jnp.dot(normed, full_gate, preferred_element_type=jnp.float32)
     conv_out = causal_conv(conv_input, channel[N : N + CONV], channel[N + CONV], offset)
     sigmoid = jax.nn.sigmoid(conv_out)
     mixed, conv_slope = lax.optimization_barrier(
@@ -685,7 +794,12 @@
         [selection[:, R:], jnp.stack(kept, axis=1), jnp.zeros((row_count, LANES - 2 * N - CONV), jnp.float32)], axis=1
     )
     skip = channel[N + CONV + 2][None, :]
-    state_out, step_size, states = scan_forward(step_in, mixed, chosen, rates_low)
+    state_out, step_size, states, full_gate, full_output = scan_forward(
+        step_in, mixed, chosen, rates_low, plan, [low_gate, low_output]
+    )
+    full_gate = from_pieces(full_gate, norm_gain.shape[0], DI, dp).reshape(-1, DI)
+    full_output = from_pieces(full_output, output_weight.shape[0], output_weight.shape[1], dp).reshape(DI, -1)
+    gate_half = jnp.dot(normed, full_gate, preferred_element_type=jnp.float32)
     scanned = state_out + skip * mixed_values
     gate_value, gate_pull = jax.vjp(jax.nn.silu, gate_half)
     gated = (scanned * gate_value).astype(jnp.bfloat16)
@@ -697,7 +811,10 @@
     grad_gated = contract(grad_branch, full_output, 1, 1)
     grad_scanned = grad_gated * gate_value
     (grad_gate,) = gate_pull(grad_gated * scanned)
-    grad_conv_input, grad_pre_low, grad_selection, grad_rows, sums = scan_backward(
+    grad_gate = grad_gate.astype(jnp.bfloat16)
+    grad_gate_weight = contract(normed, grad_gate, 0, 0).astype(jnp.bfloat16)
+    heights = [norm_gain.shape[0], output_weight.shape[0]]
+    grad_conv_input, grad_pre_low, grad_selection, grad_rows, sums, sum_output, sum_gate = scan_backward(
         step_in,
         step_size,
         mixed,
@@ -710,14 +827,15 @@
         full_step,
         full_select,
         states,
-    )
-    grad_gate = grad_gate.astype(jnp.bfloat16)
+        plan,
+        [
+            to_pieces(shards, grad_output.reshape(shards, heights[1], -1), dp),
+            to_pieces(shards, grad_gate_weight.reshape(shards, heights[0], -1), dp),
+        ],
+    )
     grad_step = contract(step_low, grad_pre_low, 0, 0)
     grad_select = contract(grad_selection, mixed, 0, 0)
-    grad_conv_weight, grad_gate_weight = (
-        contract(normed, half, 0, 0).astype(jnp.bfloat16)
-        for half in (grad_conv_input, grad_gate)
-    )
+    grad_conv_weight = contract(normed, grad_conv_input, 0, 0).astype(jnp.bfloat16)
     grad_normed = contract(grad_conv_input, full_conv, 1, 1) + contract(grad_gate, full_gate, 1, 1)
     grad_inputs, grad_gain = norm_pull(grad_normed)
     input_grad = (upstream + grad_inputs).astype(jnp.bfloat16)
@@ -728,12 +846,9 @@
     small = small.reshape(-1, shards, width).transpose(1, 0, 2)
     small_gain = jnp.pad(grad_gain.reshape(shards, 1, -1), ((0, 0), (0, 0), (0, width - grad_gain.shape[0] // shards)))
     small = jnp.concatenate([small, small_gain], axis=1).astype(jnp.bfloat16)
-    heights = [norm_gain.shape[0], output_weight.shape[0]]
-    sum_output, sum_gate, sum_conv, sum_small = reduce_pieces(
+    sum_conv, sum_small = reduce_pieces(
         plan,
         [
-            to_pieces(shards, grad_output.reshape(shards, heights[1], -1), dp),
-            to_pieces(shards, grad_gate_weight.reshape(shards, heights[0], -1), dp),
             to_pieces(shards, grad_conv_weight.reshape(shards, heights[0], -1), dp),
             to_pieces(shards, small, dp),
         ],

time: 536 us -> 464 us (0.87); the launches traced: 526 us -> 461 us
  Pallas kernels: 370 us -> 303 us
    pallas_call x1, Pallas kernels: 112 us -> 53.1 us  [reduce_pieces(): pl.pallas_call(functools.partial(reduce_kernel, plan, count), in_specs=[p...]
    pallas_call x1, Pallas kernels: 95.3 us -> 47.9 us  [gather_pieces(): pl.pallas_call(functools.partial(gather_kernel, plan, count), in_specs=[p...]
    pallas_call x2, Pallas kernels: 163 us -> 202 us  [the longest x1 129 us: scan_backward(): pl.pallas_call(functools.partial(backward_kernel, plan, len(summed)), gri...]
where the time goes in v4:
time: 464 us; the launch traced here: 461 us
  Pallas kernels  303 us (65%)
  matrix products  64.6 us (14%)
  other arithmetic  44.3 us (10%)
  local copies, waits for them, and re-layouts  23.5 us (5%)
  blocking collectives  15 us (3%)
  between operations  10.9 us (2%)
    pallas_call x1, Pallas kernels, scan_backward(): pl.pallas_call(functools.partial(backward_kernel, plan, len(summed)), gri...  129 us
    pallas_call x1, Pallas kernels, scan_forward(): pl.pallas_call(functools.partial(forward_kernel, plan, len(pieces)), grid...  73 us
    pallas_call x1, Pallas kernels, reduce_pieces(): pl.pallas_call(functools.partial(reduce_kernel, plan, count), in_specs=[p...  53.1 us
    pallas_call x1, Pallas kernels, gather_pieces(): pl.pallas_call(functools.partial(gather_kernel, plan, count), in_specs=[p...  47.9 us
    dot_general x9, matrix products, contract(): lax.dot_general(left, right, (((left_dim,), (right_dim,)), ((), ())), pre...  36.8 us
    add x6, other arithmetic, adam_direction(): first_hat / (jnp.sqrt(second_hat) + adam_eps) + decay_rate * decay * weight  15.4 us
    psum x1, blocking collectives, local(): total_square = lax.psum(local_square, 'fsdp')  15 us
    dot_general x1, matrix products, local(): gate_half = jnp.dot(normed, full_gate, preferred_element_type=jnp.float32)  11.8 us

profile of v4, /device:TPU:0, one launch (start us, length us, event | category | flops | bytes accessed | tf_op | source)
XLA Modules:
  0.0 460.8 jit_solution(11347544052815489826)
XLA Ops:
  0.7 3.6 fusion.80
  4.3 1.7 dynamic-slice_convert_fusion.1
  7.4 47.9 %gather_weights.1 = (bf16[4,4,2,32,2048]{4,3,2,1,0:T(8,128)(2,1)}, bf16[4,4,2,80,128]{4,3,2,1,0:T(8,128)(2,1)}, f32[4,4,2,16,128]{4,3,2,1,0:T(8,128)}) custom-call(bf16[32,2048]{1,0:T(8,128)(2,1)} %get-tuple-element.89.refs_0_, bf16[80,128]{1,0:T(8,128)(2,1)} %fusion.63.refs_1_, f32[16,128]{1,0:T(8,128)} %fusion.65.refs_2_), custom_call_target="tpu_custom_call" | custom-call | bytes 33554432 | tf_op jit(solution)/shard_map/gather_weights/pallas_call | solution.py:172
  55.3 1.4 copy.46
  61.7 5.8 %fusion.77.conv_ref = f32[768,2048]{1,0:T(8,128)S(1)} fusion(bf16[1024,2048]{1,0:T(8,128)(2,1)} %bitcast.146, bf16[768,1024]{1,0:T(8,128)(2,1)S(1)} %copy-done.7, f32[1024]{0:T(1024)S(1)} %bitcast.135, f32[768]{0:T(1024)S(1)} %fusion.69), kind=kOutput, calls=%fused_computation.163 | convolution fusion | flops 3224371200 | bytes 12065792 | tf_op jit(solution)/shard_map/dot_general | solution.py:780
  68.4 7.1 %add_multiply_fusion = (f32[768,2048]{1,0:T(8,128)}, f32[768,2048]{1,0:T(8,128)S(1)}) fusion(f32[768]{0:T(1024)S(1)} %get-tuple-element.94, f32[768,2048]{1,0:T(8,128)S(1)} %fusion.77.conv_ref, f32[2048]{0:T(1024)S(1)} %bitcast.130, f32[768]{0:T(1024)S(1)} %get-tuple-element.95, f32[2048]{0:T(1024)S(1)} %bitcast.131, f32[768]{0:T(1024)S(1)} %compare_convert_fusion.6, ...), kind=kLoop, calls=%fused_computation.21 | loop fusion | flops 28311552 | bytes 18924544 | tf_op jit(solution)/shard_map/mul | solution.py:784
  75.4 1.7 multiply_convert_fusion.1.mixed_ref
  79.6 3.6 convolution_add_fusion.v_ref
  84.1 1.7 compare_convert_fusion.2
  85.8 1.7 compare_convert_fusion
  88.3 2.1 concatenate.25.sel.flags
  90.4 1.8 fusion.54
  92.2 1.6 mul.485.rates
  96.6 73.0 %scan_forward.1 = (f32[768,2048]{1,0:T(8,128)}, f32[768,2048]{1,0:T(8,128)}, f32[768,16,16,128]{3,2,1,0:T(8,128)}, bf16[4,4,2,32,2048]{4,3,2,1,0:T(8,128)(2,1)}, bf16[4,4,2,64,1024]{4,3,2,1,0:T(8,128)(2,1)}) custom-call(f32[768,2048]{1,0:T(8,128)} %convolution_add_fusion.v_ref, bf16[768,2048]{1,0:T(8,128)(2,1)S(1)} %multiply_convert_fusion.1.mixed_ref, ...), custom_call_target="tpu_custom_call" | custom-call | flops 150994944 | bytes 100663296 | tf_op jit(solution)/shard_map/scan_forward/pallas_call | solution.py:609
  170.3 5.9 %fusion.38 = f32[768,2048]{1,0:T(8,128)S(1)} fusion(bf16[2048,1024]{1,0:T(8,128)(2,1)} %bitcast.150, bf16[768,1024]{1,0:T(8,128)(2,1)} %param.23, f32[768]{0:T(1024)S(1)} %fusion.68), kind=kOutput, calls=%fused_computation.71 | convolution fusion | flops 3223584768 | bytes 12061696 | tf_op jit(solution)/shard_map/dot_general | solution.py:710
  176.3 11.8 %fusion.11 = (bf16[768,2048]{1,0:T(8,128)(2,1)}, bf16[768,2048]{1,0:T(8,128)(2,1)}, f32[768,2048]{1,0:T(8,128)}) fusion(f32[768,2048]{1,0:T(8,128)S(1)} %fusion.38, f32[768,2048]{1,0:T(8,128)} %get-tuple-element.38, bf16[768,2048]{1,0:T(8,128)(2,1)S(1)} %multiply_convert_fusion.1.mixed_ref, f32[2048]{0:T(1024)S(1)} %bitcast.141, ...), kind=kOutput, calls=%fused_computation.15 | convolution fusion | flops 3252682752 | bytes 34094080 | tf_op jit(solution)/shard_map/dot_general | solution.py:802
  188.1 6.6 %fusion.26 = bf16[768,1024]{1,0:T(8,128)(2,1)} fusion(bf16[768,1024]{1,0:T(8,128)(2,1)S(1)} %copy-done.8, bf16[768,2048]{1,0:T(8,128)(2,1)} %get-tuple-element.68, bf16[2048,1024]{1,0:T(8,128)(2,1)S(1)} %bitcast.151, f32[768]{0:T(1024)S(1)} %fusion.68), kind=kOutput, calls=%fused_computation.50 | convolution fusion | flops 3224371200 | bytes 10488832 | tf_op jit(solution)/shard_map/dot_general | solution.py:806
  196.1 5.2 %convolution_convert_fusion.2 = bf16[2048,1024]{1,0:T(8,128)(2,1)} fusion(bf16[768,2048]{1,0:T(8,128)(2,1)S(1)} %copy-done.54, bf16[768,1024]{1,0:T(8,128)(2,1)S(1)} %copy-done.20, f32[768]{0:T(1024)S(1)} %fusion.68), kind=kOutput, calls=%fused_computation.42 | convolution fusion | flops 3225681920 | bytes 8915968 | tf_op jit(solution)/shard_map/dot_general | solution.py:710
  201.4 5.4 %convolution_convert_fusion.1 = bf16[1024,2048]{1,0:T(8,128)(2,1)} fusion(bf16[768,2048]{1,0:T(8,128)(2,1)S(1)} %copy-done.52, bf16[768,1024]{1,0:T(8,128)(2,1)S(1)} %copy-done.8, f32[1024]{0:T(1024)S(1)} %bitcast.137, f32[768]{0:T(1024)S(1)} %fusion.69), kind=kOutput, calls=%fused_computation.41 | convolution fusion | flops 3226468352 | bytes 8920064 | tf_op jit(solution)/shard_map/dot_general | solution.py:710
  206.8 128.7 %scan_backward.1 = (bf16[768,2048]{1,0:T(8,128)(2,1)}, bf16[768,2048]{1,0:T(8,128)(2,1)}, bf16[768,96]{1,0:T(8,128)(2,1)}, f32[8,8,2048]{2,1,0:T(8,128)}, f32[16...) custom-call(f32[768,2048]{1,0:T(8,128)} %convolution_add_fusion.v_ref, ...), custom_call_target="tpu_custom_call" | custom-call | flops 503316480 | bytes 100663296 | tf_op jit(solution)/shard_map/scan_backward/pallas_call | solution.py:657
  335.5 6.6 %fusion.83 = f32[768,1024]{1,0:T(8,128)S(1)} fusion(bf16[768,2048]{1,0:T(8,128)(2,1)} %get-tuple-element.44, bf16[1024,2048]{1,0:T(8,128)(2,1)} %bitcast.147), kind=kOutput, calls=%fused_computation.167 | convolution fusion | flops 3221225472 | bytes 10485760 | tf_op jit(solution)/shard_map/dot_general | solution.py:710
  342.1 4.0 fusion.22
  346.2 2.1 fusion.24
  348.3 5.3 %convolution_convert_fusion = bf16[1024,2048]{1,0:T(8,128)(2,1)} fusion(bf16[768,2048]{1,0:T(8,128)(2,1)S(1)} %copy-done.48, bf16[768,1024]{1,0:T(8,128)(2,1)S(1)} %copy-done.9, f32[1024]{0:T(1024)S(1)} %bitcast.140, f32[768]{0:T(1024)S(1)} %fusion.69), kind=kOutput, calls=%fused_computation.40 | convolution fusion | flops 3226468352 | bytes 8920064 | tf_op jit(solution)/shard_map/dot_general | solution.py:710
  353.7 1.3 slice_reduce_fusion
  356.9 2.6 convolution_convert_fusion.4
  361.3 2.2 copy-done.2
  363.5 53.1 %sum_gradients.1 = (bf16[4,2,32,2048]{3,2,1,0:T(8,128)(2,1)S(1)}, bf16[4,2,48,256]{3,2,1,0:T(8,128)(2,1)S(1)}) custom-call(bf16[4,4,2,32,2048]{4,3,2,1,0:T(8,128)(2,1)S(1)} %bitcast.107, bf16[4,4,2,48,256]{4,3,2,1,0:T(8,128)(2,1)S(1)} %bitcast.108), custom_call_target="tpu_custom_call" | custom-call | bytes 33554432 | tf_op jit(solution)/shard_map/sum_gradients/pallas_call | solution.py:334
  417.6 3.6 multiply_reduce_fusion
  428.2 15.0 %psum.7 = f32[]{:T(128)} all-reduce(f32[]{:T(128)S(6)} %add.251), channel_id=1, replica_groups=mesh['dp'=8,'fsdp'=4] {'fsdp'}, use_global_device_ids=true, to_apply=%region_10.11 | all-reduce | flops 1 | bytes 8 | tf_op jit(solution)/shard_map/psum | solution.py:872
  444.6 8.8 %fusion.18 = f32[256,4096]{1,0:T(8,128)} fusion(f32[256,4096]{1,0:T(8,128)} %param.25, f32[256,4096]{1,0:T(8,128)} %param.37, f32[256,4096]{1,0:T(8,128)} %get-tuple-element.64, f32[256,4096]{1,0:T(8,128)} %param.31, f32[]{:T(128)S(6)} %min.3), kind=kLoop, calls=%fused_computation.35 | loop fusion | flops 14680064 | bytes 20971524 | tf_op jit(solution)/shard_map/add | solution.py:726
  455.8 3.7 fusion.33
  (170 shorter events, 23.4 us)
Async XLA Ops:
  4.3 53.1 %copy-start.42 = (s32[1,4]{1,0:T(1,128)S(1)}, s32[1,4]{1,0:T(1,128)}, u32[]{:S(2)}) copy-start(s32[1,4]{1,0:T(1,128)} %param.22) | copy-start | bytes 52
  4.3 57.0 %copy-start.7 = (bf16[768,1024]{1,0:T(8,128)(2,1)S(1)}, bf16[768,1024]{1,0:T(8,128)(2,1)}, u32[]{:S(2)}) copy-start(bf16[768,1024]{1,0:T(8,128)(2,1)} %param.21) | copy-start | bytes 4718596
  56.9 10.7 %copy-start.14 = (bf16[4,160,512]{2,0,1:T(4,128)(2,1)}, bf16[4,160,512]{2,0,1:T(4,128)(2,1)S(1)}, u32[]{:S(2)}) copy-start(bf16[4,160,512]{2,0,1:T(4,128)(2,1)S(1)} %reshape.224) | copy-start | bytes 1966084
  57.1 22.5 %copy-start.17 = (bf16[8,8,4,512]{3,1,2,0:T(8,128)(2,1)}, bf16[8,8,4,512]{3,1,2,0:T(8,128)(2,1)S(1)}, u32[]{:S(2)}) copy-start(bf16[8,8,4,512]{3,1,2,0:T(8,128)(2,1)S(1)} %copy.61) | copy-start | bytes 786436
  57.4 10.2 %copy-start.22 = (f32[23,4,512]{2,1,0:T(4,128)}, f32[23,4,512]{2,1,0:T(4,128)S(1)}, u32[]{:S(2)}) copy-start(f32[23,4,512]{2,1,0:T(4,128)S(1)} %slice_bitcast_fusion.1) | copy-start | bytes 565252
  77.2 99.1 %copy-start = (bf16[768,2048]{1,0:T(8,128)(2,1)}, bf16[768,2048]{1,0:T(8,128)(2,1)S(1)}, u32[]{:S(2)}) copy-start(bf16[768,2048]{1,0:T(8,128)(2,1)S(1)} %multiply_convert_fusion.1.mixed_ref) | copy-start | bytes 9437188
  90.4 79.2 %copy-start.3 = (f32[768,128]{1,0:T(8,128)}, f32[768,128]{1,0:T(8,128)S(1)}, u32[]{:S(2)}) copy-start(f32[768,128]{1,0:T(8,128)S(1)} %concatenate.25.sel.flags) | copy-start | bytes 1179652
  176.3 11.8 %copy-start.51 = (bf16[4,4,2,64,1024]{4,3,2,1,0:T(8,128)(2,1)S(1)}, bf16[4,4,2,64,1024]{4,3,2,1,0:T(8,128)(2,1)}, u32[]{:S(2)}) copy-start(bf16[4,4,2,64,1024]{4,3,2,1,0:T(8,128)(2,1)} %get-tuple-element.40) | copy-start | bytes 12582916
  188.0 8.1 %copy-start.20 = (bf16[768,1024]{1,0:T(8,128)(2,1)S(1)}, bf16[768,1024]{1,0:T(8,128)(2,1)}, u32[]{:S(2)}) copy-start(bf16[768,1024]{1,0:T(8,128)(2,1)} %param.23) | copy-start | bytes 4718596
  188.0 8.1 %copy-start.54 = (bf16[768,2048]{1,0:T(8,128)(2,1)S(1)}, bf16[768,2048]{1,0:T(8,128)(2,1)}, u32[]{:S(2)}) copy-start(bf16[768,2048]{1,0:T(8,128)(2,1)} %get-tuple-element.68) | copy-start | bytes 9437188
  348.3 8.6 %copy-start.13 = (f32[768,96]{0,1:T(8,128)S(1)}, f32[768,96]{0,1:T(8,128)}, u32[]{:S(2)}) copy-start(f32[768,96]{0,1:T(8,128)} %copy-done.12) | copy-start | bytes 884740
  363.5 54.1 %copy-start.21 = (bf16[4,2,32,2048]{3,2,1,0:T(8,128)(2,1)S(1)}, bf16[4,2,32,2048]{3,2,1,0:T(8,128)(2,1)}, u32[]{:S(2)}) copy-start(bf16[4,2,32,2048]{3,2,1,0:T(8,128)(2,1)} %get-tuple-element.51) | copy-start | bytes 3145732
  416.9 26.9 %copy-start.45 = (f32[1,256]{1,0:T(1,128)}, f32[1,256]{1,0:T(1,128)S(1)}, u32[]{:S(2)}) copy-start(f32[1,256]{1,0:T(1,128)S(1)} %slice.182) | copy-start | bytes 3076
  417.5 8.8 %copy-start.10 = (bf16[4,2,64,1024]{3,2,1,0:T(8,128)(2,1)S(1)}, bf16[4,2,64,1024]{3,2,1,0:T(8,128)(2,1)}, u32[]{:S(2)}) copy-start(bf16[4,2,64,1024]{3,2,1,0:T(8,128)(2,1)} %get-tuple-element.52) | copy-start | bytes 3145732
  417.5 26.3 %copy-start.44 = (f32[256]{0:T(256)S(1)}, f32[256]{0:T(256)}, u32[]{:S(2)}) copy-start(f32[256]{0:T(256)} %param.24) | copy-start | bytes 3076
  417.5 26.3 %copy-start.46 = (f32[256]{0:T(256)S(1)}, f32[256]{0:T(256)}, u32[]{:S(2)}) copy-start(f32[256]{0:T(256)} %param.36) | copy-start | bytes 3076
  417.5 26.3 %copy-start.47 = (f32[256]{0:T(256)S(1)}, f32[256]{0:T(256)}, u32[]{:S(2)}) copy-start(f32[256]{0:T(256)} %param.30) | copy-start | bytes 3076
  423.1 30.3 %copy-start.23 = (f32[96,512]{1,0:T(8,128)}, f32[96,512]{1,0:T(8,128)S(1)}, u32[]{:S(2)}) copy-start(f32[96,512]{1,0:T(8,128)S(1)} %get-tuple-element.62) | copy-start | bytes 589828
  424.4 29.9 %copy-start.28 = (f32[64,512]{1,0:T(8,128)}, f32[64,512]{1,0:T(8,128)S(1)}, u32[]{:S(2)}) copy-start(f32[64,512]{1,0:T(8,128)S(1)} %get-tuple-element.60) | copy-start | bytes 393220
  425.7 29.4 %copy-start.33 = (f32[23,512]{1,0:T(8,128)}, f32[23,512]{1,0:T(8,128)S(1)}, u32[]{:S(2)}) copy-start(f32[23,512]{1,0:T(8,128)S(1)} %get-tuple-element.58) | copy-start | bytes 141316
  444.5 8.9 %copy-start.25 = (f32[96,512]{1,0:T(8,128)S(1)}, f32[96,512]{1,0:T(8,128)}, u32[]{:S(2)}) copy-start(f32[96,512]{1,0:T(8,128)} %param.26) | copy-start | bytes 589828
  444.5 9.0 %copy-start.31 = (f32[96,512]{1,0:T(8,128)S(1)}, f32[96,512]{1,0:T(8,128)}, u32[]{:S(2)}) copy-start(f32[96,512]{1,0:T(8,128)} %param.38) | copy-start | bytes 589828
  444.5 9.0 %copy-start.32 = (f32[96,512]{1,0:T(8,128)S(1)}, f32[96,512]{1,0:T(8,128)}, u32[]{:S(2)}) copy-start(f32[96,512]{1,0:T(8,128)} %param.32) | copy-start | bytes 589828
  444.5 9.8 %copy-start.27 = (f32[64,512]{1,0:T(8,128)S(1)}, f32[64,512]{1,0:T(8,128)}, u32[]{:S(2)}) copy-start(f32[64,512]{1,0:T(8,128)} %param.27) | copy-start | bytes 393220
  444.5 9.8 %copy-start.36 = (f32[64,512]{1,0:T(8,128)S(1)}, f32[64,512]{1,0:T(8,128)}, u32[]{:S(2)}) copy-start(f32[64,512]{1,0:T(8,128)} %param.39) | copy-start | bytes 393220
  444.5 9.8 %copy-start.37 = (f32[64,512]{1,0:T(8,128)S(1)}, f32[64,512]{1,0:T(8,128)}, u32[]{:S(2)}) copy-start(f32[64,512]{1,0:T(8,128)} %param.33) | copy-start | bytes 393220
  444.5 10.6 %copy-start.35 = (f32[23,512]{1,0:T(8,128)S(1)}, f32[23,512]{1,0:T(8,128)}, u32[]{:S(2)}) copy-start(f32[23,512]{1,0:T(8,128)} %param.28) | copy-start | bytes 141316
  444.5 10.6 %copy-start.38 = (f32[23,512]{1,0:T(8,128)S(1)}, f32[23,512]{1,0:T(8,128)}, u32[]{:S(2)}) copy-start(f32[23,512]{1,0:T(8,128)} %param.40) | copy-start | bytes 141316
  444.5 10.5 %copy-start.39 = (f32[23,512]{1,0:T(8,128)S(1)}, f32[23,512]{1,0:T(8,128)}, u32[]{:S(2)}) copy-start(f32[23,512]{1,0:T(8,128)} %param.34) | copy-start | bytes 141316
  444.5 11.2 %copy-start.16 = (f32[512,1024]{1,0:T(8,128)S(1)}, f32[512,1024]{1,0:T(8,128)}, u32[]{:S(2)}) copy-start(f32[512,1024]{1,0:T(8,128)} %param.29) | copy-start | bytes 6291460
  444.6 11.2 %copy-start.18 = (f32[512,1024]{1,0:T(8,128)S(1)}, f32[512,1024]{1,0:T(8,128)}, u32[]{:S(2)}) copy-start(f32[512,1024]{1,0:T(8,128)} %param.41) | copy-start | bytes 6291460
  444.6 11.2 %copy-start.19 = (f32[512,1024]{1,0:T(8,128)S(1)}, f32[512,1024]{1,0:T(8,128)}, u32[]{:S(2)}) copy-start(f32[512,1024]{1,0:T(8,128)} %param.35) | copy-start | bytes 6291460
  (23 other events, 103.5 us)

commit v5 on v4

--- a/solution.py
+++ b/solution.py
@@ -18,6 +18,8 @@
 BLOCK = 64
 GROUP = 8
 BACK = 4
+GATHER_CUTS = (2, 2)
+REDUCE_CUTS = (2, 2)
 WIDE = 512
 TAIL = 2
 
@@ -32,14 +34,14 @@
 
 
 def block_layout(lengths_row, count):
-    places = jnp.arange(count, dtype=jnp.int32)
-    begun = jnp.zeros((count,), jnp.int32)
+    places = lax.broadcasted_iota(jnp.int32, (count, LANES), 0)
+    begun = jnp.zeros((count, LANES), jnp.int32)
     end = jnp.zeros((), jnp.int32)
     for cluster in range(lengths_row.shape[0]):
         begun = jnp.where(end <= places, jnp.maximum(begun, end), begun)
         end = end + lengths_row[cluster]
-    live_mask = (places < end).astype(jnp.float32)
-    return live_mask, places - begun
+    return (places[:, :1] < end).astype(jnp.float32), places - begun
+
 
 def rms_scale(values, scales):
     return (
@@ -53,7 +55,7 @@
     total = shift[None, :] + kernel[CONV - 1][None, :] * values
     for distance in range(1, CONV):
         moved = jnp.pad(values, ((distance, 0), (0, 0)))[:-distance]
-        keep = (offset >= distance).astype(jnp.float32)[:, None]
+        keep = (offset[:, :1] >= distance).astype(jnp.float32)
         total = total + kernel[CONV - 1 - distance][None, :] * moved * keep
     return total
 
@@ -91,11 +93,28 @@
     pl.semaphore_wait(barrier, len(everyone))
 
 
+def chunks(arrays, cuts):
+    made = []
+    for i, (array, cut) in enumerate(zip(arrays, cuts)):
+        width = array.shape[-1] // cut
+        made += [(i, pl.ds(k * width, width)) for k in range(cut)]
+    return made
+
+
 class Gather:
-    def __init__(self, plan, own, full, near, far, wide, cross):
-        self.plan, self.own, self.full = plan, own, full
+    def __init__(self, plan, cuts, own, full, near, far, wide, cross):
+        self.plan, self.all_own, self.all_full = plan, own, full
         self.near, self.far, self.wide, self.cross = near, far, wide, cross
-        self.count = len(own)
+        self.chunks = chunks(own, cuts)
+        self.count = len(self.chunks)
+
+    def own(self, s):
+        i, columns = self.chunks[s]
+        return self.all_own[i].at[:, columns]
+
+    def full(self, s, *at):
+        i, columns = self.chunks[s]
+        return self.all_full[i].at[(*at, slice(None), columns)]
 
     @staticmethod
     def scratch(plan, count):
@@ -103,7 +122,7 @@
         return [
             pltpu.SemaphoreType.DMA((count,)),
             pltpu.SemaphoreType.DMA((2, count * (shards - 1))),
-            pltpu.SemaphoreType.DMA((2, count * (places - 1))),
+            pltpu.SemaphoreType.DMA((2, count * places)),
             pltpu.SemaphoreType.DMA((2, count)),
         ]
 
@@ -113,27 +132,38 @@
 
     def keep(self, s):
         mine, place, side = placed(self.plan)
-        return pltpu.make_async_copy(self.own[s], self.full[s].at[mine, place, side], self.near.at[s])
+        return pltpu.make_async_copy(self.own(s), self.full(s, mine, place, side), self.near.at[s])
 
     def along(self, s):
         mine, place, side = placed(self.plan)
         return [
-            mesh_copy(
-                self.own[s], self.full[s].at[mine, place, side], self.far, s * (self.plan[0] - 1) + k, device
-            )
+            mesh_copy(self.own(s), self.full(s, mine, place, side), self.far, s * (self.plan[0] - 1) + k, device)
             for k, device in enumerate(peers_of(self.plan)[0])
         ]
 
     def plane(self, s):
         _, place, side = placed(self.plan)
-        part = self.full[s].at[:, place, side]
+        part = self.full(s, slice(None), place, side)
+        devices = peers_of(self.plan)[1]
         return [
-            mesh_copy(part, part, self.wide, s * (self.plan[1] - 1) + k, device)
-            for k, device in enumerate(peers_of(self.plan)[1])
-        ]
+            mesh_copy(part, part, self.wide, s * self.plan[1] + k, device)
+            for k, device in enumerate(devices[:2] if self.plan[1] == 4 else devices)
+        ]
+
+    def relay(self, s):
+        if self.plan[1] != 4:
+            return []
+        _, place, side = placed(self.plan)
+        devices = peers_of(self.plan)[1]
+        half = self.plan[0] // 2
+        made = []
+        for k, rows in enumerate((pl.ds(0, half), pl.ds(half, self.plan[0] - half))):
+            part = self.full(s, rows, place ^ (k + 1), side)
+            made.append(mesh_copy(part, part, self.wide, s * 4 + 2 + k, devices[1 - k]))
+        return made
 
     def pair(self, s):
-        part = self.full[s].at[:, :, placed(self.plan)[2]]
+        part = self.full(s, slice(None), slice(None), placed(self.plan)[2])
         return mesh_copy(part, part, self.cross, s, peers_of(self.plan)[2])
 
     def start(self, s):
@@ -148,33 +178,43 @@
         for copy in self.plane(s):
             copy.start()
 
-    def share(self, s):
+    def pass_on(self, s):
         for copy in self.plane(s):
             copy.wait_recv()
+        for copy in self.relay(s):
+            copy.start()
+
+    def share(self, s):
+        for copy in self.relay(s):
+            copy.wait_recv()
         self.pair(s).start()
 
     def end(self, s):
-        for copy in self.along(s) + self.plane(s):
+        for copy in self.along(s) + self.plane(s) + self.relay(s):
             copy.wait_send()
         self.pair(s).wait()
 
 
-def gather_kernel(plan, count, *refs):
-    gather = Gather(plan, refs[:count], refs[count : 2 * count], *refs[2 * count :])
+def gather_kernel(plan, cuts, count, *refs):
+    gather = Gather(plan, cuts, refs[:count], refs[count : 2 * count], *refs[2 * count :])
     greet(plan)
-    for stage in (gather.start, gather.spread, gather.share, gather.end):
-        for s in range(count):
-            stage(s)
-
-
-def gather_pieces(plan, pieces, name, collective_id):
+    ahead = 2
+    for s in range(gather.count + 4):
+        for stage, wait in ((gather.start, 0), (gather.spread, ahead), (gather.pass_on, 3), (gather.share, 4)):
+            if 0 <= s - wait < gather.count:
+                stage(s - wait)
+    for s in range(gather.count):
+        gather.end(s)
+
+
+def gather_pieces(plan, pieces, cuts, name, collective_id):
     count = len(pieces)
     return pl.pallas_call(
-        functools.partial(gather_kernel, plan, count),
+        functools.partial(gather_kernel, plan, cuts, count),
         in_specs=[pl.BlockSpec(memory_space=pl.ANY)] * count,
         out_specs=[pl.BlockSpec(memory_space=pl.ANY)] * count,
         out_shape=Gather.shapes(plan, pieces),
-        scratch_shapes=Gather.scratch(plan, count),
+        scratch_shapes=Gather.scratch(plan, sum(cuts)),
         compiler_params=pltpu.CompilerParams(collective_id=collective_id, has_side_effects=True),
         cost_estimate=pl.CostEstimate(flops=0, bytes_accessed=32 << 20, transcendentals=0),
         name=name,
@@ -189,20 +229,31 @@
 
 
 class Reduce:
-    def __init__(self, plan, parts, full, scratch):
-        count = len(parts)
-        self.plan, self.parts, self.full, self.count = plan, parts, full, count
+    def __init__(self, plan, cuts, parts, full, squares, scratch):
+        count = sum(cuts)
+        self.squares = squares
+        self.plan, self.all_parts, self.all_full, self.count = plan, parts, full, count
+        self.chunks = chunks(parts, cuts)
         self.held, self.from_pair, self.from_plane, self.from_along, self.piece = (
             scratch[k * count : (k + 1) * count] for k in range(5)
         )
         self.near, self.cross, self.wide, self.far, self.back, self.over = scratch[5 * count :]
 
+    def parts(self, s, *at):
+        i, columns = self.chunks[s]
+        return self.all_parts[i].at[(*at, slice(None), columns)]
+
+    def full(self, s, *at):
+        i, columns = self.chunks[s]
+        return self.all_full[i].at[(*at, slice(None), columns)]
+
     @staticmethod
-    def scratch(plan, parts):
+    def scratch(plan, cuts, parts):
         shards, places = plan
-        count = len(parts)
+        count = sum(cuts)
+        tails = [(part.shape[3], part.shape[4] // cut) for part, cut in zip(parts, cuts) for _ in range(cut)]
         leads = [(shards, places), (shards, places), (places - 1, shards), (shards - 1,), ()]
-        return [pltpu.VMEM(lead + part.shape[3:], jnp.bfloat16) for lead in leads for part in parts] + [
+        return [pltpu.VMEM(lead + tail, jnp.bfloat16) for lead in leads for tail in tails] + [
             pltpu.SemaphoreType.DMA((2, count)),
             pltpu.SemaphoreType.DMA((2, count)),
             pltpu.SemaphoreType.DMA((2, count * (places - 1))),
@@ -217,12 +268,12 @@
 
     def keep(self, s):
         side = placed(self.plan)[2]
-        return pltpu.make_async_copy(self.parts[s].at[:, :, side], self.held[s], self.near.at[0, s])
+        return pltpu.make_async_copy(self.parts(s, slice(None), slice(None), side), self.held[s], self.near.at[0, s])
 
     def pair(self, s):
         side = placed(self.plan)[2]
         return mesh_copy(
-            self.parts[s].at[:, :, 1 - side], self.from_pair[s], self.cross, s, peers_of(self.plan)[2]
+            self.parts(s, slice(None), slice(None), 1 - side), self.from_pair[s], self.cross, s, peers_of(self.plan)[2]
         )
 
     def plane(self, s):
@@ -254,17 +305,17 @@
 
     def put(self, s):
         _, place, side = placed(self.plan)
-        return pltpu.make_async_copy(self.piece[s], self.full[s].at[place, side], self.near.at[1, s])
+        return pltpu.make_async_copy(self.piece[s], self.full(s, place, side), self.near.at[1, s])
 
     def home(self, s):
         _, place, side = placed(self.plan)
         return [
-            mesh_copy(self.piece[s], self.full[s].at[place, side], self.back, s * (self.plan[1] - 1) + k, device)
+            mesh_copy(self.piece[s], self.full(s, place, side), self.back, s * (self.plan[1] - 1) + k, device)
             for k, device in enumerate(peers_of(self.plan)[1])
         ]
 
     def other(self, s):
-        part = self.full[s].at[:, placed(self.plan)[2]]
+        part = self.full(s, slice(None), placed(self.plan)[2])
         return mesh_copy(part, part, self.over, s, peers_of(self.plan)[2])
 
     def start(self, s):
@@ -302,7 +353,12 @@
         for copy in self.along(s):
             copy.wait_recv()
         others = self.from_along[s]
-        self.piece[s][...] = wide_sum([self.held[s][mine, place]] + [others[k] for k in range(self.plan[0] - 1)])
+        piece = wide_sum([self.held[s][mine, place]] + [others[k] for k in range(self.plan[0] - 1)])
+        self.piece[s][...] = piece
+        square = piece.astype(jnp.float32) * piece.astype(jnp.float32)
+        square = jnp.sum(square.reshape(-1, 8, square.shape[1]), axis=0)
+        for first in range(0, square.shape[1], LANES):
+            self.squares[...] += square[:, first : first + LANES]
         self.put(s).start()
         for copy in self.home(s):
             copy.start()
@@ -320,29 +376,80 @@
         self.other(s).wait()
 
 
-def reduce_kernel(plan, count, *refs):
-    reduce = Reduce(plan, refs[:count], refs[count : 2 * count], refs[2 * count :])
+class Total:
+    def __init__(self, plan, value, scratch):
+        self.plan, self.value = plan, value
+        self.slots, self.sent, self.sems = scratch[:3], scratch[3], scratch[4:]
+
+    @staticmethod
+    def scratch(plan):
+        sizes = (plan[0], plan[1], 2)
+        return (
+            [pltpu.VMEM((size, 8, LANES), jnp.float32) for size in sizes]
+            + [pltpu.VMEM((3, 8, LANES), jnp.float32)]
+            + [pltpu.SemaphoreType.DMA((2, size - 1)) for size in sizes]
+        )
+
+    def copies(self, level):
+        along, plane, pair = peers_of(self.plan)
+        at = placed(self.plan)[level]
+        return [
+            mesh_copy(self.sent.at[level], self.slots[level].at[at], self.sems[level], k, device)
+            for k, device in enumerate((along, plane, [pair])[level])
+        ]
+
+    def start(self, level):
+        self.sent[level] = self.value[...]
+        self.slots[level][placed(self.plan)[level]] = self.value[...]
+        for copy in self.copies(level):
+            copy.start()
+
+    def end(self, level):
+        for copy in self.copies(level):
+            copy.wait()
+        total = self.slots[level][0]
+        for k in range(1, self.slots[level].shape[0]):
+            total = total + self.slots[level][k]
+        self.value[...] = total
+
+
+def reduce_kernel(plan, cuts, count, *refs):
+    given, refs = refs[:count], refs[count:]
+    before, refs = refs[0], refs[1:]
+    full, squares, refs = refs[:count], refs[count], refs[count + 1 :]
+    reduce = Reduce(plan, cuts, given, full, squares, refs[:-7])
+    total = Total(plan, squares, refs[-7:])
+    squares[...] = before[...]
     greet(plan)
-    stages = (reduce.start, reduce.sum_pair, reduce.sum_plane, reduce.sum_along, reduce.share, reduce.end)
-    for stage in stages:
-        for s in range(count):
+    for stage in (reduce.start, reduce.sum_pair, reduce.sum_plane, reduce.sum_along):
+        for s in range(reduce.count):
             stage(s)
-
-
-def reduce_pieces(plan, parts, name, collective_id):
+    total.start(0)
+    total.end(0)
+    total.start(1)
+    for s in range(reduce.count):
+        reduce.share(s)
+    total.end(1)
+    total.start(2)
+    for s in range(reduce.count):
+        reduce.end(s)
+    total.end(2)
+
+
+def reduce_pieces(plan, parts, squares, cuts, name, collective_id):
     count = len(parts)
     return pl.pallas_call(
-        functools.partial(reduce_kernel, plan, count),
-        in_specs=[pl.BlockSpec(memory_space=pl.ANY)] * count,
-        out_specs=[pl.BlockSpec(memory_space=pl.ANY)] * count,
-        out_shape=Reduce.shapes(plan, parts),
-        scratch_shapes=Reduce.scratch(plan, parts),
+        functools.partial(reduce_kernel, plan, cuts, count),
+        in_specs=[pl.BlockSpec(memory_space=pl.ANY)] * count + [pl.BlockSpec(memory_space=pltpu.VMEM)],
+        out_specs=[pl.BlockSpec(memory_space=pl.ANY)] * count + [pl.BlockSpec(memory_space=pltpu.VMEM)],
+        out_shape=Reduce.shapes(plan, parts) + [jax.ShapeDtypeStruct((8, LANES), jnp.float32)],
+        scratch_shapes=Reduce.scratch(plan, cuts, parts) + Total.scratch(plan),
         compiler_params=pltpu.CompilerParams(
             collective_id=collective_id, has_side_effects=True, vmem_limit_bytes=48 << 20
         ),
         cost_estimate=pl.CostEstimate(flops=0, bytes_accessed=32 << 20, transcendentals=0),
         name=name,
-    )(*parts)
+    )(*parts, squares)
 
 
 def at_steps(stages, count, steps):
@@ -378,12 +485,12 @@
     return array.reshape(shards, down * tall, columns)[:, :rows]
 
 
-def own_piece(array, dp):
-    rows, columns = array.shape
-    down, across, tall = cut_of(rows, columns, dp)
-    array = jnp.pad(array, ((0, down * tall - rows), (0, 0)))
+def own_piece(array, dp, first=0, columns=None):
+    columns = columns or array.shape[1]
+    down, across, tall = cut_of(array.shape[0], columns, dp)
+    array = jnp.pad(array, ((0, down * tall - array.shape[0]), (0, 0)))
     group = lax.axis_index("dp")
-    at = (group // across * tall, lax.rem(group, across) * (columns // across))
+    at = (group // across * tall, first + lax.rem(group, across) * (columns // across))
     return lax.dynamic_slice(array, at, (tall, columns // across))
 
 
@@ -396,6 +503,11 @@
     rows = pl.multiple_of(g * 8, 8)
     for col in range(COLS):
         out[pl.ds(rows, 8), LANES * col : LANES * (col + 1)] = ref[pl.ds(g * 8 * COLS + col, 8, stride=COLS), :]
+
+
+def lay_rates(ref, rates):
+    for col in range(COLS):
+        ref[pl.ds(col, N, stride=COLS), :] = rates[:, LANES * col : LANES * (col + 1)]
 
 
 def token_rows(g, token):
@@ -424,15 +536,20 @@
 def forward_kernel(plan, count, v_ref, mixed_ref, sel, rates, *refs):
     own, refs = refs[:count], refs[count:]
     (y_ref, dt_ref, hs_ref), full, refs = refs[:3], refs[3 : 3 + count], refs[3 + count :]
-    state, dts, us, bb, ys = refs[:5]
-    gather = Gather(plan, own, full, *refs[5:])
+    state, laid, dts, us, bb, ys = refs[:6]
+    gather = Gather(plan, GATHER_CUTS, own, full, *refs[6:])
 
     @pl.when(pl.program_id(0) == 0)
     def _():
         state[...] = jnp.zeros_like(state)
+        lay_rates(laid, rates)
         greet(plan)
 
-    at_steps((gather.start, gather.spread, gather.share), count, ((0, 0), (3, 6), (8, 11)))
+    at_steps(
+        (gather.start, gather.spread, gather.pass_on, gather.share),
+        gather.count,
+        ((0, 0, 1, 2), (2, 3, 5, 6), (4, 5, 7, 9), (5, 7, 9, 11)),
+    )
 
     @pl.loop(0, BLOCK // 8)
     def _(g):
@@ -449,11 +566,12 @@
 
     for low in range(0, N, GROUP):
         part = pl.ds(low, GROUP)
+        laid_part = pl.ds(low * COLS, GROUP * COLS)
 
         def steps(g, kept):
             for token in range(8):
                 at = token_rows(g, token)
-                decay = jnp.exp2(dts[at, :][None] * rates[part])
+                decay = jnp.exp2(dts[at, :][None] * laid[laid_part, :].reshape(GROUP, COLS, LANES))
                 kept = decay * kept + splat(bb, g, low, GROUP, token) * us[at, :][None]
                 hs_ref[g * 8 + token, part] = kept
                 total = jnp.sum(splat(bb, g, N + low, GROUP, token) * kept, axis=0)
@@ -466,7 +584,7 @@
     def _(g):
         unspread(y_ref, ys, g)
 
-    at_steps((gather.end,), count, ((11, 11),))
+    at_steps((gather.end,), gather.count, ((11,) * gather.count,))
 
 
 def fold(value):
@@ -479,10 +597,10 @@
     *refs,
 ):
     given, refs = refs[:count], refs[count:]
-    (grad_conv_in, pre_low, chosen, grad_rows, grad_rates), refs = refs[:5], refs[5:]
+    (grad_conv_in, pre_low, chosen, grad_rows, grad_rates, squares), refs = refs[:6], refs[6:]
     full, refs = refs[:count], refs[count:]
-    (carry, dts, us, gss, bb, s1, s2, prods, parts, nat1, nat2, grad_mixed, taps), refs = refs[:13], refs[13:]
-    reduce = Reduce(plan, given, full, refs)
+    (carry, laid, dts, us, gss, bb, s1, s2, prods, parts, nat1, nat2, grad_mixed, taps), refs = refs[:14], refs[14:]
+    reduce = Reduce(plan, REDUCE_CUTS, given, full, squares, refs)
     turn = lax.rem(pl.program_id(0), TAIL)
     tall = BLOCK * TAIL
     own = pl.ds(pl.multiple_of((TAIL - 1 - turn) * BLOCK, BLOCK), BLOCK)
@@ -492,12 +610,14 @@
         for ref in (carry, grad_rates, grad_rows, parts):
             ref[...] = jnp.zeros_like(ref)
         taps[:, tall:, :] = jnp.zeros_like(taps[:, tall:, :])
+        lay_rates(laid, rates)
+        squares[...] = jnp.zeros_like(squares)
         greet(plan)
 
     at_steps(
         (reduce.start, reduce.sum_pair, reduce.sum_plane, reduce.sum_along, reduce.share),
-        count,
-        ((0, 0), (1, 2), (4, 6), (7, 9), (9, 11)),
+        reduce.count,
+        ((0, 0, 0, 0), (1, 1, 2, 2), (3, 4, 5, 6), (5, 6, 7, 8), (7, 8, 9, 10)),
     )
 
     @pl.loop(0, BLOCK // 16)
@@ -512,6 +632,7 @@
     spot = lax.broadcasted_iota(jnp.int32, (8, LANES), 1)
     for low in range(0, N, BACK):
         part = pl.ds(low, BACK)
+        laid_part = pl.ds(low * COLS, BACK * COLS)
 
         def steps(step, carried):
             g = BLOCK // 8 - 1 - step
@@ -523,7 +644,7 @@
                     before = hs_ref[g * 8 + token - 1, part]
                 else:
                     before = jnp.where(g == 0, last_ref[0, part], hs_ref[jnp.maximum(g * 8 - 1, 0), part])
-                rate = rates[part]
+                rate = laid[laid_part, :].reshape(BACK, COLS, LANES)
                 adjoint = splat(bb, g, N + low, BACK, token) * gs + kept
                 for_c = gs * hs_ref[g * 8 + token, part]
                 for_b = adjoint * u
@@ -593,7 +714,7 @@
                 taps[j - 1, tall:, lanes] = taps[j - 1, :8, lanes]
             grad_conv_in[:, lanes] = result.astype(jnp.bfloat16)
 
-    at_steps((reduce.end,), count, ((11, 11),))
+    at_steps((reduce.end,), reduce.count, ((11,) * reduce.count,))
 
 
 def dot(left, right, left_dim, right_dim):
@@ -613,7 +734,7 @@
             rows,
             rows,
             pl.BlockSpec((BLOCK, LANES), lambda i: (i, 0)),
-            pl.BlockSpec((N, COLS, LANES), lambda i: (0, 0, 0)),
+            pl.BlockSpec((N, DI), lambda i: (0, 0)),
         ]
         + anywhere,
         out_specs=[rows, rows, pl.BlockSpec((BLOCK, N, COLS, LANES), lambda i: (i, 0, 0, 0))] + anywhere,
@@ -625,12 +746,13 @@
         + Gather.shapes(plan, pieces),
         scratch_shapes=[
             pltpu.VMEM((N, COLS, LANES), jnp.float32),
+            pltpu.VMEM((N * COLS, LANES), jnp.float32),
             pltpu.VMEM((BLOCK * COLS, LANES), jnp.float32),
             pltpu.VMEM((BLOCK * COLS, LANES), jnp.float32),
             pltpu.VMEM((BLOCK // 8, 2 * N, 8, LANES), jnp.float32),
             pltpu.VMEM((BLOCK * COLS, LANES), jnp.float32),
         ]
-        + Gather.scratch(plan, len(pieces)),
+        + Gather.scratch(plan, sum(GATHER_CUTS)),
         compiler_params=pltpu.CompilerParams(
             vmem_limit_bytes=48 << 20, collective_id=2, has_side_effects=True
         ),
@@ -663,7 +785,7 @@
             rows,
             rows,
             pl.BlockSpec((BLOCK, LANES), lambda i: (blocks - 1 - i, 0)),
-            whole(*state),
+            whole(N, DI),
             whole(8, DI),
             whole(R, DI),
             whole(R + 2 * N, DI),
@@ -674,16 +796,18 @@
             tall(LANES),
         ]
         + anywhere,
-        out_specs=[tall(DI), tall(DI), tall(R + 2 * N), whole(8, 8, DI), whole(*state)] + anywhere,
+        out_specs=[tall(DI), tall(DI), tall(R + 2 * N), whole(8, 8, DI), whole(*state), whole(8, LANES)]
+        + anywhere,
         out_shape=[
             jax.ShapeDtypeStruct((count, DI), jnp.bfloat16),
             jax.ShapeDtypeStruct((count, DI), jnp.bfloat16),
             jax.ShapeDtypeStruct((count, R + 2 * N), jnp.bfloat16),
             jax.ShapeDtypeStruct((8, 8, DI), jnp.float32),
             jax.ShapeDtypeStruct(state, jnp.float32),
+            jax.ShapeDtypeStruct((8, LANES), jnp.float32),
         ]
         + Reduce.shapes(plan, summed),
-        scratch_shapes=[pltpu.VMEM(state, jnp.float32)]
+        scratch_shapes=[pltpu.VMEM(state, jnp.float32), pltpu.VMEM((N * COLS, LANES), jnp.float32)]
         + [pltpu.VMEM((BLOCK * COLS, LANES), jnp.float32)] * 3
         + [pltpu.VMEM((BLOCK // 8, 2 * N, 8, LANES), jnp.float32)]
         + [pltpu.VMEM((BLOCK * COLS, LANES), jnp.float32)] * 2
@@ -692,7 +816,7 @@
         + [pltpu.VMEM((BLOCK, DI), jnp.float32)] * 2
         + [pltpu.VMEM((BLOCK * TAIL, DI), jnp.float32)]
         + [pltpu.VMEM((CONV - 1, BLOCK * TAIL + 8, DI), jnp.float32)]
-        + Reduce.scratch(plan, summed),
+        + Reduce.scratch(plan, REDUCE_CUTS, summed),
         compiler_params=pltpu.CompilerParams(
             vmem_limit_bytes=60 << 20, collective_id=3, has_side_effects=True
         ),
@@ -753,19 +877,17 @@
 ):
     row_count = tokens.shape[0]
     live_mask, offset = block_layout(lengths[0], row_count)
-    restart = (offset == 0).astype(jnp.float32)
     plan = (shards, dp // 2)
-    low_conv, low_gate, low_output = (
-        own_piece(weight, dp).astype(jnp.bfloat16)
-        for weight in (input_weight[:, :DI], input_weight[:, DI:], output_weight)
-    )
+    low_conv = own_piece(input_weight, dp, 0, DI).astype(jnp.bfloat16)
+    low_gate = own_piece(input_weight, dp, DI, DI).astype(jnp.bfloat16)
+    low_output = own_piece(output_weight, dp).astype(jnp.bfloat16)
     low_small = own_piece(jnp.concatenate([select_weight, step_weight], axis=0), dp).astype(jnp.bfloat16)
     width = channel_params.shape[1]
     vectors = jnp.concatenate(
         [channel_params, jnp.pad(norm_gain, (0, width - norm_gain.shape[0]))[None, :]], axis=0
     )
     full_conv, full_small, full_vectors = gather_pieces(
-        plan, [low_conv, low_small, own_piece(vectors, dp)], "gather_weights", 0
+        plan, [low_conv, low_small, own_piece(vectors, dp)], (4, 1, 1), "gather_weights", 0
     )
     full_conv = from_pieces(full_conv, norm_gain.shape[0], DI, dp).reshape(-1, DI)
     small_rows = R + 2 * N + R
@@ -784,15 +906,15 @@
         ((conv_out * sigmoid).astype(jnp.bfloat16), sigmoid * (1.0 + conv_out * (1.0 - sigmoid)))
     )
     mixed_values = mixed.astype(jnp.float32)
-    selection = contract(mixed, full_select, 1, 1)
-    step_low = selection[:, :R].astype(jnp.bfloat16)
+    wide_select = jnp.concatenate([full_select[R:], jnp.zeros((R - 2 * N, DI), jnp.bfloat16), full_select[:R]], axis=0)
+    selection = contract(mixed, wide_select, 1, 1)
+    step_low = selection[:, LANES - R :].astype(jnp.bfloat16)
     step_in = jnp.dot(step_low, full_step, preferred_element_type=jnp.float32) + channel[N + CONV + 1][None, :]
     rates = -jnp.exp(channel[:N])
-    rates_low = (rates * math.log2(math.e)).reshape(N, COLS, LANES)
-    kept = [restart] + [(offset >= j).astype(jnp.float32) for j in range(1, CONV)]
-    chosen = jnp.concatenate(
-        [selection[:, R:], jnp.stack(kept, axis=1), jnp.zeros((row_count, LANES - 2 * N - CONV), jnp.float32)], axis=1
-    )
+    rates_low = rates * math.log2(math.e)
+    lane = lax.broadcasted_iota(jnp.int32, (row_count, LANES), 1)
+    flag = jnp.where(lane == 2 * N, offset == 0, offset >= lane - 2 * N).astype(jnp.float32)
+    chosen = jnp.where(lane < 2 * N, selection, jnp.where(lane < 2 * N + CONV, flag, 0.0))
     skip = channel[N + CONV + 2][None, :]
     state_out, step_size, states, full_gate, full_output = scan_forward(
         step_in, mixed, chosen, rates_low, plan, [low_gate, low_output]
@@ -804,9 +926,9 @@
     gate_value, gate_pull = jax.vjp(jax.nn.silu, gate_half)
     gated = (scanned * gate_value).astype(jnp.bfloat16)
     branch = jnp.dot(gated, full_output, preferred_element_type=jnp.float32)
-    layer_output = (inputs + live_mask[:, None] * branch).astype(jnp.bfloat16)
+    layer_output = (inputs + live_mask * branch).astype(jnp.bfloat16)
     upstream = cotangent.astype(jnp.float32)
-    grad_branch = (upstream * live_mask[:, None]).astype(jnp.bfloat16)
+    grad_branch = (upstream * live_mask).astype(jnp.bfloat16)
     grad_output = contract(gated, grad_branch, 0, 0).astype(jnp.bfloat16)
     grad_gated = contract(grad_branch, full_output, 1, 1)
     grad_scanned = grad_gated * gate_value
@@ -814,7 +936,7 @@
     grad_gate = grad_gate.astype(jnp.bfloat16)
     grad_gate_weight = contract(normed, grad_gate, 0, 0).astype(jnp.bfloat16)
     heights = [norm_gain.shape[0], output_weight.shape[0]]
-    grad_conv_input, grad_pre_low, grad_selection, grad_rows, sums, sum_output, sum_gate = scan_backward(
+    grad_conv_input, grad_pre_low, grad_selection, grad_rows, sums, squares, sum_output, sum_gate = scan_backward(
         step_in,
         step_size,
         mixed,
@@ -846,12 +968,14 @@
     small = small.reshape(-1, shards, width).transpose(1, 0, 2)
     small_gain = jnp.pad(grad_gain.reshape(shards, 1, -1), ((0, 0), (0, 0), (0, width - grad_gain.shape[0] // shards)))
     small = jnp.concatenate([small, small_gain], axis=1).astype(jnp.bfloat16)
-    sum_conv, sum_small = reduce_pieces(
+    sum_conv, sum_small, squares = reduce_pieces(
         plan,
         [
             to_pieces(shards, grad_conv_weight.reshape(shards, heights[0], -1), dp),
             to_pieces(shards, small, dp),
         ],
+        squares,
+        (4, 1),
         "sum_gradients",
         1,
     )
@@ -868,9 +992,7 @@
     sum_select, sum_step = sum_small[: R + 2 * N], sum_small[R + 2 * N : small_rows]
     sum_channel, sum_gain = sum_small[small_rows:-1], sum_small[-1, : norm_gain.shape[0]]
     grads = (sum_gain, sum_input, sum_select, sum_step, sum_channel, sum_output)
-    local_square = sum([jnp.sum(grad * grad) for grad in grads])
-    total_square = lax.psum(local_square, "fsdp")
-    grad_norm = jnp.sqrt(total_square)
+    grad_norm = jnp.sqrt(jnp.sum(squares))
     factor = jnp.minimum(1.0, clip_norm / (grad_norm + 1e-06))
     params = (norm_gain, input_weight, select_weight, step_weight, channel_params, output_weight)
     firsts = (moment_gain, moment_input, moment_select, moment_step, moment_channel, moment_output)

time: 464 us -> 407 us (0.88)
  Pallas kernels: 303 us -> 276 us
  blocking collectives: 15 us -> 0 us
  other arithmetic: 44.3 us -> 37.4 us
  local copies, waits for them, and re-layouts: 23.5 us -> 17.5 us
    pallas_call x2, Pallas kernels: 101 us -> 84.6 us  [the longest x1 46.9 us: reduce_pieces(): pl.pallas_call(functools.partial(reduce_kernel, plan, cuts, count), in_sp...]
    psum x1 -> x0, blocking collectives: 15 us -> none  [local(): total_square = lax.psum(local_square, 'fsdp')]
    pallas_call x1, Pallas kernels: 73 us -> 62.8 us  [scan_forward(): pl.pallas_call(functools.partial(forward_kernel, plan, len(pieces)), grid...]
    reduce_sum x6 -> x1, other arithmetic: 7.26 us -> 0.6 us  [local(): grad_norm = jnp.sqrt(jnp.sum(squares))]
    convert_element_type x5 -> x1, other arithmetic: 4.8 us -> 0.01 us  [block_layout(): return ((places[:, :1] < end).astype(jnp.float32), places - begun)]
where the time goes in v5:
time: 407 us; the launch traced here: 403 us
  Pallas kernels  276 us (68%)
  matrix products  64.6 us (16%)
  other arithmetic  37.4 us (9%)
  local copies, waits for them, and re-layouts  17.5 us (4%)
  between operations  6.95 us (2%)
    pallas_call x1, Pallas kernels, scan_backward(): pl.pallas_call(functools.partial(backward_kernel, plan, len(summed)), gri...  129 us
    pallas_call x1, Pallas kernels, scan_forward(): pl.pallas_call(functools.partial(forward_kernel, plan, len(pieces)), grid...  62.8 us
    pallas_call x1, Pallas kernels, reduce_pieces(): pl.pallas_call(functools.partial(reduce_kernel, plan, cuts, count), in_sp...  46.9 us
    pallas_call x1, Pallas kernels, gather_pieces(): pl.pallas_call(functools.partial(gather_kernel, plan, cuts, count), in_sp...  37.6 us
    dot_general x9, matrix products, contract(): lax.dot_general(left, right, (((left_dim,), (right_dim,)), ((), ())), pre...  37.2 us
    add x6, other arithmetic, adam_direction(): first_hat / (jnp.sqrt(second_hat) + adam_eps) + decay_rate * decay * weight  15.1 us
    dot_general x1, matrix products, local(): gate_half = jnp.dot(normed, full_gate, preferred_element_type=jnp.float32)  11.8 us

profile of v5, /device:TPU:0, one launch (start us, length us, event | category | flops | bytes accessed | tf_op | source)
XLA Modules:
  0.0 402.8 jit_solution(3039652507114208516)
XLA Ops:
  0.6 1.8 dynamic-slice_convert_fusion.1
  2.4 1.4 fusion.69.refs_1_
  4.5 1.4 fusion.71.refs_2_
  5.9 37.6 %gather_weights.1 = (bf16[4,4,2,32,2048]{4,3,2,1,0:T(8,128)(2,1)}, bf16[4,4,2,80,128]{4,3,2,1,0:T(8,128)(2,1)}, f32[4,4,2,16,128]{4,3,2,1,0:T(8,128)}) custom-call(bf16[32,2048]{1,0:T(8,128)(2,1)} %get-tuple-element.78.refs_0_, bf16[80,128]{1,0:T(8,128)(2,1)} %fusion.69.refs_1_, f32[16,128]{1,0:T(8,128)} %fusion.71.refs_2_), custom_call_target="tpu_custom_call" | custom-call | bytes 33554432 | tf_op jit(solution)/shard_map/gather_weights/pallas_call | solution.py:212
  43.5 1.5 copy.46
  51.7 5.5 %fusion.84.conv_ref = f32[768,2048]{1,0:T(8,128)S(1)} fusion(bf16[1024,2048]{1,0:T(8,128)(2,1)} %bitcast.154, bf16[768,1024]{1,0:T(8,128)(2,1)S(1)} %copy-done.7, f32[1024]{0:T(1024)S(1)} %bitcast.144, f32[768]{0:T(1024)S(1)} %fusion.75), kind=kOutput, calls=%fused_computation.161 | convolution fusion | flops 3224371200 | bytes 12065792 | tf_op jit(solution)/shard_map/dot_general | solution.py:902
  57.3 7.1 %add_multiply_fusion = (f32[768,2048]{1,0:T(8,128)}, f32[768,2048]{1,0:T(8,128)S(1)}) fusion(f32[768]{0:T(1024)S(1)} %get-tuple-element.60, f32[768,2048]{1,0:T(8,128)S(1)} %fusion.84.conv_ref, f32[2048]{0:T(1024)S(1)} %bitcast.139, f32[768]{0:T(1024)S(1)} %get-tuple-element.61, f32[2048]{0:T(1024)S(1)} %bitcast.140, f32[768]{0:T(1024)S(1)} %get-tuple-element.59, ...), kind=kLoop, calls=%fused_computation.21 | loop fusion | flops 28311552 | bytes 18924544 | tf_op jit(solution)/shard_map/mul | solution.py:906
  64.4 1.7 multiply_convert_fusion.1.mixed_ref
  66.2 1.1 slice.187
  67.5 1.2 fusion.40
  69.4 3.6 convolution_add_fusion.v_ref
  73.0 1.9 copy.47
  74.9 1.9 select_select_fusion.sel.flags
  76.8 1.1 fusion.60
  79.3 1.0 dynamic-slice_convert_fusion.refs_1_
  82.1 62.8 %scan_forward.1 = (f32[768,2048]{1,0:T(8,128)}, f32[768,2048]{1,0:T(8,128)}, f32[768,16,16,128]{3,2,1,0:T(8,128)}, bf16[4,4,2,32,2048]{4,3,2,1,0:T(8,128)(2,1)}, bf16[4,4,2,64,1024]{4,3,2,1,0:T(8,128)(2,1)}) custom-call(f32[768,2048]{1,0:T(8,128)} %convolution_add_fusion.v_ref, bf16[768,2048]{1,0:T(8,128)(2,1)S(1)} %multiply_convert_fusion.1.mixed_ref, ...), custom_call_target="tpu_custom_call" | custom-call | flops 150994944 | bytes 100663296 | tf_op jit(solution)/shard_map/scan_forward/pallas_call | solution.py:730
  145.6 5.9 %fusion.38 = f32[768,2048]{1,0:T(8,128)S(1)} fusion(bf16[2048,1024]{1,0:T(8,128)(2,1)} %bitcast.158, bf16[768,1024]{1,0:T(8,128)(2,1)} %param.23, f32[768]{0:T(1024)S(1)} %fusion.73), kind=kOutput, calls=%fused_computation.70 | convolution fusion | flops 3223584768 | bytes 12061696 | tf_op jit(solution)/shard_map/dot_general | solution.py:834
  151.6 11.8 %fusion.11 = (bf16[768,2048]{1,0:T(8,128)(2,1)}, bf16[768,2048]{1,0:T(8,128)(2,1)}, f32[768,2048]{1,0:T(8,128)}) fusion(f32[768,2048]{1,0:T(8,128)S(1)} %fusion.38, f32[768,2048]{1,0:T(8,128)} %get-tuple-element.40, bf16[768,2048]{1,0:T(8,128)(2,1)S(1)} %multiply_convert_fusion.1.mixed_ref, f32[2048]{0:T(1024)S(1)} %bitcast.150, ...), kind=kOutput, calls=%fused_computation.15 | convolution fusion | flops 3252682752 | bytes 34094080 | tf_op jit(solution)/shard_map/dot_general | solution.py:924
  163.4 6.6 %fusion.26 = bf16[768,1024]{1,0:T(8,128)(2,1)} fusion(bf16[768,1024]{1,0:T(8,128)(2,1)S(1)} %copy-done.8, bf16[768,2048]{1,0:T(8,128)(2,1)} %get-tuple-element.75, bf16[2048,1024]{1,0:T(8,128)(2,1)S(1)} %bitcast.159, f32[768]{0:T(1024)S(1)} %fusion.73), kind=kOutput, calls=%fused_computation.49 | convolution fusion | flops 3224371200 | bytes 10488832 | tf_op jit(solution)/shard_map/dot_general | solution.py:928
  172.5 5.2 %convolution_convert_fusion.2 = bf16[2048,1024]{1,0:T(8,128)(2,1)} fusion(bf16[768,2048]{1,0:T(8,128)(2,1)S(1)} %copy-done.54, bf16[768,1024]{1,0:T(8,128)(2,1)S(1)} %copy-done.18, f32[768]{0:T(1024)S(1)} %fusion.73), kind=kOutput, calls=%fused_computation.41 | convolution fusion | flops 3225681920 | bytes 8915968 | tf_op jit(solution)/shard_map/dot_general | solution.py:834
  177.7 5.4 %convolution_convert_fusion.1 = bf16[1024,2048]{1,0:T(8,128)(2,1)} fusion(bf16[768,2048]{1,0:T(8,128)(2,1)S(1)} %copy-done.52, bf16[768,1024]{1,0:T(8,128)(2,1)S(1)} %copy-done.8, f32[1024]{0:T(1024)S(1)} %bitcast.146, f32[768]{0:T(1024)S(1)} %copy-done.40), kind=kOutput, calls=%fused_computation.40 | convolution fusion | flops 3226468352 | bytes 8920064 | tf_op jit(solution)/shard_map/dot_general | solution.py:834
  183.1 128.9 %scan_backward.1 = (bf16[768,2048]{1,0:T(8,128)(2,1)}, bf16[768,2048]{1,0:T(8,128)(2,1)}, bf16[768,96]{1,0:T(8,128)(2,1)}, f32[8,8,2048]{2,1,0:T(8,128)}, f32[16...) custom-call(f32[768,2048]{1,0:T(8,128)} %convolution_add_fusion.v_ref,, ...), custom_call_target="tpu_custom_call" | custom-call | flops 503316480 | bytes 100663296 | tf_op jit(solution)/shard_map/scan_backward/pallas_call | solution.py:779
  312.1 6.8 %fusion.89 = f32[768,1024]{1,0:T(8,128)S(1)} fusion(bf16[768,2048]{1,0:T(8,128)(2,1)} %get-tuple-element.46, bf16[1024,2048]{1,0:T(8,128)(2,1)} %bitcast.155), kind=kOutput, calls=%fused_computation.164 | convolution fusion | flops 3221225472 | bytes 10485760 | tf_op jit(solution)/shard_map/dot_general | solution.py:834
  319.0 4.0 %fusion.22 = (bf16[1024]{0:T(1024)(128)(2,1)S(1)}, f32[768]{0:T(1024)S(1)}, f32[768,1024]{1,0:T(8,128)S(1)}) fusion(bf16[768,1024]{1,0:T(8,128)(2,1)S(1)} %copy-done.9, f32[768]{0:T(1024)S(1)} %copy-done.40, f32[1024]{0:T(1024)S(1)} %bitcast.147, f32[768,1024]{1,0:T(8,128)S(1)} %fusion.89, bf16[768,2048]{1,0:T(8,128)(2,1)S(1)} %copy-done.53, ...), kind=kOutput, calls=%fused_computation.45 | convolution fusion | flops 3227515136 | bytes 15216640 | tf_op jit(solution)/shard_map/dot_general | solution.py:834
  323.1 2.1 fusion.24
  325.2 5.3 %convolution_convert_fusion = bf16[1024,2048]{1,0:T(8,128)(2,1)} fusion(bf16[768,2048]{1,0:T(8,128)(2,1)S(1)} %copy-done.48, bf16[768,1024]{1,0:T(8,128)(2,1)S(1)} %copy-done.9, f32[1024]{0:T(1024)S(1)} %bitcast.149, f32[768]{0:T(1024)S(1)} %copy-done.40), kind=kOutput, calls=%fused_computation.39 | convolution fusion | flops 3226468352 | bytes 8920064 | tf_op jit(solution)/shard_map/dot_general | solution.py:834
  330.6 1.3 slice_reduce_fusion
  331.8 1.0 fusion.59
  332.9 2.5 convolution_convert_fusion.4
  337.4 46.9 %sum_gradients.1 = (bf16[4,2,32,2048]{3,2,1,0:T(8,128)(2,1)S(1)}, bf16[4,2,48,256]{3,2,1,0:T(8,128)(2,1)S(1)}, f32[8,128]{1,0:T(8,128)S(1)}) custom-call(bf16[4,4,2,32,2048]{4,3,2,1,0:T(8,128)(2,1)} %bitcast.119, bf16[4,4,2,48,256]{4,3,2,1,0:T(8,128)(2,1)S(1)} %bitcast.111, f32[8,128]{1,0:T(8,128)S(1)} %copy-done.5), custom_call_target="tpu_custom_call" | custom-call | bytes 33554432 | tf_op jit(solution)/shard_map/sum_gradients/pallas_call | solution.py:441
  386.9 8.6 %fusion.18 = (f32[256,4096]{1,0:T(8,128)}, f32[256,4096]{1,0:T(8,128)}) fusion(f32[256,4096]{1,0:T(8,128)} %param.25, f32[256,4096]{1,0:T(8,128)} %param.37, f32[256,4096]{1,0:T(8,128)} %param.31, f32[]{:T(128)S(6)} %min.3, bf16[256,2048]{1,0:T(8,128)(2,1)S(1)} %bitcast.127, bf16[256,2048]{1,0:T(8,128)(2,1)S(1)} %bitcast.112), kind=kLoop, calls=%fused_computation.35 | loop fusion | flops 18874368 | bytes 23068676 | tf_op jit(solution)/shard_map/add | solution.py:850
  397.8 3.7 fusion.33
  (169 shorter events, 17.1 us)
Async XLA Ops:
  2.4 44.2 %copy-start.43 = (s32[1,4]{1,0:T(1,128)S(1)}, s32[1,4]{1,0:T(1,128)}, u32[]{:S(2)}) copy-start(s32[1,4]{1,0:T(1,128)} %param.22) | copy-start | bytes 52
  43.5 7.8 %copy-start.7 = (bf16[768,1024]{1,0:T(8,128)(2,1)S(1)}, bf16[768,1024]{1,0:T(8,128)(2,1)}, u32[]{:S(2)}) copy-start(bf16[768,1024]{1,0:T(8,128)(2,1)} %param.21) | copy-start | bytes 4718596
  45.3 11.9 %copy-start.10 = (bf16[4,160,512]{2,0,1:T(4,128)(2,1)}, bf16[4,160,512]{2,0,1:T(4,128)(2,1)S(1)}, u32[]{:S(2)}) copy-start(bf16[4,160,512]{2,0,1:T(4,128)(2,1)S(1)} %reshape.153) | copy-start | bytes 1966084
  46.2 22.4 %copy-start.13 = (bf16[8,8,4,512]{3,1,2,0:T(8,128)(2,1)}, bf16[8,8,4,512]{3,1,2,0:T(8,128)(2,1)S(1)}, u32[]{:S(2)}) copy-start(bf16[8,8,4,512]{3,1,2,0:T(8,128)(2,1)S(1)} %copy.61) | copy-start | bytes 786436
  57.2 7.2 %copy-start.6 = (f32[768,2048]{1,0:T(8,128)}, f32[768,2048]{1,0:T(8,128)S(1)}, u32[]{:S(2)}) copy-start(f32[768,2048]{1,0:T(8,128)S(1)} %fusion.84.conv_ref) | copy-start | bytes 18874372
  66.2 85.4 %copy-start = (bf16[768,2048]{1,0:T(8,128)(2,1)}, bf16[768,2048]{1,0:T(8,128)(2,1)S(1)}, u32[]{:S(2)}) copy-start(bf16[768,2048]{1,0:T(8,128)(2,1)S(1)} %multiply_convert_fusion.1.mixed_ref) | copy-start | bytes 9437188
  76.8 68.1 %copy-start.2 = (f32[768,128]{1,0:T(8,128)}, f32[768,128]{1,0:T(8,128)S(1)}, u32[]{:S(2)}) copy-start(f32[768,128]{1,0:T(8,128)S(1)} %select_select_fusion.sel.flags) | copy-start | bytes 1179652
  151.6 11.8 %copy-start.51 = (bf16[4,4,2,64,1024]{4,3,2,1,0:T(8,128)(2,1)S(1)}, bf16[4,4,2,64,1024]{4,3,2,1,0:T(8,128)(2,1)}, u32[]{:S(2)}) copy-start(bf16[4,4,2,64,1024]{4,3,2,1,0:T(8,128)(2,1)} %get-tuple-element.42) | copy-start | bytes 12582916
  163.4 8.1 %copy-start.11 = (bf16[4,160,512]{2,0,1:T(4,128)(2,1)S(1)}, bf16[4,160,512]{2,0,1:T(4,128)(2,1)}, u32[]{:S(2)}) copy-start(bf16[4,160,512]{2,0,1:T(4,128)(2,1)} %copy-done.10) | copy-start | bytes 1966084
  163.4 9.0 %copy-start.18 = (bf16[768,1024]{1,0:T(8,128)(2,1)S(1)}, bf16[768,1024]{1,0:T(8,128)(2,1)}, u32[]{:S(2)}) copy-start(bf16[768,1024]{1,0:T(8,128)(2,1)} %param.23) | copy-start | bytes 4718596
  163.4 9.0 %copy-start.54 = (bf16[768,2048]{1,0:T(8,128)(2,1)S(1)}, bf16[768,2048]{1,0:T(8,128)(2,1)}, u32[]{:S(2)}) copy-start(bf16[768,2048]{1,0:T(8,128)(2,1)} %get-tuple-element.75) | copy-start | bytes 9437188
  312.1 6.9 %copy-start.9 = (bf16[768,1024]{1,0:T(8,128)(2,1)S(1)}, bf16[768,1024]{1,0:T(8,128)(2,1)}, u32[]{:S(2)}) copy-start(bf16[768,1024]{1,0:T(8,128)(2,1)} %param.21) | copy-start | bytes 4718596
  312.1 6.9 %copy-start.50 = (bf16[4,4,2,32,2048]{4,3,2,1,0:T(8,128)(2,1)S(1)}, bf16[4,4,2,32,2048]{4,3,2,1,0:T(8,128)(2,1)}, u32[]{:S(2)}) copy-start(bf16[4,4,2,32,2048]{4,3,2,1,0:T(8,128)(2,1)} %get-tuple-element.41) | copy-start | bytes 12582916
  312.1 6.9 %copy-start.53 = (bf16[768,2048]{1,0:T(8,128)(2,1)S(1)}, bf16[768,2048]{1,0:T(8,128)(2,1)}, u32[]{:S(2)}) copy-start(bf16[768,2048]{1,0:T(8,128)(2,1)} %get-tuple-element.74) | copy-start | bytes 9437188
  325.2 7.7 %copy-start.15 = (f32[768,128]{0,1:T(8,128)S(1)}, f32[768,128]{0,1:T(8,128)}, u32[]{:S(2)}) copy-start(f32[768,128]{0,1:T(8,128)} %copy-done.14) | copy-start | bytes 1179652
  337.4 48.7 %copy-start.44 = (f32[256]{0:T(256)S(1)}, f32[256]{0:T(256)}, u32[]{:S(2)}) copy-start(f32[256]{0:T(256)} %param.24) | copy-start | bytes 3076
  337.4 48.7 %copy-start.46 = (f32[256]{0:T(256)S(1)}, f32[256]{0:T(256)}, u32[]{:S(2)}) copy-start(f32[256]{0:T(256)} %param.36) | copy-start | bytes 3076
  337.4 48.7 %copy-start.47 = (f32[256]{0:T(256)S(1)}, f32[256]{0:T(256)}, u32[]{:S(2)}) copy-start(f32[256]{0:T(256)} %param.30) | copy-start | bytes 3076
  337.4 49.3 %copy-start.21 = (bf16[4,2,32,2048]{3,2,1,0:T(8,128)(2,1)S(1)}, bf16[4,2,32,2048]{3,2,1,0:T(8,128)(2,1)}, u32[]{:S(2)}) copy-start(bf16[4,2,32,2048]{3,2,1,0:T(8,128)(2,1)} %get-tuple-element.55) | copy-start | bytes 3145732
  386.1 9.4 %copy-start.45 = (f32[1,256]{1,0:T(1,128)}, f32[1,256]{1,0:T(1,128)S(1)}, u32[]{:S(2)}) copy-start(f32[1,256]{1,0:T(1,128)S(1)} %slice.197) | copy-start | bytes 3076
  386.7 8.7 %copy-start.24 = (f32[96,512]{1,0:T(8,128)S(1)}, f32[96,512]{1,0:T(8,128)}, u32[]{:S(2)}) copy-start(f32[96,512]{1,0:T(8,128)} %param.26) | copy-start | bytes 589828
  386.7 8.7 %copy-start.29 = (f32[96,512]{1,0:T(8,128)S(1)}, f32[96,512]{1,0:T(8,128)}, u32[]{:S(2)}) copy-start(f32[96,512]{1,0:T(8,128)} %param.38) | copy-start | bytes 589828
  386.7 8.7 %copy-start.30 = (f32[96,512]{1,0:T(8,128)S(1)}, f32[96,512]{1,0:T(8,128)}, u32[]{:S(2)}) copy-start(f32[96,512]{1,0:T(8,128)} %param.32) | copy-start | bytes 589828
  386.7 9.6 %copy-start.25 = (f32[64,512]{1,0:T(8,128)S(1)}, f32[64,512]{1,0:T(8,128)}, u32[]{:S(2)}) copy-start(f32[64,512]{1,0:T(8,128)} %param.27) | copy-start | bytes 393220
  386.8 9.6 %copy-start.31 = (f32[64,512]{1,0:T(8,128)S(1)}, f32[64,512]{1,0:T(8,128)}, u32[]{:S(2)}) copy-start(f32[64,512]{1,0:T(8,128)} %param.39) | copy-start | bytes 393220
  386.8 9.5 %copy-start.32 = (f32[64,512]{1,0:T(8,128)S(1)}, f32[64,512]{1,0:T(8,128)}, u32[]{:S(2)}) copy-start(f32[64,512]{1,0:T(8,128)} %param.33) | copy-start | bytes 393220
  386.8 10.3 %copy-start.28 = (f32[23,512]{1,0:T(8,128)S(1)}, f32[23,512]{1,0:T(8,128)}, u32[]{:S(2)}) copy-start(f32[23,512]{1,0:T(8,128)} %param.28) | copy-start | bytes 141316
  386.8 10.3 %copy-start.33 = (f32[23,512]{1,0:T(8,128)S(1)}, f32[23,512]{1,0:T(8,128)}, u32[]{:S(2)}) copy-start(f32[23,512]{1,0:T(8,128)} %param.40) | copy-start | bytes 141316
  386.8 10.3 %copy-start.34 = (f32[23,512]{1,0:T(8,128)S(1)}, f32[23,512]{1,0:T(8,128)}, u32[]{:S(2)}) copy-start(f32[23,512]{1,0:T(8,128)} %param.34) | copy-start | bytes 141316
  386.8 11.0 %copy-start.16 = (f32[512,1024]{1,0:T(8,128)S(1)}, f32[512,1024]{1,0:T(8,128)}, u32[]{:S(2)}) copy-start(f32[512,1024]{1,0:T(8,128)} %param.41) | copy-start | bytes 6291460
  386.8 11.0 %copy-start.17 = (f32[512,1024]{1,0:T(8,128)S(1)}, f32[512,1024]{1,0:T(8,128)}, u32[]{:S(2)}) copy-start(f32[512,1024]{1,0:T(8,128)} %param.35) | copy-start | bytes 6291460
  386.8 11.0 %copy-start.20 = (bf16[4,2,64,1024]{3,2,1,0:T(8,128)(2,1)S(1)}, bf16[4,2,64,1024]{3,2,1,0:T(8,128)(2,1)}, u32[]{:S(2)}) copy-start(bf16[4,2,64,1024]{3,2,1,0:T(8,128)(2,1)} %get-tuple-element.56) | copy-start | bytes 3145732
  (23 other events, 78.4 us)
